TPU v7x, 256 devices: a whole 4x4x8 slice. The times are simulated.
256 devices in a mesh: row: 8 (over x_lo, y), col: 32 (over z, x_hi, core).
Axes of the slice: x: 4 (x_hi: 2, x_lo: 2; x = x_hi * 2 + x_lo), y: 4, z: 8, core: 2. Of those that a mesh axis runs over, the one named last changes fastest.
Arguments:
- features: bfloat16 [2048, 16384], P(None, 'col'), may hold values from -6 to 6
- cross_weight: bfloat16 [16384, 16384], P('row', 'col'), may hold values from -0.046875 to 0.046875
- cross_bias: float32 [16384], P('row'), may hold values from -5 to 5
- expert_ids: int32 [2048, 2], P('col'), may hold values from 0 to 31, all different within a row; in each aligned block of 64 rows (0 to 63, 64 to 127, ...) at most 8 rows name the same one
- route_gates: float32 [2048, 2], P('col'), may hold values from 0.2 to 1
- expert_weight: bfloat16 [32, 16384, 2048], P('col', 'row'), may hold values from -0.046875 to 0.046875
- mixed_grad: bfloat16 [2048, 2048], P('col'), may hold values from -6 to 6
Outputs:
- combined: bfloat16 [2048, 2048], P('col', 'row')
- cross_grad: bfloat16 [2048, 16384], P('col', 'row')
Inputs may be any that keep to these rules, and one draw needn't show every extreme that they name: `expert_ids`: each row names two different experts. In each aligned block of 64 rows no expert is named more than 8 times, a bound that some block reaches.
All inputs are finite; a program needn't handle non-finite values.
Results may differ from a plain program's by a relative error of at most 0.025.
Values may be sent and summed in bfloat16 or wider, within the bound.
No kernel may reach another device: no remote copies, remote signals or barrier semaphores. Data moves between devices by JAX's collectives and lax.ppermute only.
A program may use at most 128 MiB of HBM per device.

v0:
```python
import jax
import jax.numpy as jnp
from jax import lax
from jax.sharding import PartitionSpec as P


def silu_slope(values):
    sigma = jax.nn.sigmoid(values)
    return sigma * (1.0 + values * (1.0 - sigma))


def slot_table(expert_ids, experts, capacity):
    flat_ids = expert_ids.reshape(-1)
    labels = jnp.arange(experts, dtype=jnp.int32)
    member = (flat_ids[:, None] == labels[None, :]).astype(jnp.int32)
    before = jnp.cumsum(member, axis=0) - member
    position = jnp.sum(before * member, axis=1)
    target = flat_ids * capacity + position
    places = jnp.arange(experts * capacity, dtype=jnp.int32)
    return (places[:, None] == target[None, :]).astype(jnp.bfloat16)


def pull_rows(table, values):
    return lax.dot_general(
        table, values, (((0,), (0,)), ((), ())), preferred_element_type=jnp.float32
    )


def local(features, cross_weight, cross_bias, expert_ids, route_gates, expert_weight, mixed_grad):
    row_count = lax.axis_size("row")
    col_count = lax.axis_size("col")
    row_index = lax.axis_index("row")
    local_rows = expert_ids.shape[0]
    feat_width = cross_weight.shape[0]
    out_width = expert_weight.shape[2]
    out_share = out_width // row_count
    capacity = 4 * local_rows // col_count
    slots_total = col_count * capacity
    crossed = lax.psum_scatter(
        lax.dot_general(
            features, cross_weight, (((1,), (1,)), ((), ())), preferred_element_type=jnp.float32
        ).astype(jnp.bfloat16),
        "col",
        scatter_dimension=0,
        tiled=True,
    ).astype(jnp.float32)
    spread = lax.all_to_all(features, "col", split_axis=0, concat_axis=1, tiled=True)
    base_rows = lax.dynamic_slice_in_dim(spread, row_index * feat_width, feat_width, 1)
    base_float = base_rows.astype(jnp.float32)
    hidden = (base_float * (crossed + cross_bias) + base_float).astype(jnp.bfloat16)
    table = slot_table(expert_ids, col_count, capacity)
    chooser = jnp.sum(table.reshape(slots_total, local_rows, 2), axis=2)
    send_rows = jnp.dot(chooser, hidden, preferred_element_type=jnp.float32).astype(jnp.bfloat16)
    route_grad = (route_gates[:, :, None] * mixed_grad[:, None, :].astype(jnp.float32)).astype(
        jnp.bfloat16
    )
    send_grad = jnp.dot(
        table, route_grad.reshape(2 * local_rows, out_width), preferred_element_type=jnp.float32
    ).astype(jnp.bfloat16)
    weight_slab = expert_weight[0]
    routed_rows = lax.all_to_all(
        send_rows.reshape(col_count, capacity, feat_width),
        "col",
        split_axis=0,
        concat_axis=0,
        tiled=True,
    )
    routed_grad = lax.all_to_all(
        send_grad.reshape(col_count, capacity, out_width),
        "col",
        split_axis=0,
        concat_axis=0,
        tiled=True,
    )
    sources = routed_rows.shape[0]
    amount = routed_rows.shape[1]
    flat_rows = routed_rows.reshape(sources * amount, feat_width)
    partial_pre = jnp.dot(flat_rows, weight_slab, preferred_element_type=jnp.float32)
    preact = lax.psum(partial_pre.astype(jnp.bfloat16), "row").astype(jnp.float32)
    own_part = lax.dynamic_slice_in_dim(preact, row_index * out_share, out_share, 1)
    activated = jax.nn.silu(own_part).astype(jnp.bfloat16)
    flat_grad = routed_grad.reshape(sources * amount, out_width).astype(jnp.float32)
    slope_grad = (flat_grad * silu_slope(preact)).astype(jnp.bfloat16)
    back_rows = lax.dot_general(
        slope_grad, weight_slab, (((1,), (1,)), ((), ())), preferred_element_type=jnp.float32
    ).astype(jnp.bfloat16)
    returned_act = lax.all_to_all(
        activated.reshape(sources, amount, out_share),
        "col",
        split_axis=0,
        concat_axis=0,
        tiled=True,
    )
    returned_back = lax.all_to_all(
        back_rows.reshape(sources, amount, feat_width),
        "col",
        split_axis=0,
        concat_axis=0,
        tiled=True,
    )
    pair_act = pull_rows(table, returned_act.reshape(slots_total, out_share))
    combined = jnp.sum(
        route_gates[:, :, None] * pair_act.reshape(local_rows, 2, out_share), axis=1
    ).astype(jnp.bfloat16)
    cross_grad = pull_rows(chooser, returned_back.reshape(slots_total, feat_width)).astype(
        jnp.bfloat16
    )
    return (combined, cross_grad)


def solution(mesh):
    return jax.shard_map(
        local,
        mesh=mesh,
        in_specs=(
            P(None, "col"),
            P("row", "col"),
            P("row"),
            P("col", None),
            P("col", None),
            P("col", "row", None),
            P("col", None),
        ),
        out_specs=(P("col", "row"), P("col", "row")),
        check_vma=False,
    )
```

profile of v0, /device:TPU:1, one launch (start us, length us, event | category | flops | bytes accessed | tf_op | source)
XLA Modules:
  0.0 375.0 jit_solution(3415311743031842005)
XLA Ops:
  7.2 1.5 copy-done
  8.8 8.4 %convolution_convert_fusion = bf16[2048,2048]{1,0:T(8,128)(2,1)} fusion(bf16[2048,512]{1,0:T(8,128)(2,1)} %param.7, bf16[2048,512]{1,0:T(8,128)(2,1)S(1)} %copy-done), kind=kOutput, calls=%fused_computation.4 | convolution fusion | flops 4299161600 | bytes 12582912 | tf_op jit(solution)/shard_map/dot_general | solution.py:40
  17.2 12.7 %all-to-all-start = ((bf16[32,64,512]{2,1,0:T(8,128)(2,1)}), bf16[32,64,512]{2,1,0:T(8,128)(2,1)}, u32[]{:S(2)}, u32[]{:S(2)}) async-start(bf16[32,64,512]{2,1,0:T(8,128)(2,1)} %bitcast.45), calls=%async_computation | async-start | bytes 4194304 | tf_op jit(solution)/shard_map/all_to_all | solution.py:47
  30.9 49.1 %all-to-all-done = bf16[32,64,512]{2,1,0:T(8,128)(2,1)} async-done(((bf16[32,64,512]{2,1,0:T(8,128)(2,1)}), bf16[32,64,512]{2,1,0:T(8,128)(2,1)}, u32[]{:S(2)}, u32[]{:S(2)}) %all-to-all-start) | async-done | bytes 2097184 | tf_op jit(solution)/shard_map/all_to_all | solution.py:47
  80.0 3.2 copy.37
  83.1 87.7 %reduce-scatter.2.cloned.1.call-done = bf16[64,2048]{1,0:T(8,128)(2,1)} async-done(((bf16[2048,2048]{1,0:T(8,128)(2,1)}), bf16[64,2048]{1,0:T(8,128)(2,1)}) %reduce-scatter.2.cloned.1.call-update) | async-done | bytes 262160 | tf_op jit(solution)/shard_map/reduce_scatter | solution.py:39
  170.8 2.5 fusion.10
  173.2 10.9 %all-to-all-start.1 = ((bf16[32,8,2048]{2,1,0:T(8,128)(2,1)}), bf16[32,8,2048]{2,1,0:T(8,128)(2,1)}, u32[]{:S(2)}, u32[]{:S(2)}) async-start(bf16[32,8,2048]{2,1,0:T(8,128)(2,1)} %fusion.10), calls=%async_computation.2 | async-start | bytes 2097152 | tf_op jit(solution)/shard_map/all_to_all | solution.py:61
  184.2 0.5 mul.79
  184.7 1.7 mul.80
  186.6 2.7 fusion.14
  189.4 23.0 %all-to-all-done.1 = bf16[32,8,2048]{2,1,0:T(8,128)(2,1)} async-done(((bf16[32,8,2048]{2,1,0:T(8,128)(2,1)}), bf16[32,8,2048]{2,1,0:T(8,128)(2,1)}, u32[]{:S(2)}, u32[]{:S(2)}) %all-to-all-start.1) | async-done | bytes 1048608 | tf_op jit(solution)/shard_map/all_to_all | solution.py:61
  212.3 5.9 %all-to-all-start.3 = ((bf16[32,8,2048]{2,1,0:T(8,128)(2,1)}), bf16[32,8,2048]{2,1,0:T(8,128)(2,1)}, u32[]{:S(2)}, u32[]{:S(2)}) async-start(bf16[32,8,2048]{2,1,0:T(8,128)(2,1)} %fusion.14), calls=%async_computation.4 | async-start | bytes 2097152 | tf_op jit(solution)/shard_map/all_to_all | solution.py:68
  218.2 7.0 %fusion.4 = bf16[256,2048]{1,0:T(8,128)(2,1)} fusion(bf16[1,2048,2048]{2,1,0:T(8,128)(2,1)} %param.12, bf16[32,8,2048]{2,1,0:T(8,128)(2,1)} %all-to-all-done.1), kind=kOutput, calls=%fused_computation.6 | convolution fusion | flops 2148007936 | bytes 10485760 | tf_op jit(solution)/shard_map/dot_general | solution.py:78
  225.3 79.2 %all-reduce.2.cloned.1.call-done = bf16[256,2048]{1,0:T(8,128)(2,1)} async-done(((bf16[256,2048]{1,0:T(8,128)(2,1)}), bf16[256,2048]{1,0:T(8,128)(2,1)}) %all-reduce.2.cloned.1.call-update) | async-done | bytes 1048592 | tf_op jit(solution)/shard_map/psum | solution.py:79
  304.5 1.5 convert_element_type.70
  306.1 0.7 fusion.29
  306.8 15.0 %all-to-all-start.2 = ((bf16[32,8,256]{2,1,0:T(8,128)(2,1)}), bf16[32,8,256]{2,1,0:T(8,128)(2,1)S(1)}, u32[]{:S(2)}, u32[]{:S(2)}) async-start(bf16[32,8,256]{2,1,0:T(8,128)(2,1)} %fusion.29), calls=%async_computation.3 | async-start | bytes 262144 | tf_op jit(solution)/shard_map/all_to_all | solution.py:87
  321.8 7.5 %fusion.11 = bf16[32,8,2048]{2,1,0:T(8,128)(2,1)} fusion(bf16[1,2048,2048]{2,1,0:T(8,128)(2,1)} %param.12, bf16[32,8,2048]{2,1,0:T(8,128)(2,1)} %all-to-all-done.3, bf16[256,2048]{1,0:T(8,128)(2,1)S(1)} %copy-done.1), kind=kOutput, calls=%fused_computation.10 | convolution fusion | flops 2153775104 | bytes 11534336 | tf_op jit(solution)/shard_map/dot_general | solution.py:84
  329.3 3.3 all-to-all-done.2
  332.5 6.5 %all-to-all-start.4 = ((bf16[32,8,2048]{2,1,0:T(8,128)(2,1)}), bf16[32,8,2048]{2,1,0:T(8,128)(2,1)S(1)}, u32[]{:S(2)}, u32[]{:S(2)}) async-start(bf16[32,8,2048]{2,1,0:T(8,128)(2,1)} %fusion.11), calls=%async_computation.5 | async-start | bytes 2097152 | tf_op jit(solution)/shard_map/all_to_all | solution.py:94
  339.2 0.8 fusion.16
  340.0 27.2 %all-to-all-done.4 = bf16[32,8,2048]{2,1,0:T(8,128)(2,1)S(1)} async-done(((bf16[32,8,2048]{2,1,0:T(8,128)(2,1)}), bf16[32,8,2048]{2,1,0:T(8,128)(2,1)S(1)}, u32[]{:S(2)}, u32[]{:S(2)}) %all-to-all-start.4) | async-done | bytes 1048608 | tf_op jit(solution)/shard_map/all_to_all | solution.py:94
  367.2 1.0 convolution_convert_fusion.3
  (30 shorter events, 1.5 us)
Async XLA Ops:
  7.2 1.6 copy-start
  7.2 163.6 %reduce-scatter.2.cloned.1.call-start = ((), (), s32[]{:S(2)}) async-start(), calls=%async_computation.6 | async-start | bytes 8650752 | tf_op jit(solution)/shard_map/reduce_scatter | solution.py:39
  17.2 12.7 %copy-start.4 = (s32[64,2]{0,1:T(2,128)S(1)}, s32[64,2]{0,1:T(2,128)}, u32[]{:S(2)}) copy-start(s32[64,2]{0,1:T(2,128)} %param.10) | copy-start | bytes 1540
  17.2 62.8 %all-to-all-start = ((bf16[32,64,512]{2,1,0:T(8,128)(2,1)}), bf16[32,64,512]{2,1,0:T(8,128)(2,1)}, u32[]{:S(2)}, u32[]{:S(2)}) async-start(bf16[32,64,512]{2,1,0:T(8,128)(2,1)} %bitcast.45), calls=%async_computation | async-start | bytes 4194304 | tf_op jit(solution)/shard_map/all_to_all | solution.py:47
  80.0 90.8 %copy-start.3 = (f32[2048]{0:T(1024)S(1)}, f32[2048]{0:T(1024)}, u32[]{:S(2)}) copy-start(f32[2048]{0:T(1024)} %param.9) | copy-start | bytes 24580
  83.1 101.0 %copy-start.2 = (bf16[64,2048]{1,0:T(8,128)(2,1)S(1)}, bf16[64,2048]{1,0:T(8,128)(2,1)}, u32[]{:S(2)}) copy-start(bf16[64,2048]{1,0:T(8,128)(2,1)} %param.13) | copy-start | bytes 786436
  173.2 39.1 %all-to-all-start.1 = ((bf16[32,8,2048]{2,1,0:T(8,128)(2,1)}), bf16[32,8,2048]{2,1,0:T(8,128)(2,1)}, u32[]{:S(2)}, u32[]{:S(2)}) async-start(bf16[32,8,2048]{2,1,0:T(8,128)(2,1)} %fusion.10), calls=%async_computation.2 | async-start | bytes 2097152 | tf_op jit(solution)/shard_map/all_to_all | solution.py:61
  184.2 2.2 copy-start.5
  212.3 94.5 %all-to-all-start.3 = ((bf16[32,8,2048]{2,1,0:T(8,128)(2,1)}), bf16[32,8,2048]{2,1,0:T(8,128)(2,1)}, u32[]{:S(2)}, u32[]{:S(2)}) async-start(bf16[32,8,2048]{2,1,0:T(8,128)(2,1)} %fusion.14), calls=%async_computation.4 | async-start | bytes 2097152 | tf_op jit(solution)/shard_map/all_to_all | solution.py:68
  218.2 86.3 %all-reduce.2.cloned.1.call-start = ((), (), s32[]{:S(2)}) async-start(), calls=%async_computation.7 | async-start | bytes 2097152 | tf_op jit(solution)/shard_map/psum | solution.py:79
  304.5 17.3 %copy-start.1 = (bf16[256,2048]{1,0:T(8,128)(2,1)S(1)}, bf16[256,2048]{1,0:T(8,128)(2,1)}, u32[]{:S(2)}) copy-start(bf16[256,2048]{1,0:T(8,128)(2,1)} %all-reduce.2.cloned.1.call-done) | copy-start | bytes 3145732
  306.8 25.7 %all-to-all-start.2 = ((bf16[32,8,256]{2,1,0:T(8,128)(2,1)}), bf16[32,8,256]{2,1,0:T(8,128)(2,1)S(1)}, u32[]{:S(2)}, u32[]{:S(2)}) async-start(bf16[32,8,256]{2,1,0:T(8,128)(2,1)} %fusion.29), calls=%async_computation.3 | async-start | bytes 262144 | tf_op jit(solution)/shard_map/all_to_all | solution.py:87
  332.5 34.6 %all-to-all-start.4 = ((bf16[32,8,2048]{2,1,0:T(8,128)(2,1)}), bf16[32,8,2048]{2,1,0:T(8,128)(2,1)S(1)}, u32[]{:S(2)}, u32[]{:S(2)}) async-start(bf16[32,8,2048]{2,1,0:T(8,128)(2,1)} %fusion.11), calls=%async_computation.5 | async-start | bytes 2097152 | tf_op jit(solution)/shard_map/all_to_all | solution.py:94
Sparse Core Ops, SparseCore 0:
  17.3 153.4 reduce-scatter.1
  225.4 79.0 all-reduce.1
where the time goes:
time: 376 us; the launch traced here: 375 us
  waiting for transfers between devices  269 us (72%)
  starting transfers between devices  50.9 us (14%)
  matrix products  29.8 us (8%)
  between operations  14.2 us (4%)
  local copies, waits for them, and re-layouts  7.65 us (2%)
    reduce_scatter x1, waiting for transfers between devices, local(): lax.psum_scatter(lax.dot_general(features, cross_weight, (((1,), (1,)), (...  87.7 us
    psum x1, waiting for transfers between devices, local(): lax.psum(partial_pre.astype(jnp.bfloat16), 'row').astype(jnp.float32)  79.2 us
    all_to_all x1, waiting for transfers between devices, local(): lax.all_to_all(features, 'col', split_axis=0, concat_axis=1, tiled=True)  49.1 us
    all_to_all x1, waiting for transfers between devices, local(): lax.all_to_all(back_rows.reshape(sources, amount, feat_width), 'col', spl...  27.2 us
    all_to_all x1, waiting for transfers between devices, local(): lax.all_to_all(send_rows.reshape(col_count, capacity, feat_width), 'col',...  23 us
    all_to_all x1, starting transfers between devices, local(): lax.all_to_all(activated.reshape(sources, amount, out_share), 'col', spli...  15 us
    all_to_all x1, starting transfers between devices, local(): lax.all_to_all(features, 'col', split_axis=0, concat_axis=1, tiled=True)  12.7 us
    all_to_all x1, starting transfers between devices, local(): lax.all_to_all(send_rows.reshape(col_count, capacity, feat_width), 'col',...  10.9 us
  transfers between devices with their start and end apart: 7, of which 6 were waited for; matrix products, arithmetic and copies ran while one was open for 7% of the time, Pallas kernels for 0%

commit v1 on v0

v1 whole, which is shorter than its diff:
```python
import jax
import jax.numpy as jnp
from jax import lax
from jax.sharding import Mesh, PartitionSpec as P

COL = ("z", "xh", "core")
ALL = ("row", "z", "xh", "core")
ROWS_N, Z_N, XH_N, CORE_N = 8, 8, 2, 2
COL_N = Z_N * XH_N * CORE_N
CAP = 8


def swap(values, axis):
    return lax.ppermute(values, axis, [(0, 1), (1, 0)])


def piece(values, index, size, axis=0):
    return lax.dynamic_slice_in_dim(values, index * size, size, axis)


def slot_targets(expert_ids):
    flat = expert_ids.reshape(-1)
    count = flat.shape[0]
    order = jnp.arange(count, dtype=jnp.int32)
    same = (flat[:, None] == flat[None, :]) & (order[None, :] < order[:, None])
    position = jnp.sum(same.astype(jnp.int32), axis=1)
    return flat, position


def local(features, cross_weight, cross_bias, expert_ids, route_gates, expert_weight, mixed_grad):
    row_at = lax.axis_index("row")
    z_at = lax.axis_index("z")
    xh_at = lax.axis_index("xh")
    core_at = lax.axis_index("core")
    batch, block = features.shape
    width = cross_weight.shape[0]
    half = width // 2
    rows = expert_ids.shape[0]
    out_width = expert_weight.shape[2]
    share = out_width // ROWS_N
    slots = COL_N * CAP

    features_there = swap(features, "core")
    weight_there = swap(piece(cross_weight, 1 - core_at, half), "core")
    contract = (((1,), (1,)), ((), ()))
    products = lax.dot_general(
        features, piece(cross_weight, core_at, half), contract, preferred_element_type=jnp.float32
    )
    products = products + lax.dot_general(
        features_there, weight_there, contract, preferred_element_type=jnp.float32
    )
    part = lax.psum_scatter(
        products.astype(jnp.bfloat16), "z", scatter_dimension=0, tiled=True
    )

    perm = []
    for r in range(ROWS_N):
        for z in range(Z_N):
            for u in range(XH_N):
                for v in range(CORE_N):
                    src = ((r * Z_N + z) * XH_N + u) * CORE_N + v
                    dst = ((z * Z_N + r) * XH_N + v) * CORE_N + u
                    perm.append((src, dst))
    plane = lax.ppermute(piece(features, row_at, 4 * rows), ALL, perm)
    base_own = piece(plane, xh_at, 2 * rows)
    base_other = swap(piece(plane, 1 - xh_at, 2 * rows), "xh")
    first = xh_at == 0
    base = jnp.concatenate(
        [jnp.where(first, base_own, base_other), jnp.where(first, base_other, base_own)], axis=1
    ).astype(jnp.float32)

    ids_there = swap(expert_ids, "core")
    flat, position = slot_targets(expert_ids)
    flat_there, position_there = slot_targets(ids_there)
    places = jnp.arange(slots, dtype=jnp.int32)
    target = flat * CAP + position
    table = (places[:, None] == target[None, :]).astype(jnp.bfloat16)
    chooser = jnp.sum(table.reshape(slots, rows, 2), axis=2)
    chip_places = jnp.arange(2 * slots, dtype=jnp.int32)
    here = flat * (2 * CAP) + core_at * CAP + position
    there = flat_there * (2 * CAP) + (1 - core_at) * CAP + position_there
    chip_target = jnp.where(
        core_at == 0, jnp.concatenate([here, there]), jnp.concatenate([there, here])
    )
    chip_chooser = jnp.sum(
        (chip_places[:, None] == chip_target[None, :])
        .astype(jnp.bfloat16)
        .reshape(2 * slots, 2 * rows, 2),
        axis=2,
    )

    grad_share = piece(mixed_grad, row_at, share, 1).astype(jnp.float32)
    route_grad = (route_gates[:, :, None] * grad_share[:, None, :]).astype(jnp.bfloat16)
    send_grad = jnp.dot(
        table, route_grad.reshape(2 * rows, share), preferred_element_type=jnp.float32
    ).astype(jnp.bfloat16)
    routed_grad = lax.all_to_all(
        send_grad.reshape(COL_N, CAP, share), COL, split_axis=0, concat_axis=0, tiled=True
    ).reshape(slots, share)

    part_there = swap(piece(part, 1 - xh_at, 2 * rows), "xh")
    crossed = piece(part, xh_at, 2 * rows).astype(jnp.float32) + part_there.astype(jnp.float32)
    bias = piece(cross_bias, core_at, half)
    hidden = (base * (crossed + bias) + base).astype(jnp.bfloat16)
    send_rows = jnp.dot(chip_chooser, hidden, preferred_element_type=jnp.float32).astype(
        jnp.bfloat16
    )
    routed = lax.all_to_all(
        send_rows.reshape(COL_N, 2 * CAP, half), COL, split_axis=0, concat_axis=0, tiled=True
    ).reshape(COL_N // 2, 2, 2 * CAP, half)

    weight = expert_weight[0]
    pre = jnp.dot(
        routed[:, 0].reshape(slots, half), weight[:half], preferred_element_type=jnp.float32
    ) + jnp.dot(
        routed[:, 1].reshape(slots, half), weight[half:], preferred_element_type=jnp.float32
    )
    pre = pre.astype(jnp.bfloat16).reshape(slots, ROWS_N, share).transpose(1, 0, 2)
    parts = lax.all_to_all(pre, "row", split_axis=0, concat_axis=0, tiled=True)
    preact = jnp.sum(parts.astype(jnp.float32), axis=0)
    sigma = jax.nn.sigmoid(preact)
    activated = (preact * sigma).astype(jnp.bfloat16)
    slope = (
        routed_grad.astype(jnp.float32) * (sigma * (1.0 + preact * (1.0 - sigma)))
    ).astype(jnp.bfloat16)
    slopes = lax.all_to_all(
        jnp.broadcast_to(slope[None], (ROWS_N, slots, share)),
        "row",
        split_axis=0,
        concat_axis=0,
        tiled=True,
    )
    slope_grad = slopes.transpose(1, 0, 2).reshape(slots, out_width)
    back = lax.dot_general(
        slope_grad, weight, contract, preferred_element_type=jnp.float32
    ).astype(jnp.bfloat16)

    answer = jnp.concatenate([back, activated], axis=1).reshape(COL_N, CAP, width + share)
    returned = lax.all_to_all(answer, COL, split_axis=0, concat_axis=0, tiled=True).reshape(
        slots, width + share
    )
    pull = (((0,), (0,)), ((), ()))
    pair_act = lax.dot_general(
        table, returned[:, width:], pull, preferred_element_type=jnp.float32
    )
    combined = jnp.sum(
        route_gates[:, :, None] * pair_act.reshape(rows, 2, share), axis=1
    ).astype(jnp.bfloat16)
    cross_grad = lax.dot_general(
        chooser, returned[:, :width], pull, preferred_element_type=jnp.float32
    ).astype(jnp.bfloat16)
    return combined, cross_grad


def solution(mesh):
    split = Mesh(mesh.devices.reshape(ROWS_N, Z_N, XH_N, CORE_N), ALL)
    return jax.shard_map(
        local,
        mesh=split,
        in_specs=(
            P(None, COL),
            P("row", COL),
            P("row"),
            P(COL, None),
            P(COL, None),
            P(COL, "row", None),
            P(COL, None),
        ),
        out_specs=(P(COL, "row"), P(COL, "row")),
        check_vma=False,
    )
```

time: 376 us -> 259 us (0.69)
  waiting for transfers between devices: 269 us -> 126 us
  blocking collectives: 0 us -> 49.5 us
  starting transfers between devices: 50.9 us -> 31.4 us
  matrix products: 29.8 us -> 25.2 us
    psum x1 -> x0, waiting for transfers between devices: 79.2 us -> none  [local(): lax.psum(partial_pre.astype(jnp.bfloat16), 'row').astype(jnp.float32)]
    all_to_all x5 -> x3, waiting for transfers between devices: 103 us -> 52.8 us  [the longest x1 30.3 us: local(): lax.all_to_all(answer, COL, split_axis=0, concat_axis=0, tiled=True)]
    all_to_all x0 -> x2, blocking collectives: none -> 49.5 us  [the longest x1 32.5 us: local(): lax.all_to_all(send_rows.reshape(COL_N, 2 * CAP, half), COL, split_axis=0...]
    reduce_scatter x1, waiting for transfers between devices: 87.7 us -> 46.4 us  [local(): lax.psum_scatter(products.astype(jnp.bfloat16), 'z', scatter_dimension=0,...]
    all_to_all x5 -> x3, starting transfers between devices: 50.9 us -> 21.3 us  [the longest x1 7.85 us: local(): parts = lax.all_to_all(pre, 'row', split_axis=0, concat_axis=0, tiled=True)]
    ppermute x0 -> x6, waiting for transfers between devices: none -> 26.8 us  [the longest x1 19.6 us: local(): plane = lax.ppermute(piece(features, row_at, 4 * rows), ALL, perm)]
    ppermute x0 -> x6, starting transfers between devices: none -> 10 us  [the longest x5 6.92 us: swap(): return lax.ppermute(values, axis, [(0, 1), (1, 0)])]
    dot_general x7 -> x9, matrix products: 29.8 us -> 25.2 us  [the longest x1 6.23 us: local(): lax.dot_general(features_there, weight_there, contract, preferred_element...]
  transfers between devices with their start and end apart: 7 -> 10, of which waited for: 6 -> 6; matrix products, arithmetic and copies ran while one was open for 7% -> 4% of each run, Pallas kernels for 0% -> 0%
where the time goes in v1:
time: 259 us; the launch traced here: 258 us
  waiting for transfers between devices  126 us (49%)
  blocking collectives  49.5 us (19%)
  starting transfers between devices  31.4 us (12%)
  matrix products  25.2 us (10%)
  between operations  14.4 us (6%)
  local copies, waits for them, and re-layouts  6.11 us (2%)
  other arithmetic  4.95 us (2%)
    reduce_scatter x1, waiting for transfers between devices, local(): lax.psum_scatter(products.astype(jnp.bfloat16), 'z', scatter_dimension=0,...  46.4 us
    all_to_all x1, blocking collectives, local(): lax.all_to_all(send_rows.reshape(COL_N, 2 * CAP, half), COL, split_axis=0...  32.5 us
    all_to_all x1, waiting for transfers between devices, local(): lax.all_to_all(answer, COL, split_axis=0, concat_axis=0, tiled=True)  30.3 us
    ppermute x1, waiting for transfers between devices, local(): plane = lax.ppermute(piece(features, row_at, 4 * rows), ALL, perm)  19.6 us
    all_to_all x1, blocking collectives, local(): lax.all_to_all(jnp.broadcast_to(slope[None], (ROWS_N, slots, share)), 'ro...  16.9 us
    all_to_all x1, waiting for transfers between devices, local(): parts = lax.all_to_all(pre, 'row', split_axis=0, concat_axis=0, tiled=True)  11.9 us
    all_to_all x1, waiting for transfers between devices, local(): lax.all_to_all(send_grad.reshape(COL_N, CAP, share), COL, split_axis=0, c...  10.6 us
    all_to_all x1, starting transfers between devices, local(): parts = lax.all_to_all(pre, 'row', split_axis=0, concat_axis=0, tiled=True)  7.85 us
  transfers between devices with their start and end apart: 10, of which 6 were waited for; matrix products, arithmetic and copies ran while one was open for 4% of the time, Pallas kernels for 0%

profile of v1, /device:TPU:1, one launch (start us, length us, event | category | flops | bytes accessed | tf_op | source)
XLA Modules:
  0.0 257.6 jit_solution(7820738367043443382)
XLA Ops:
  7.2 3.3 %collective-permute-start.4 = (bf16[2048,512]{1,0:T(8,128)(2,1)}, bf16[2048,512]{1,0:T(8,128)(2,1)}, u32[]{:S(2)}, u32[]{:S(2)}) collective-permute-start(bf16[2048,512]{1,0:T(8,128)(2,1)} %param.7), channel_id=1, source_target_pairs={{0,1},{1,0},{2,3},{3,2},{4,5},{5,4},{6,7},{7,6},{8,9},{9,8},{10,11... | collective-permute-start | bytes 6291464 | tf_op jit(solution)/shard_map/ppermute | solution.py:14
  10.6 1.5 collective-permute-start.3
  12.2 4.0 %fusion.20 = f32[1024,2048]{1,0:T(8,128)S(1)} fusion(bf16[2048,512]{1,0:T(8,128)(2,1)} %param.7, bf16[2048,512]{1,0:T(8,128)(2,1)S(1)} %copy-done, s32[]{:T(128)} %select_n.55), kind=kOutput, calls=%fused_computation.21 | convolution fusion | flops 2147483648 | bytes 11534340 | tf_op jit(solution)/shard_map/dot_general | solution.py:46
  16.1 6.2 %fusion.2 = bf16[2048,1024]{0,1:T(8,128)(2,1)} fusion(f32[1024,2048]{1,0:T(8,128)S(1)} %fusion.20, bf16[1024,512]{1,0:T(8,128)(2,1)} %collective-permute-done.3, bf16[2048,512]{1,0:T(8,128)(2,1)} %collective-permute-done.4), kind=kOutput, calls=%fused_computation.3 | convolution fusion | flops 2151677952 | bytes 15728640 | tf_op jit(solution)/shard_map/dot_general | solution.py:49
  24.4 3.1 %collective-permute-start.1 = (bf16[256,512]{0,1:T(8,128)(2,1)S(1)}, bf16[256,512]{0,1:T(8,128)(2,1)S(1)}, u32[]{:S(2)}, u32[]{:S(2)}) collective-permute-start(bf16[256,512]{0,1:T(8,128)(2,1)S(1)} %copy.63), channel_id=1, source_target_pairs={{0,0},{1,2},{2,1},{3,3},{4,32},{5,34},{6,33},{7,35},{8,64},{9,66},... | collective-permute-start | bytes 786440 | tf_op jit(solution)/shard_map/ppermute | solution.py:64
  29.3 19.6 %collective-permute-done.1 = bf16[256,512]{0,1:T(8,128)(2,1)S(1)} collective-permute-done((bf16[256,512]{0,1:T(8,128)(2,1)S(1)}, bf16[256,512]{0,1:T(8,128)(2,1)S(1)}, u32[]{:S(2)}, u32[]{:S(2)}) %collective-permute-start.1) | collective-permute-done | bytes 262176 | tf_op jit(solution)/shard_map/ppermute | solution.py:64
  49.1 46.4 %reduce-scatter.2.cloned.1.call-done = bf16[256,1024]{0,1:T(8,128)(2,1)} async-done(((bf16[2048,1024]{0,1:T(8,128)(2,1)}), bf16[256,1024]{0,1:T(8,128)(2,1)}) %reduce-scatter.2.cloned.1.call-update) | async-done | bytes 524304 | tf_op jit(solution)/shard_map/reduce_scatter | solution.py:52
  95.5 1.1 constant_dynamic-slice_fusion
  96.6 1.8 collective-permute-start.5
  98.5 7.2 %collective-permute-done.5 = bf16[128,1024]{0,1:T(8,128)(2,1)S(1)} collective-permute-done((bf16[128,1024]{0,1:T(8,128)(2,1)S(1)}, bf16[128,1024]{0,1:T(8,128)(2,1)S(1)}, u32[]{:S(2)}, u32[]{:S(2)}) %collective-permute-start.5) | collective-permute-done | bytes 262176 | tf_op jit(solution)/shard_map/ppermute | solution.py:14
  105.7 1.5 convolution_convert_fusion.1
  107.2 32.5 %all_to_all.25 = bf16[32,16,1024]{2,1,0:T(8,128)(2,1)S(1)} all-to-all(bf16[32,16,1024]{2,1,0:T(8,128)(2,1)S(1)} %bitcast.54), channel_id=1, replica_groups=mesh['row'=8,'z'=8,'xh'=2,'core'=2] {'z','xh','core'}, dimensions={0} | all-to-all | bytes 2097152 | tf_op jit(solution)/shard_map/all_to_all | solution.py:108
  139.9 3.6 %fusion.3 = f32[256,2048]{1,0:T(8,128)S(1)} fusion(bf16[256,1024]{1,0:T(8,128)(2,1)S(1)} %bitcast.59, bf16[1,2048,2048]{2,1,0:T(8,128)(2,1)} %param.12), kind=kOutput, calls=%fused_computation.4 | convolution fusion | flops 1073741824 | bytes 6815744 | tf_op jit(solution)/shard_map/dot_general | solution.py:115
  143.5 1.3 fusion.12
  145.8 7.9 %all-to-all-start.2 = ((bf16[8,256,256]{2,1,0:T(8,128)(2,1)}), bf16[8,256,256]{2,1,0:T(8,128)(2,1)S(1)}, u32[]{:S(2)}, u32[]{:S(2)}) async-start(bf16[8,256,256]{2,1,0:T(8,128)(2,1)} %bitcast.53), calls=%async_computation.3 | async-start | bytes 2097152 | tf_op jit(solution)/shard_map/all_to_all | solution.py:119
  155.8 11.9 %all-to-all-done.2 = bf16[8,256,256]{2,1,0:T(8,128)(2,1)S(1)} async-done(((bf16[8,256,256]{2,1,0:T(8,128)(2,1)}), bf16[8,256,256]{2,1,0:T(8,128)(2,1)S(1)}, u32[]{:S(2)}, u32[]{:S(2)}) %all-to-all-start.2) | async-done | bytes 1048608 | tf_op jit(solution)/shard_map/all_to_all | solution.py:119
  167.7 7.6 %all-to-all-start = ((bf16[32,8,256]{2,1,0:T(8,128)(2,1)}), bf16[32,8,256]{2,1,0:T(8,128)(2,1)S(1)}, u32[]{:S(2)}, u32[]{:S(2)}) async-start(bf16[32,8,256]{2,1,0:T(8,128)(2,1)} %fusion.18), calls=%async_computation | async-start | bytes 262144 | tf_op jit(solution)/shard_map/all_to_all | solution.py:97
  175.5 10.6 %all-to-all-done = bf16[32,8,256]{2,1,0:T(8,128)(2,1)S(1)} async-done(((bf16[32,8,256]{2,1,0:T(8,128)(2,1)}), bf16[32,8,256]{2,1,0:T(8,128)(2,1)S(1)}, u32[]{:S(2)}, u32[]{:S(2)}) %all-to-all-start) | async-done | bytes 131104 | tf_op jit(solution)/shard_map/all_to_all | solution.py:97
  186.4 16.9 %all_to_all.26 = bf16[8,256,256]{1,2,0:T(8,128)(2,1)S(1)} all-to-all(bf16[8,256,256]{1,2,0:T(8,128)(2,1)S(1)} %broadcast_in_dim.2), channel_id=1, replica_groups=mesh['row'=8,'z'=8,'xh'=2,'core'=2] {'row'}, dimensions={0} | all-to-all | bytes 2097152 | tf_op jit(solution)/shard_map/all_to_all | solution.py:126
  203.3 5.8 %fusion.15 = bf16[256,2048]{1,0:T(8,128)(2,1)S(1)} fusion(bf16[256,2048]{0,1:T(8,128)(2,1)S(1)} %bitcast.57, bf16[1,2048,2048]{2,1,0:T(8,128)(2,1)} %param.12), kind=kOutput, calls=%fused_computation.12 | convolution fusion | flops 2148007936 | bytes 10485760 | tf_op jit(solution)/shard_map/dot_general | solution.py:134
  210.2 5.9 %all-to-all-start.4 = ((bf16[32,8,2304]{2,1,0:T(8,128)(2,1)}), bf16[32,8,2304]{2,1,0:T(8,128)(2,1)S(1)}, u32[]{:S(2)}, u32[]{:S(2)}) async-start(bf16[32,8,2304]{2,1,0:T(8,128)(2,1)} %maximum_bitcast_fusion), calls=%async_computation.5 | async-start | bytes 2359296 | tf_op jit(solution)/shard_map/all_to_all | solution.py:139
  216.8 30.3 %all-to-all-done.4 = bf16[32,8,2304]{2,1,0:T(8,128)(2,1)S(1)} async-done(((bf16[32,8,2304]{2,1,0:T(8,128)(2,1)}), bf16[32,8,2304]{2,1,0:T(8,128)(2,1)S(1)}, u32[]{:S(2)}, u32[]{:S(2)}) %all-to-all-start.4) | async-done | bytes 1179680 | tf_op jit(solution)/shard_map/all_to_all | solution.py:139
  247.4 1.6 multiply_reduce_fusion
  249.0 1.8 convolution_convert_fusion
  (65 shorter events, 9.8 us)
Async XLA Ops:
  7.2 3.4 %copy-start = (bf16[2048,512]{1,0:T(8,128)(2,1)S(1)}, bf16[2048,512]{1,0:T(8,128)(2,1)}, u32[]{:S(2)}) copy-start(bf16[2048,512]{1,0:T(8,128)(2,1)} %param.8) | copy-start | bytes 6291460
  7.2 88.3 %reduce-scatter.2.cloned.1.call-start = ((), (), s32[]{:S(2)}) async-start(), calls=%async_computation.6 | async-start | bytes 4718592 | tf_op jit(solution)/shard_map/reduce_scatter | solution.py:52
  7.2 8.9 %collective-permute-start.4 = (bf16[2048,512]{1,0:T(8,128)(2,1)}, bf16[2048,512]{1,0:T(8,128)(2,1)}, u32[]{:S(2)}, u32[]{:S(2)}) collective-permute-start(bf16[2048,512]{1,0:T(8,128)(2,1)} %param.7), channel_id=1, source_target_pairs={{0,1},{1,0},{2,3},{3,2},{4,5},{5,4},{6,7},{7,6},{8,9},{9,8},{10,11... | collective-permute-start | bytes 6291464 | tf_op jit(solution)/shard_map/ppermute | solution.py:14
  10.6 5.5 %collective-permute-start.3 = (bf16[1024,512]{1,0:T(8,128)(2,1)S(1)}, bf16[1024,512]{1,0:T(8,128)(2,1)}, u32[]{:S(2)}, u32[]{:S(2)}) collective-permute-start(bf16[1024,512]{1,0:T(8,128)(2,1)S(1)} %constant_dynamic-slice_fusion.1), channel_id=1, source_target_pairs={{0,1},{1,0},{2,3},{3,2},{4,5},{5,4},{6,7},{7,6},{8,9},{9,8},{10,11... | collective-permute-start | bytes 3145736 | tf_op jit(solution)/shard_map/ppermute | solution.py:14
  22.4 0.7 copy-start.2
  23.1 82.6 %dynamic-slice-start = ((f32[2048]{0:T(1024)}, s32[]{:T(128)}), f32[1024]{0:T(1024)S(1)}, s32[]{:S(2)}) async-start(f32[2048]{0:T(1024)} %param.9, s32[]{:T(128)} %select_n.55), calls=%async_computation.7 | async-start | bytes 8704 | tf_op jit(solution)/shard_map/dynamic_slice | solution.py:18
  23.1 5.4 %collective-permute-start = (s32[64,2]{0,1:T(2,128)S(1)}, s32[64,2]{0,1:T(2,128)S(1)}, u32[]{:S(2)}, u32[]{:S(2)}) collective-permute-start(s32[64,2]{0,1:T(2,128)S(1)} %copy-done.2), channel_id=1, source_target_pairs={{0,1},{1,0},{2,3},{3,2},{4,5},{5,4},{6,7},{7,6},{8,9},{9,8},{10,11... | collective-permute-start | bytes 1544 | tf_op jit(solution)/shard_map/ppermute | solution.py:14
  24.4 24.6 %collective-permute-start.1 = (bf16[256,512]{0,1:T(8,128)(2,1)S(1)}, bf16[256,512]{0,1:T(8,128)(2,1)S(1)}, u32[]{:S(2)}, u32[]{:S(2)}) collective-permute-start(bf16[256,512]{0,1:T(8,128)(2,1)S(1)} %copy.63), channel_id=1, source_target_pairs={{0,0},{1,2},{2,1},{3,3},{4,32},{5,34},{6,33},{7,35},{8,64},{9,66},... | collective-permute-start | bytes 786440 | tf_op jit(solution)/shard_map/ppermute | solution.py:64
  49.0 49.5 %collective-permute-start.2 = (bf16[128,512]{0,1:T(8,128)(2,1)S(1)}, bf16[128,512]{0,1:T(8,128)(2,1)S(1)}, u32[]{:S(2)}, u32[]{:S(2)}) collective-permute-start(bf16[128,512]{0,1:T(8,128)(2,1)S(1)} %constant_dynamic-slice_fusion.2), channel_id=1, source_target_pairs={{0,2},{2,0},{1,3},{3,1},{4,6},{6,4},{5,7},{7,5},{8,10},{10,8},{9,1... | collective-permute-start | bytes 393224 | tf_op jit(solution)/shard_map/ppermute | solution.py:14
  95.5 48.0 %slice-start = ((s8[8388608]{0:T(1024)(128)(4,1)}), s8[4194304]{0:T(1024)(128)(4,1)S(1)}, s32[]{:S(2)}) async-start(s8[8388608]{0:T(1024)(128)(4,1)} %bitcast.60), calls=%async_computation.8 | async-start | bytes 8388608
  96.6 9.1 %collective-permute-start.5 = (bf16[128,1024]{0,1:T(8,128)(2,1)S(1)}, bf16[128,1024]{0,1:T(8,128)(2,1)S(1)}, u32[]{:S(2)}, u32[]{:S(2)}) collective-permute-start(bf16[128,1024]{0,1:T(8,128)(2,1)S(1)} %constant_dynamic-slice_fusion), channel_id=1, source_target_pairs={{0,2},{2,0},{1,3},{3,1},{4,6},{6,4},{5,7},{7,5},{8,10},{10,8},{9,1... | collective-permute-start | bytes 786440 | tf_op jit(solution)/shard_map/ppermute | solution.py:14
  139.8 3.6 %slice-start.1 = ((s8[8388608]{0:T(1024)(128)(4,1)}), s8[4194304]{0:T(1024)(128)(4,1)S(1)}, s32[]{:S(2)}) async-start(s8[8388608]{0:T(1024)(128)(4,1)} %bitcast.60), calls=%async_computation.9 | async-start | bytes 8388608
  144.8 9.8 %copy-start.3 = (f32[64,2]{0,1:T(2,128)S(1)}, f32[64,2]{0,1:T(2,128)}, u32[]{:S(2)}) copy-start(f32[64,2]{0,1:T(2,128)} %param.11) | copy-start | bytes 1540
  145.8 21.9 %all-to-all-start.2 = ((bf16[8,256,256]{2,1,0:T(8,128)(2,1)}), bf16[8,256,256]{2,1,0:T(8,128)(2,1)S(1)}, u32[]{:S(2)}, u32[]{:S(2)}) async-start(bf16[8,256,256]{2,1,0:T(8,128)(2,1)} %bitcast.53), calls=%async_computation.3 | async-start | bytes 2097152 | tf_op jit(solution)/shard_map/all_to_all | solution.py:119
  154.7 13.0 %copy-start.1 = (f32[64,2]{1,0:T(8,128)}, f32[64,2]{1,0:T(8,128)S(1)}, u32[]{:S(2)}) copy-start(f32[64,2]{1,0:T(8,128)S(1)} %copy.52) | copy-start | bytes 1540
  167.7 18.4 %all-to-all-start = ((bf16[32,8,256]{2,1,0:T(8,128)(2,1)}), bf16[32,8,256]{2,1,0:T(8,128)(2,1)S(1)}, u32[]{:S(2)}, u32[]{:S(2)}) async-start(bf16[32,8,256]{2,1,0:T(8,128)(2,1)} %fusion.18), calls=%async_computation | async-start | bytes 262144 | tf_op jit(solution)/shard_map/all_to_all | solution.py:97
  210.2 36.8 %all-to-all-start.4 = ((bf16[32,8,2304]{2,1,0:T(8,128)(2,1)}), bf16[32,8,2304]{2,1,0:T(8,128)(2,1)S(1)}, u32[]{:S(2)}, u32[]{:S(2)}) async-start(bf16[32,8,2304]{2,1,0:T(8,128)(2,1)} %maximum_bitcast_fusion), calls=%async_computation.5 | async-start | bytes 2359296 | tf_op jit(solution)/shard_map/all_to_all | solution.py:139
Sparse Core Ops, SparseCore 0:
  22.5 72.9 reduce-scatter.1

commit v2 on v1

--- a/solution.py
+++ b/solution.py
@@ -40,6 +40,12 @@
     share = out_width // ROWS_N
     slots = COL_N * CAP
 
+    plane_there = (3 * z_at + row_at) % Z_N
+    perm = [
+        (r * Z_N + z, r * Z_N + (3 * z + r) % Z_N) for r in range(ROWS_N) for z in range(Z_N)
+    ]
+    plane = lax.ppermute(piece(features, plane_there, 4 * rows), ("row", "z"), perm)
+
     features_there = swap(features, "core")
     weight_there = swap(piece(cross_weight, 1 - core_at, half), "core")
     contract = (((1,), (1,)), ((), ()))
@@ -49,9 +55,8 @@
     products = products + lax.dot_general(
         features_there, weight_there, contract, preferred_element_type=jnp.float32
     )
-    part = lax.psum_scatter(
-        products.astype(jnp.bfloat16), "z", scatter_dimension=0, tiled=True
-    )
+    products, plane = lax.optimization_barrier((products.astype(jnp.bfloat16), plane))
+    part = lax.psum_scatter(products, "z", scatter_dimension=0, tiled=True)
 
     perm = []
     for r in range(ROWS_N):
@@ -59,9 +64,9 @@
             for u in range(XH_N):
                 for v in range(CORE_N):
                     src = ((r * Z_N + z) * XH_N + u) * CORE_N + v
-                    dst = ((z * Z_N + r) * XH_N + v) * CORE_N + u
+                    dst = ((3 * (z - r) % Z_N * Z_N + z) * XH_N + v) * CORE_N + u
                     perm.append((src, dst))
-    plane = lax.ppermute(piece(features, row_at, 4 * rows), ALL, perm)
+    plane = lax.ppermute(plane, ALL, perm)
     base_own = piece(plane, xh_at, 2 * rows)
     base_other = swap(piece(plane, 1 - xh_at, 2 * rows), "xh")
     first = xh_at == 0
@@ -98,6 +103,9 @@
         send_grad.reshape(COL_N, CAP, share), COL, split_axis=0, concat_axis=0, tiled=True
     ).reshape(slots, share)
 
+    part, base, routed_grad, chip_chooser, chooser, table = lax.optimization_barrier(
+        (part, base, routed_grad, chip_chooser, chooser, table)
+    )
     part_there = swap(piece(part, 1 - xh_at, 2 * rows), "xh")
     crossed = piece(part, xh_at, 2 * rows).astype(jnp.float32) + part_there.astype(jnp.float32)
     bias = piece(cross_bias, core_at, half)

time: 259 us -> 240 us (0.927)
  waiting for transfers between devices: 126 us -> 45.8 us
  blocking collectives: 49.5 us -> 113 us
    all_to_all x0 -> x2, blocking collectives: none -> 60.2 us  [the longest x1 43 us: local(): lax.all_to_all(answer, COL, split_axis=0, concat_axis=0, tiled=True)]
    all_to_all x2 -> x0, waiting for transfers between devices: 42.2 us -> none  [the longest x1 30.3 us: local(): lax.all_to_all(answer, COL, split_axis=0, concat_axis=0, tiled=True)]
    reduce_scatter x1, waiting for transfers between devices: 46.4 us -> 28.9 us  [local(): part = lax.psum_scatter(products, 'z', scatter_dimension=0, tiled=True)]
    ppermute x1 -> x2, waiting for transfers between devices: 19.6 us -> 4.58 us  [the longest x1 4.58 us: local(): plane = lax.ppermute(plane, ALL, perm)]
    all_to_all x2 -> x0, starting transfers between devices: 13.7 us -> none  [the longest x1 7.85 us: local(): parts = lax.all_to_all(pre, 'row', split_axis=0, concat_axis=0, tiled=True)]
    all_to_all x1, waiting for transfers between devices: 10.6 us -> 0.01 us  [local(): lax.all_to_all(send_grad.reshape(COL_N, CAP, share), COL, split_axis=0, c...]
    all_to_all x1, starting transfers between devices: 7.6 us -> 14.5 us  [local(): lax.all_to_all(send_grad.reshape(COL_N, CAP, share), COL, split_axis=0, c...]
    ppermute x5, waiting for transfers between devices: 7.18 us -> 12.3 us  [swap(): return lax.ppermute(values, axis, [(0, 1), (1, 0)])]
  transfers between devices with their start and end apart: 10 -> 9, of which waited for: 6 -> 4; matrix products, arithmetic and copies ran while one was open for 4% -> 7% of each run, Pallas kernels for 0% -> 0%
where the time goes in v2:
time: 240 us; the launch traced here: 239 us
  blocking collectives  113 us (47%)
  waiting for transfers between devices  45.8 us (19%)
  starting transfers between devices  29 us (12%)
  matrix products  27.3 us (11%)
  between operations  14.3 us (6%)
  local copies, waits for them, and re-layouts  5.69 us (2%)
  other arithmetic  4.02 us (2%)
    all_to_all x1, blocking collectives, local(): lax.all_to_all(answer, COL, split_axis=0, concat_axis=0, tiled=True)  43 us
    all_to_all x1, blocking collectives, local(): lax.all_to_all(send_rows.reshape(COL_N, 2 * CAP, half), COL, split_axis=0...  36 us
    reduce_scatter x1, waiting for transfers between devices, local(): part = lax.psum_scatter(products, 'z', scatter_dimension=0, tiled=True)  28.9 us
    all_to_all x1, blocking collectives, local(): parts = lax.all_to_all(pre, 'row', split_axis=0, concat_axis=0, tiled=True)  17.2 us
    all_to_all x1, blocking collectives, local(): lax.all_to_all(jnp.broadcast_to(slope[None], (ROWS_N, slots, share)), 'ro...  16.4 us
    all_to_all x1, starting transfers between devices, local(): lax.all_to_all(send_grad.reshape(COL_N, CAP, share), COL, split_axis=0, c...  14.5 us
    ppermute x5, waiting for transfers between devices, swap(): return lax.ppermute(values, axis, [(0, 1), (1, 0)])  12.3 us
    ppermute x5, starting transfers between devices, swap(): return lax.ppermute(values, axis, [(0, 1), (1, 0)])  7.78 us
  transfers between devices with their start and end apart: 9, of which 4 were waited for; matrix products, arithmetic and copies ran while one was open for 7% of the time, Pallas kernels for 0%

profile of v2, /device:TPU:1, one launch (start us, length us, event | category | flops | bytes accessed | tf_op | source)
XLA Modules:
  0.0 238.7 jit_solution(14560981231298517845)
XLA Ops:
  7.2 3.3 %collective-permute-start.1 = (bf16[2048,512]{1,0:T(8,128)(2,1)}, bf16[2048,512]{1,0:T(8,128)(2,1)}, u32[]{:S(2)}, u32[]{:S(2)}) collective-permute-start(bf16[2048,512]{1,0:T(8,128)(2,1)} %param.7), channel_id=1, source_target_pairs={{0,1},{1,0},{2,3},{3,2},{4,5},{5,4},{6,7},{7,6},{8,9},{9,8},{10,11... | collective-permute-start | bytes 6291464 | tf_op jit(solution)/shard_map/ppermute | solution.py:14
  10.6 1.5 collective-permute-start
  12.2 1.0 constant_dynamic-slice_fusion.2
  14.0 1.6 collective-permute-start.2
  15.6 4.0 %fusion.20 = f32[1024,2048]{1,0:T(8,128)S(1)} fusion(bf16[2048,512]{1,0:T(8,128)(2,1)} %param.7, bf16[2048,512]{1,0:T(8,128)(2,1)S(1)} %copy-done, s32[]{:T(128)} %select_n.55), kind=kOutput, calls=%fused_computation.21 | convolution fusion | flops 2147483648 | bytes 11534340 | tf_op jit(solution)/shard_map/dot_general | solution.py:52
  19.6 6.2 %fusion.2 = bf16[2048,1024]{0,1:T(8,128)(2,1)} fusion(f32[1024,2048]{1,0:T(8,128)S(1)} %fusion.20, bf16[1024,512]{1,0:T(8,128)(2,1)} %collective-permute-done, bf16[2048,512]{1,0:T(8,128)(2,1)} %collective-permute-done.1), kind=kOutput, calls=%fused_computation.3 | convolution fusion | flops 2151677952 | bytes 15728640 | tf_op jit(solution)/shard_map/dot_general | solution.py:55
  29.0 14.5 %all-to-all-start = ((bf16[32,8,256]{2,1,0:T(8,128)(2,1)}), bf16[32,8,256]{2,1,0:T(8,128)(2,1)S(1)}, u32[]{:S(2)}, u32[]{:S(2)}) async-start(bf16[32,8,256]{2,1,0:T(8,128)(2,1)} %fusion.18), calls=%async_computation.1 | async-start | bytes 262144 | tf_op jit(solution)/shard_map/all_to_all | solution.py:102
  44.7 5.0 %collective-permute-start.3 = (bf16[256,512]{0,1:T(8,128)(2,1)}, bf16[256,512]{0,1:T(8,128)(2,1)S(1)}, u32[]{:S(2)}, u32[]{:S(2)}) collective-permute-start(bf16[256,512]{0,1:T(8,128)(2,1)} %copy-done.4), channel_id=1, source_target_pairs={{0,0},{1,2},{2,1},{3,3},{4,100},{5,102},{6,101},{7,103},{8,200},{9... | collective-permute-start | bytes 786440 | tf_op jit(solution)/shard_map/ppermute | solution.py:69
  50.5 4.6 %collective-permute-done.3 = bf16[256,512]{0,1:T(8,128)(2,1)S(1)} collective-permute-done((bf16[256,512]{0,1:T(8,128)(2,1)}, bf16[256,512]{0,1:T(8,128)(2,1)S(1)}, u32[]{:S(2)}, u32[]{:S(2)}) %collective-permute-start.3) | collective-permute-done | bytes 262176 | tf_op jit(solution)/shard_map/ppermute | solution.py:69
  55.5 6.1 %collective-permute-done.4 = bf16[128,512]{0,1:T(8,128)(2,1)S(1)} collective-permute-done((bf16[128,512]{0,1:T(8,128)(2,1)S(1)}, bf16[128,512]{0,1:T(8,128)(2,1)S(1)}, u32[]{:S(2)}, u32[]{:S(2)}) %collective-permute-start.4) | collective-permute-done | bytes 131104 | tf_op jit(solution)/shard_map/ppermute | solution.py:14
  61.7 28.9 %reduce-scatter.2.cloned.1.call-done = bf16[256,1024]{0,1:T(8,128)(2,1)} async-done(((bf16[2048,1024]{0,1:T(8,128)(2,1)}), bf16[256,1024]{0,1:T(8,128)(2,1)}) %reduce-scatter.2.cloned.1.call-update) | async-done | bytes 524304 | tf_op jit(solution)/shard_map/reduce_scatter | solution.py:59
  90.6 1.0 constant_dynamic-slice_fusion
  91.5 2.8 %collective-permute-start.6 = (bf16[128,1024]{0,1:T(8,128)(2,1)S(1)}, bf16[128,1024]{0,1:T(8,128)(2,1)S(1)}, u32[]{:S(2)}, u32[]{:S(2)}) collective-permute-start(bf16[128,1024]{0,1:T(8,128)(2,1)S(1)} %constant_dynamic-slice_fusion), channel_id=1, source_target_pairs={{0,2},{2,0},{1,3},{3,1},{4,6},{6,4},{5,7},{7,5},{8,10},{10,8},{9,1... | collective-permute-start | bytes 786440 | tf_op jit(solution)/shard_map/ppermute | solution.py:14
  94.3 6.3 %collective-permute-done.6 = bf16[128,1024]{0,1:T(8,128)(2,1)S(1)} collective-permute-done((bf16[128,1024]{0,1:T(8,128)(2,1)S(1)}, bf16[128,1024]{0,1:T(8,128)(2,1)S(1)}, u32[]{:S(2)}, u32[]{:S(2)}) %collective-permute-start.6) | collective-permute-done | bytes 262176 | tf_op jit(solution)/shard_map/ppermute | solution.py:14
  100.6 1.5 convolution_convert_fusion.1
  102.1 36.0 %all_to_all.25 = bf16[32,16,1024]{2,1,0:T(8,128)(2,1)S(1)} all-to-all(bf16[32,16,1024]{2,1,0:T(8,128)(2,1)S(1)} %bitcast.52), channel_id=1, replica_groups=mesh['row'=8,'z'=8,'xh'=2,'core'=2] {'z','xh','core'}, dimensions={0} | all-to-all | bytes 2097152 | tf_op jit(solution)/shard_map/all_to_all | solution.py:116
  138.3 3.4 %fusion.3 = f32[256,2048]{1,0:T(8,128)S(1)} fusion(bf16[256,1024]{1,0:T(8,128)(2,1)S(1)} %bitcast.59, bf16[1,2048,2048]{2,1,0:T(8,128)(2,1)} %param.12), kind=kOutput, calls=%fused_computation.4 | convolution fusion | flops 1073741824 | bytes 6815744 | tf_op jit(solution)/shard_map/dot_general | solution.py:123
  141.7 3.5 %fusion.12 = bf16[256,2048]{1,0:T(8,128)(2,1)S(1)} fusion(f32[256,2048]{1,0:T(8,128)S(1)} %fusion.3, bf16[256,1024]{1,0:T(8,128)(2,1)S(1)} %bitcast.58, bf16[1,2048,2048]{2,1,0:T(8,128)(2,1)} %param.12), kind=kOutput, calls=%fused_computation.11 | convolution fusion | flops 1074790400 | bytes 7864320 | tf_op jit(solution)/shard_map/dot_general | solution.py:121
  145.3 17.2 %all_to_all.26 = bf16[8,256,256]{2,1,0:T(8,128)(2,1)S(1)} all-to-all(bf16[8,256,256]{2,1,0:T(8,128)(2,1)S(1)} %bitcast.54), channel_id=1, replica_groups=mesh['row'=8,'z'=8,'xh'=2,'core'=2] {'row'}, dimensions={0} | all-to-all | bytes 2097152 | tf_op jit(solution)/shard_map/all_to_all | solution.py:127
  163.0 16.4 %all_to_all.27 = bf16[8,256,256]{1,2,0:T(8,128)(2,1)S(1)} all-to-all(bf16[8,256,256]{1,2,0:T(8,128)(2,1)S(1)} %broadcast_in_dim.2), channel_id=1, replica_groups=mesh['row'=8,'z'=8,'xh'=2,'core'=2] {'row'}, dimensions={0} | all-to-all | bytes 2097152 | tf_op jit(solution)/shard_map/all_to_all | solution.py:134
  179.4 5.8 %fusion.15 = bf16[256,2048]{1,0:T(8,128)(2,1)S(1)} fusion(bf16[256,2048]{0,1:T(8,128)(2,1)S(1)} %bitcast.56, bf16[1,2048,2048]{2,1,0:T(8,128)(2,1)} %param.12), kind=kOutput, calls=%fused_computation.12 | convolution fusion | flops 2148007936 | bytes 10485760 | tf_op jit(solution)/shard_map/dot_general | solution.py:142
  185.2 43.0 %all_to_all.28 = bf16[32,8,2304]{2,1,0:T(8,128)(2,1)S(1)} all-to-all(bf16[32,8,2304]{2,1,0:T(8,128)(2,1)S(1)} %maximum_bitcast_fusion), channel_id=1, replica_groups=mesh['row'=8,'z'=8,'xh'=2,'core'=2] {'z','xh','core'}, dimensions={0} | all-to-all | bytes 2359296 | tf_op jit(solution)/shard_map/all_to_all | solution.py:147
  228.5 1.6 multiply_reduce_fusion
  230.1 1.8 convolution_convert_fusion
  (64 shorter events, 7.5 us)
Async XLA Ops:
  7.2 3.4 %copy-start = (bf16[2048,512]{1,0:T(8,128)(2,1)S(1)}, bf16[2048,512]{1,0:T(8,128)(2,1)}, u32[]{:S(2)}) copy-start(bf16[2048,512]{1,0:T(8,128)(2,1)} %param.8) | copy-start | bytes 6291460
  7.2 83.4 %reduce-scatter.2.cloned.1.call-start = ((), (), s32[]{:S(2)}) async-start(), calls=%async_computation.6 | async-start | bytes 4718592 | tf_op jit(solution)/shard_map/reduce_scatter | solution.py:59
  7.2 12.3 %collective-permute-start.1 = (bf16[2048,512]{1,0:T(8,128)(2,1)}, bf16[2048,512]{1,0:T(8,128)(2,1)}, u32[]{:S(2)}, u32[]{:S(2)}) collective-permute-start(bf16[2048,512]{1,0:T(8,128)(2,1)} %param.7), channel_id=1, source_target_pairs={{0,1},{1,0},{2,3},{3,2},{4,5},{5,4},{6,7},{7,6},{8,9},{9,8},{10,11... | collective-permute-start | bytes 6291464 | tf_op jit(solution)/shard_map/ppermute | solution.py:14
  10.6 8.9 %collective-permute-start = (bf16[1024,512]{1,0:T(8,128)(2,1)S(1)}, bf16[1024,512]{1,0:T(8,128)(2,1)}, u32[]{:S(2)}, u32[]{:S(2)}) collective-permute-start(bf16[1024,512]{1,0:T(8,128)(2,1)S(1)} %constant_dynamic-slice_fusion.3), channel_id=1, source_target_pairs={{0,1},{1,0},{2,3},{3,2},{4,5},{5,4},{6,7},{7,6},{8,9},{9,8},{10,11... | collective-permute-start | bytes 3145736 | tf_op jit(solution)/shard_map/ppermute | solution.py:14
  14.0 11.8 %collective-permute-start.2 = (bf16[256,512]{0,1:T(8,128)(2,1)}, bf16[256,512]{0,1:T(8,128)(2,1)S(1)}, u32[]{:S(2)}, u32[]{:S(2)}) collective-permute-start(bf16[256,512]{0,1:T(8,128)(2,1)} %copy.63), channel_id=1, source_target_pairs={{0,0},{4,12},{8,24},{12,4},{16,16},{20,28},{24,8},{28,20},{32,36},... | collective-permute-start | bytes 786440 | tf_op jit(solution)/shard_map/ppermute | solution.py:47
  25.8 0.7 copy-start.2
  25.8 1.8 copy-start.3
  25.8 0.7 copy-start.4
  26.5 74.1 %dynamic-slice-start = ((f32[2048]{0:T(1024)}, s32[]{:T(128)}), f32[1024]{0:T(1024)S(1)}, s32[]{:S(2)}) async-start(f32[2048]{0:T(1024)} %param.9, s32[]{:T(128)} %select_n.55), calls=%async_computation.7 | async-start | bytes 8704 | tf_op jit(solution)/shard_map/dynamic_slice | solution.py:18
  26.5 23.3 %collective-permute-start.5 = (s32[64,2]{0,1:T(2,128)S(1)}, s32[64,2]{0,1:T(2,128)S(1)}, u32[]{:S(2)}, u32[]{:S(2)}) collective-permute-start(s32[64,2]{0,1:T(2,128)S(1)} %copy-done.2), channel_id=1, source_target_pairs={{0,1},{1,0},{2,3},{3,2},{4,5},{5,4},{6,7},{7,6},{8,9},{9,8},{10,11... | collective-permute-start | bytes 1544 | tf_op jit(solution)/shard_map/ppermute | solution.py:14
  27.6 27.7 %copy-start.1 = (f32[64,2]{1,0:T(8,128)}, f32[64,2]{1,0:T(8,128)S(1)}, u32[]{:S(2)}) copy-start(f32[64,2]{1,0:T(8,128)S(1)} %copy.52) | copy-start | bytes 1540
  29.0 32.7 %all-to-all-start = ((bf16[32,8,256]{2,1,0:T(8,128)(2,1)}), bf16[32,8,256]{2,1,0:T(8,128)(2,1)S(1)}, u32[]{:S(2)}, u32[]{:S(2)}) async-start(bf16[32,8,256]{2,1,0:T(8,128)(2,1)} %fusion.18), calls=%async_computation.1 | async-start | bytes 262144 | tf_op jit(solution)/shard_map/all_to_all | solution.py:102
  44.7 10.3 %collective-permute-start.3 = (bf16[256,512]{0,1:T(8,128)(2,1)}, bf16[256,512]{0,1:T(8,128)(2,1)S(1)}, u32[]{:S(2)}, u32[]{:S(2)}) collective-permute-start(bf16[256,512]{0,1:T(8,128)(2,1)} %copy-done.4), channel_id=1, source_target_pairs={{0,0},{1,2},{2,1},{3,3},{4,100},{5,102},{6,101},{7,103},{8,200},{9... | collective-permute-start | bytes 786440 | tf_op jit(solution)/shard_map/ppermute | solution.py:69
  55.1 6.5 %collective-permute-start.4 = (bf16[128,512]{0,1:T(8,128)(2,1)S(1)}, bf16[128,512]{0,1:T(8,128)(2,1)S(1)}, u32[]{:S(2)}, u32[]{:S(2)}) collective-permute-start(bf16[128,512]{0,1:T(8,128)(2,1)S(1)} %constant_dynamic-slice_fusion.1), channel_id=1, source_target_pairs={{0,2},{2,0},{1,3},{3,1},{4,6},{6,4},{5,7},{7,5},{8,10},{10,8},{9,1... | collective-permute-start | bytes 393224 | tf_op jit(solution)/shard_map/ppermute | solution.py:14
  91.5 9.1 %collective-permute-start.6 = (bf16[128,1024]{0,1:T(8,128)(2,1)S(1)}, bf16[128,1024]{0,1:T(8,128)(2,1)S(1)}, u32[]{:S(2)}, u32[]{:S(2)}) collective-permute-start(bf16[128,1024]{0,1:T(8,128)(2,1)S(1)} %constant_dynamic-slice_fusion), channel_id=1, source_target_pairs={{0,2},{2,0},{1,3},{3,1},{4,6},{6,4},{5,7},{7,5},{8,10},{10,8},{9,1... | collective-permute-start | bytes 786440 | tf_op jit(solution)/shard_map/ppermute | solution.py:14
Sparse Core Ops, SparseCore 0:
  25.9 64.5 reduce-scatter.1

commit v3 on v2

--- a/solution.py
+++ b/solution.py
@@ -1,6 +1,8 @@
 import jax
 import jax.numpy as jnp
 from jax import lax
+from jax.experimental import pallas as pl
+from jax.experimental.pallas import tpu as pltpu
 from jax.sharding import Mesh, PartitionSpec as P
 
 COL = ("z", "xh", "core")
@@ -16,6 +18,69 @@
 
 def piece(values, index, size, axis=0):
     return lax.dynamic_slice_in_dim(values, index * size, size, axis)
+
+
+def block_products(at, here, there, weight_here, weight_there):
+    contract = (((1,), (1,)), ((), ()))
+    own = lax.dot_general(
+        here[...], weight_here[...], contract, preferred_element_type=jnp.float32
+    )
+    other = lax.dot_general(
+        there[...], weight_there[...], contract, preferred_element_type=jnp.float32
+    )
+    return (own + other).astype(jnp.bfloat16)
+
+
+def early_kernel(at, here, there, weight_here, weight_there, out):
+    out[...] = block_products(at, here, there, weight_here, weight_there)
+
+
+def late_kernel(at, here, there, weight_here, weight_there, own, other):
+    values = block_products(at, here, there, weight_here, weight_there)
+    rows = values.shape[0] // 2
+    low, high = values[:rows], values[rows:]
+    first = at[1] == 0
+
+    @pl.when(first)
+    def _():
+        own[0] = low
+        other[0] = high
+
+    @pl.when(jnp.logical_not(first))
+    def _():
+        own[0] = high
+        other[0] = low
+
+
+def cross_products(part, at, features, features_there, cross_weight, weight_there):
+    batch, block = features.shape
+    columns = weight_there.shape[0] // 2
+    tile = batch // Z_N
+    rows = pl.BlockSpec((tile, block), lambda i, at: (i, 0))
+    in_specs = [
+        rows,
+        rows,
+        pl.BlockSpec((columns, block), lambda i, at: (2 * at[0] + part, 0)),
+        pl.BlockSpec((columns, block), lambda i, at: (part, 0)),
+    ]
+    if part == 0:
+        kernel = early_kernel
+        out_specs = pl.BlockSpec((tile, columns), lambda i, at: (i, 0))
+        out_shape = jax.ShapeDtypeStruct((batch, columns), jnp.bfloat16)
+    else:
+        kernel = late_kernel
+        out_specs = [pl.BlockSpec((1, tile // 2, columns), lambda i, at: (i, 0, 0))] * 2
+        out_shape = [jax.ShapeDtypeStruct((Z_N, tile // 2, columns), jnp.bfloat16)] * 2
+    return pl.pallas_call(
+        kernel,
+        grid_spec=pltpu.PrefetchScalarGridSpec(
+            num_scalar_prefetch=1, grid=(Z_N,), in_specs=in_specs, out_specs=out_specs
+        ),
+        out_shape=out_shape,
+        cost_estimate=pl.CostEstimate(
+            flops=4 * batch * columns * block, bytes_accessed=7 << 20, transcendentals=0
+        ),
+    )(at, features, features_there, cross_weight, weight_there)
 
 
 def slot_targets(expert_ids):
@@ -49,14 +114,15 @@
     features_there = swap(features, "core")
     weight_there = swap(piece(cross_weight, 1 - core_at, half), "core")
     contract = (((1,), (1,)), ((), ()))
-    products = lax.dot_general(
-        features, piece(cross_weight, core_at, half), contract, preferred_element_type=jnp.float32
-    )
-    products = products + lax.dot_general(
-        features_there, weight_there, contract, preferred_element_type=jnp.float32
-    )
-    products, plane = lax.optimization_barrier((products.astype(jnp.bfloat16), plane))
-    part = lax.psum_scatter(products, "z", scatter_dimension=0, tiled=True)
+    at = jnp.stack([core_at, xh_at]).astype(jnp.int32)
+    operands = (at, features, features_there, cross_weight, weight_there)
+    part = lax.psum_scatter(
+        cross_products(0, *operands), "z", scatter_dimension=0, tiled=True
+    )
+    late_own, late_other = cross_products(1, *operands)
+    late_sum = (
+        late_own.astype(jnp.float32) + swap(late_other, "xh").astype(jnp.float32)
+    ).astype(jnp.bfloat16)
 
     perm = []
     for r in range(ROWS_N):
@@ -103,11 +169,17 @@
         send_grad.reshape(COL_N, CAP, share), COL, split_axis=0, concat_axis=0, tiled=True
     ).reshape(slots, share)
 
-    part, base, routed_grad, chip_chooser, chooser, table = lax.optimization_barrier(
-        (part, base, routed_grad, chip_chooser, chooser, table)
+    late_sum, plane, routed_grad = lax.optimization_barrier((late_sum, plane, routed_grad))
+    late_parts = lax.all_to_all(late_sum, "z", split_axis=0, concat_axis=0, tiled=True)
+    crossed_late = jnp.sum(late_parts.astype(jnp.float32), axis=0)
+    part, crossed_late, base, chip_chooser, chooser, table = lax.optimization_barrier(
+        (part, crossed_late, base, chip_chooser, chooser, table)
     )
     part_there = swap(piece(part, 1 - xh_at, 2 * rows), "xh")
-    crossed = piece(part, xh_at, 2 * rows).astype(jnp.float32) + part_there.astype(jnp.float32)
+    crossed_early = piece(part, xh_at, 2 * rows).astype(jnp.float32) + part_there.astype(
+        jnp.float32
+    )
+    crossed = jnp.concatenate([crossed_early, crossed_late], axis=1)
     bias = piece(cross_bias, core_at, half)
     hidden = (base * (crossed + bias) + base).astype(jnp.bfloat16)
     send_rows = jnp.dot(chip_chooser, hidden, preferred_element_type=jnp.float32).astype(

time: 240 us -> 252 us (1.050)
  Pallas kernels: 0 us -> 17.7 us
  matrix products: 27.3 us -> 15.3 us
  starting transfers between devices: 29 us -> 35.6 us
  blocking collectives: 113 us -> 108 us
  local copies, waits for them, and re-layouts: 5.69 us -> 8.6 us
    reduce_scatter x1, waiting for transfers between devices: 28.9 us -> 0.02 us  [local(): lax.psum_scatter(cross_products(0, *operands), 'z', scatter_dimension=0,...]
    all_to_all x0 -> x1, waiting for transfers between devices: none -> 22.5 us  [local(): lax.all_to_all(late_sum, 'z', split_axis=0, concat_axis=0, tiled=True)]
    pallas_call x0 -> x2, Pallas kernels: none -> 17.7 us  [cross_products(): pl.pallas_call(kernel, grid_spec=pltpu.PrefetchScalarGridSpec(num_scalar_...]
    all_to_all x0 -> x1, starting transfers between devices: none -> 13 us  [local(): lax.all_to_all(late_sum, 'z', split_axis=0, concat_axis=0, tiled=True)]
    dot_general x2 -> x0, matrix products: 10.2 us -> none  [the longest x1 6.22 us: local(): lax.dot_general(features_there, weight_there, contract, preferred_element...]
    ppermute x5 -> x6, waiting for transfers between devices: 12.3 us -> 17.7 us  [swap(): return lax.ppermute(values, axis, [(0, 1), (1, 0)])]
    all_to_all x1, waiting for transfers between devices: 0.01 us -> 5.4 us  [local(): lax.all_to_all(send_grad.reshape(COL_N, CAP, share), COL, split_axis=0, c...]
    ppermute x1, waiting for transfers between devices: 4.58 us -> 0.01 us  [local(): plane = lax.ppermute(plane, ALL, perm)]
  transfers between devices with their start and end apart: 9 -> 11, of which waited for: 4 -> 6; matrix products, arithmetic and copies ran while one was open for 7% -> 4% of each run, Pallas kernels for 0% -> 4%
where the time goes in v3:
time: 252 us; the launch traced here: 251 us
  blocking collectives  108 us (43%)
  waiting for transfers between devices  45.7 us (18%)
  starting transfers between devices  35.6 us (14%)
  Pallas kernels  17.7 us (7%)
  matrix products  15.3 us (6%)
  between operations  14.4 us (6%)
  local copies, waits for them, and re-layouts  8.6 us (3%)
  other arithmetic  5.61 us (2%)
    all_to_all x1, blocking collectives, local(): lax.all_to_all(answer, COL, split_axis=0, concat_axis=0, tiled=True)  43 us
    all_to_all x1, blocking collectives, local(): lax.all_to_all(send_rows.reshape(COL_N, 2 * CAP, half), COL, split_axis=0...  32.2 us
    all_to_all x1, waiting for transfers between devices, local(): lax.all_to_all(late_sum, 'z', split_axis=0, concat_axis=0, tiled=True)  22.5 us
    ppermute x6, waiting for transfers between devices, swap(): return lax.ppermute(values, axis, [(0, 1), (1, 0)])  17.7 us
    pallas_call x2, Pallas kernels, cross_products(): pl.pallas_call(kernel, grid_spec=pltpu.PrefetchScalarGridSpec(num_scalar_...  17.7 us
    all_to_all x1, blocking collectives, local(): lax.all_to_all(jnp.broadcast_to(slope[None], (ROWS_N, slots, share)), 'ro...  16.8 us
    all_to_all x1, blocking collectives, local(): parts = lax.all_to_all(pre, 'row', split_axis=0, concat_axis=0, tiled=True)  16.1 us
    all_to_all x1, starting transfers between devices, local(): lax.all_to_all(late_sum, 'z', split_axis=0, concat_axis=0, tiled=True)  13 us
  transfers between devices with their start and end apart: 11, of which 6 were waited for; matrix products, arithmetic and copies ran while one was open for 4% of the time, Pallas kernels for 4%

profile of v3, /device:TPU:1, one launch (start us, length us, event | category | flops | bytes accessed | tf_op | source)
XLA Modules:
  0.0 250.9 jit_solution(17087653614730949674)
XLA Ops:
  7.2 3.3 %collective-permute-start = (bf16[2048,512]{1,0:T(8,128)(2,1)}, bf16[2048,512]{1,0:T(8,128)(2,1)S(1)}, u32[]{:S(2)}, u32[]{:S(2)}) collective-permute-start(bf16[2048,512]{1,0:T(8,128)(2,1)} %here.3), channel_id=1, source_target_pairs={{0,1},{1,0},{2,3},{3,2},{4,5},{5,4},{6,7},{7,6},{8,9},{9,8},{10,11... | collective-permute-start | bytes 6291464 | tf_op jit(solution)/shard_map/ppermute | solution.py:16
  10.5 2.3 constant_dynamic-slice_fusion.3
  13.4 2.6 %collective-permute-done.1.weight_there = bf16[1024,512]{1,0:T(8,128)(2,1)S(1)} collective-permute-done((bf16[1024,512]{1,0:T(8,128)(2,1)}, bf16[1024,512]{1,0:T(8,128)(2,1)S(1)}, u32[]{:S(2)}, u32[]{:S(2)}) %collective-permute-start.1) | collective-permute-done | bytes 1048608 | tf_op jit(solution)/shard_map/ppermute | solution.py:16
  17.0 1.3 copy-done
  18.3 8.7 %shard_map.86 = bf16[2048,512]{1,0:T(8,128)(2,1)} custom-call(s32[2]{0:T(128)} %pad_add_fusion.at, bf16[2048,512]{1,0:T(8,128)(2,1)} %here.3, bf16[2048,512]{1,0:T(8,128)(2,1)} %copy-done, bf16[2048,512]{1,0:T(8,128)(2,1)} %weight_here.3, bf16[1024,512]{1,0:T(8,128)(2,1)} %copy-done.2), custom_call_target="tpu_custom_call" | custom-call | flops 2147483648 | bytes 7340032 | tf_op jit(solution)/shard_map/pallas_call | solution.py:74
  27.1 9.0 %shard_map.87 = (bf16[8,128,512]{2,1,0:T(8,128)(2,1)}, bf16[8,128,512]{2,1,0:T(8,128)(2,1)}) custom-call(s32[2]{0:T(128)} %pad_add_fusion.at, bf16[2048,512]{1,0:T(8,128)(2,1)} %here.3, bf16[2048,512]{1,0:T(8,128)(2,1)} %copy-done, bf16[2048,512]{1,0:T(8,128)(2,1)} %weight_here.3, bf16[1024,512]{1,0:T(8,128)(2,1)} %copy-done.2), custom_call_target="tpu_custom_call" | custom-call | flops 2147483648 | bytes 7340032 | tf_op jit(solution)/shard_map/pallas_call | solution.py:74
  36.0 1.1 collective-permute-start.2
  42.0 11.4 %all-to-all-start = ((bf16[32,8,256]{2,1,0:T(8,128)(2,1)}), bf16[32,8,256]{2,1,0:T(8,128)(2,1)S(1)}, u32[]{:S(2)}, u32[]{:S(2)}) async-start(bf16[32,8,256]{2,1,0:T(8,128)(2,1)} %fusion.17), calls=%async_computation.1 | async-start | bytes 262144 | tf_op jit(solution)/shard_map/all_to_all | solution.py:168
  53.7 5.1 %collective-permute-start.4 = (bf16[256,512]{1,0:T(8,128)(2,1)S(1)}, bf16[256,512]{1,0:T(8,128)(2,1)S(1)}, u32[]{:S(2)}, u32[]{:S(2)}) collective-permute-start(bf16[256,512]{1,0:T(8,128)(2,1)S(1)} %collective-permute-done.3), channel_id=1, source_target_pairs={{0,0},{1,2},{2,1},{3,3},{4,100},{5,102},{6,101},{7,103},{8,200},{9... | collective-permute-start | bytes 786440 | tf_op jit(solution)/shard_map/ppermute | solution.py:135
  58.7 4.2 %collective-permute-done.2 = bf16[8,128,512]{2,1,0:T(8,128)(2,1)S(1)} collective-permute-done((bf16[8,128,512]{2,1,0:T(8,128)(2,1)}, bf16[8,128,512]{2,1,0:T(8,128)(2,1)S(1)}, u32[]{:S(2)}, u32[]{:S(2)}) %collective-permute-start.2) | collective-permute-done | bytes 1048608 | tf_op jit(solution)/shard_map/ppermute | solution.py:16
  62.9 1.3 add_convert_fusion
  64.2 5.4 %all-to-all-done = bf16[32,8,256]{2,1,0:T(8,128)(2,1)S(1)} async-done(((bf16[32,8,256]{2,1,0:T(8,128)(2,1)}), bf16[32,8,256]{2,1,0:T(8,128)(2,1)S(1)}, u32[]{:S(2)}, u32[]{:S(2)}) %all-to-all-start) | async-done | bytes 131104 | tf_op jit(solution)/shard_map/all_to_all | solution.py:168
  69.6 13.0 %all-to-all-start.1 = ((bf16[8,128,512]{2,1,0:T(8,128)(2,1)}), bf16[8,128,512]{2,1,0:T(8,128)(2,1)S(1)}, u32[]{:S(2)}, u32[]{:S(2)}) async-start(bf16[8,128,512]{2,1,0:T(8,128)(2,1)} %add_convert_fusion), calls=%async_computation.2 | async-start | bytes 2097152 | tf_op jit(solution)/shard_map/all_to_all | solution.py:173
  84.1 5.0 %collective-permute-done.5 = bf16[128,512]{1,0:T(8,128)(2,1)S(1)} collective-permute-done((bf16[128,512]{1,0:T(8,128)(2,1)S(1)}, bf16[128,512]{1,0:T(8,128)(2,1)S(1)}, u32[]{:S(2)}, u32[]{:S(2)}) %collective-permute-start.5) | collective-permute-done | bytes 131104 | tf_op jit(solution)/shard_map/ppermute | solution.py:16
  89.2 22.5 %all-to-all-done.1 = bf16[8,128,512]{2,1,0:T(8,128)(2,1)S(1)} async-done(((bf16[8,128,512]{2,1,0:T(8,128)(2,1)}), bf16[8,128,512]{2,1,0:T(8,128)(2,1)S(1)}, u32[]{:S(2)}, u32[]{:S(2)}) %all-to-all-start.1) | async-done | bytes 1048608 | tf_op jit(solution)/shard_map/all_to_all | solution.py:173
  113.0 6.0 %collective-permute-done.7 = bf16[128,512]{1,0:T(8,128)(2,1)S(1)} collective-permute-done((bf16[128,512]{1,0:T(8,128)(2,1)S(1)}, bf16[128,512]{1,0:T(8,128)(2,1)S(1)}, u32[]{:S(2)}, u32[]{:S(2)}) %collective-permute-start.7) | collective-permute-done | bytes 131104 | tf_op jit(solution)/shard_map/ppermute | solution.py:16
  120.4 32.2 %all_to_all.30 = bf16[32,16,1024]{2,1,0:T(8,128)(2,1)S(1)} all-to-all(bf16[32,16,1024]{2,1,0:T(8,128)(2,1)S(1)} %bitcast.49), channel_id=1, replica_groups=mesh['row'=8,'z'=8,'xh'=2,'core'=2] {'z','xh','core'}, dimensions={0} | all-to-all | bytes 2097152 | tf_op jit(solution)/shard_map/all_to_all | solution.py:188
  152.7 3.4 %fusion.2 = f32[256,2048]{1,0:T(8,128)S(1)} fusion(bf16[256,1024]{1,0:T(8,128)(2,1)S(1)} %bitcast.56, bf16[1,2048,2048]{2,1,0:T(8,128)(2,1)} %param.12), kind=kOutput, calls=%fused_computation.2 | convolution fusion | flops 1073741824 | bytes 6815744 | tf_op jit(solution)/shard_map/dot_general | solution.py:195
  156.1 3.5 %fusion.11 = bf16[256,2048]{1,0:T(8,128)(2,1)S(1)} fusion(f32[256,2048]{1,0:T(8,128)S(1)} %fusion.2, bf16[256,1024]{1,0:T(8,128)(2,1)S(1)} %bitcast.55, bf16[1,2048,2048]{2,1,0:T(8,128)(2,1)} %param.12), kind=kOutput, calls=%fused_computation.9 | convolution fusion | flops 1074790400 | bytes 7864320 | tf_op jit(solution)/shard_map/dot_general | solution.py:193
  159.7 16.1 %all_to_all.31 = bf16[8,256,256]{2,1,0:T(8,128)(2,1)S(1)} all-to-all(bf16[8,256,256]{2,1,0:T(8,128)(2,1)S(1)} %bitcast.51), channel_id=1, replica_groups=mesh['row'=8,'z'=8,'xh'=2,'core'=2] {'row'}, dimensions={0} | all-to-all | bytes 2097152 | tf_op jit(solution)/shard_map/all_to_all | solution.py:199
  176.3 16.8 %all_to_all.32 = bf16[8,256,256]{1,2,0:T(8,128)(2,1)S(1)} all-to-all(bf16[8,256,256]{1,2,0:T(8,128)(2,1)S(1)} %broadcast_in_dim.2), channel_id=1, replica_groups=mesh['row'=8,'z'=8,'xh'=2,'core'=2] {'row'}, dimensions={0} | all-to-all | bytes 2097152 | tf_op jit(solution)/shard_map/all_to_all | solution.py:206
  193.1 5.8 %fusion.14 = bf16[256,2048]{1,0:T(8,128)(2,1)S(1)} fusion(bf16[256,2048]{0,1:T(8,128)(2,1)S(1)} %bitcast.53, bf16[1,2048,2048]{2,1,0:T(8,128)(2,1)} %param.12), kind=kOutput, calls=%fused_computation.10 | convolution fusion | flops 2148007936 | bytes 10485760 | tf_op jit(solution)/shard_map/dot_general | solution.py:214
  199.0 43.0 %all_to_all.33 = bf16[32,8,2304]{2,1,0:T(8,128)(2,1)S(1)} all-to-all(bf16[32,8,2304]{2,1,0:T(8,128)(2,1)S(1)} %maximum_bitcast_fusion), channel_id=1, replica_groups=mesh['row'=8,'z'=8,'xh'=2,'core'=2] {'z','xh','core'}, dimensions={0} | all-to-all | bytes 2359296 | tf_op jit(solution)/shard_map/all_to_all | solution.py:219
  243.0 1.0 convolution_convert_fusion
  (72 shorter events, 12.6 us)
Async XLA Ops:
  7.2 104.8 %reduce-scatter.2.cloned.1.call-start = ((), (), s32[]{:S(2)}) async-start(), calls=%async_computation.7 | async-start | bytes 2359296 | tf_op jit(solution)/shard_map/reduce_scatter | solution.py:119
  7.2 8.8 %collective-permute-start = (bf16[2048,512]{1,0:T(8,128)(2,1)}, bf16[2048,512]{1,0:T(8,128)(2,1)S(1)}, u32[]{:S(2)}, u32[]{:S(2)}) collective-permute-start(bf16[2048,512]{1,0:T(8,128)(2,1)} %here.3), channel_id=1, source_target_pairs={{0,1},{1,0},{2,3},{3,2},{4,5},{5,4},{6,7},{7,6},{8,9},{9,8},{10,11... | collective-permute-start | bytes 6291464 | tf_op jit(solution)/shard_map/ppermute | solution.py:16
  12.8 3.2 %collective-permute-start.1 = (bf16[1024,512]{1,0:T(8,128)(2,1)}, bf16[1024,512]{1,0:T(8,128)(2,1)S(1)}, u32[]{:S(2)}, u32[]{:S(2)}) collective-permute-start(bf16[1024,512]{1,0:T(8,128)(2,1)} %constant_dynamic-slice_fusion.3), channel_id=1, source_target_pairs={{0,1},{1,0},{2,3},{3,2},{4,5},{5,4},{6,7},{7,6},{8,9},{9,8},{10,11... | collective-permute-start | bytes 3145736 | tf_op jit(solution)/shard_map/ppermute | solution.py:16
  16.0 1.0 copy-start.2
  17.0 1.3 copy-start
  27.1 11.7 %copy-start.3 = (s32[64,2]{0,1:T(2,128)S(1)}, s32[64,2]{0,1:T(2,128)}, u32[]{:S(2)}) copy-start(s32[64,2]{0,1:T(2,128)} %param.10) | copy-start | bytes 1540
  27.1 13.4 %copy-start.5 = (f32[64,2]{0,1:T(2,128)S(1)}, f32[64,2]{0,1:T(2,128)}, u32[]{:S(2)}) copy-start(f32[64,2]{0,1:T(2,128)} %param.11) | copy-start | bytes 1540
  36.0 26.8 %copy-start.1 = (bf16[8,128,512]{2,1,0:T(8,128)(2,1)S(1)}, bf16[8,128,512]{2,1,0:T(8,128)(2,1)}, u32[]{:S(2)}) copy-start(bf16[8,128,512]{2,1,0:T(8,128)(2,1)} %get-tuple-element.12) | copy-start | bytes 3145732
  36.0 26.8 %collective-permute-start.2 = (bf16[8,128,512]{2,1,0:T(8,128)(2,1)}, bf16[8,128,512]{2,1,0:T(8,128)(2,1)S(1)}, u32[]{:S(2)}, u32[]{:S(2)}) collective-permute-start(bf16[8,128,512]{2,1,0:T(8,128)(2,1)} %get-tuple-element.13), channel_id=1, source_target_pairs={{0,2},{2,0},{1,3},{3,1},{4,6},{6,4},{5,7},{7,5},{8,10},{10,8},{9,1... | collective-permute-start | bytes 3145736 | tf_op jit(solution)/shard_map/ppermute | solution.py:16
  38.1 15.6 %collective-permute-start.3 = (bf16[256,512]{1,0:T(8,128)(2,1)S(1)}, bf16[256,512]{1,0:T(8,128)(2,1)S(1)}, u32[]{:S(2)}, u32[]{:S(2)}) collective-permute-start(bf16[256,512]{1,0:T(8,128)(2,1)S(1)} %constant_dynamic-slice_fusion.2), channel_id=1, source_target_pairs={{0,0},{4,12},{8,24},{12,4},{16,16},{20,28},{24,8},{28,20},{32,36},... | collective-permute-start | bytes 786440 | tf_op jit(solution)/shard_map/ppermute | solution.py:112
  38.8 44.2 %collective-permute-start.6 = (s32[64,2]{0,1:T(2,128)S(1)}, s32[64,2]{0,1:T(2,128)S(1)}, u32[]{:S(2)}, u32[]{:S(2)}) collective-permute-start(s32[64,2]{0,1:T(2,128)S(1)} %copy-done.3), channel_id=1, source_target_pairs={{0,1},{1,0},{2,3},{3,2},{4,5},{5,4},{6,7},{7,6},{8,9},{9,8},{10,11... | collective-permute-start | bytes 1544 | tf_op jit(solution)/shard_map/ppermute | solution.py:16
  42.0 27.6 %all-to-all-start = ((bf16[32,8,256]{2,1,0:T(8,128)(2,1)}), bf16[32,8,256]{2,1,0:T(8,128)(2,1)S(1)}, u32[]{:S(2)}, u32[]{:S(2)}) async-start(bf16[32,8,256]{2,1,0:T(8,128)(2,1)} %fusion.17), calls=%async_computation.1 | async-start | bytes 262144 | tf_op jit(solution)/shard_map/all_to_all | solution.py:168
  53.7 15.9 %collective-permute-start.4 = (bf16[256,512]{1,0:T(8,128)(2,1)S(1)}, bf16[256,512]{1,0:T(8,128)(2,1)S(1)}, u32[]{:S(2)}, u32[]{:S(2)}) collective-permute-start(bf16[256,512]{1,0:T(8,128)(2,1)S(1)} %collective-permute-done.3), channel_id=1, source_target_pairs={{0,0},{1,2},{2,1},{3,3},{4,100},{5,102},{6,101},{7,103},{8,200},{9... | collective-permute-start | bytes 786440 | tf_op jit(solution)/shard_map/ppermute | solution.py:135
  69.6 42.2 %all-to-all-start.1 = ((bf16[8,128,512]{2,1,0:T(8,128)(2,1)}), bf16[8,128,512]{2,1,0:T(8,128)(2,1)S(1)}, u32[]{:S(2)}, u32[]{:S(2)}) async-start(bf16[8,128,512]{2,1,0:T(8,128)(2,1)} %add_convert_fusion), calls=%async_computation.2 | async-start | bytes 2097152 | tf_op jit(solution)/shard_map/all_to_all | solution.py:173
  82.6 30.4 %copy-start.4 = (f32[2048]{0:T(1024)S(1)}, f32[2048]{0:T(1024)}, u32[]{:S(2)}) copy-start(f32[2048]{0:T(1024)} %param.9) | copy-start | bytes 24580
  83.7 5.4 %collective-permute-start.5 = (bf16[128,512]{1,0:T(8,128)(2,1)S(1)}, bf16[128,512]{1,0:T(8,128)(2,1)S(1)}, u32[]{:S(2)}, u32[]{:S(2)}) collective-permute-start(bf16[128,512]{1,0:T(8,128)(2,1)S(1)} %constant_dynamic-slice_fusion.1), channel_id=1, source_target_pairs={{0,2},{2,0},{1,3},{3,1},{4,6},{6,4},{5,7},{7,5},{8,10},{10,8},{9,1... | collective-permute-start | bytes 393224 | tf_op jit(solution)/shard_map/ppermute | solution.py:16
  112.9 6.1 %collective-permute-start.7 = (bf16[128,512]{1,0:T(8,128)(2,1)S(1)}, bf16[128,512]{1,0:T(8,128)(2,1)S(1)}, u32[]{:S(2)}, u32[]{:S(2)}) collective-permute-start(bf16[128,512]{1,0:T(8,128)(2,1)S(1)} %constant_dynamic-slice_fusion), channel_id=1, source_target_pairs={{0,2},{2,0},{1,3},{3,1},{4,6},{6,4},{5,7},{7,5},{8,10},{10,8},{9,1... | collective-permute-start | bytes 393224 | tf_op jit(solution)/shard_map/ppermute | solution.py:16
Sparse Core Ops, SparseCore 0:
  27.2 51.5 reduce-scatter.1

commit v4 on v3

--- a/solution.py
+++ b/solution.py
@@ -20,42 +20,41 @@
     return lax.dynamic_slice_in_dim(values, index * size, size, axis)
 
 
-def block_products(at, here, there, weight_here, weight_there):
-    contract = (((1,), (1,)), ((), ()))
-    own = lax.dot_general(
-        here[...], weight_here[...], contract, preferred_element_type=jnp.float32
-    )
-    other = lax.dot_general(
-        there[...], weight_there[...], contract, preferred_element_type=jnp.float32
-    )
-    return (own + other).astype(jnp.bfloat16)
+GRANT = 57 << 20
+NT = (((1,), (1,)), ((), ()))
+
+
+def dot_nt(left, right):
+    return lax.dot_general(left, right, NT, preferred_element_type=jnp.float32)
 
 
 def early_kernel(at, here, there, weight_here, weight_there, out):
-    out[...] = block_products(at, here, there, weight_here, weight_there)
+    values = dot_nt(here[...], weight_here[...]) + dot_nt(there[...], weight_there[...])
+    out[...] = values.astype(jnp.bfloat16)
 
 
 def late_kernel(at, here, there, weight_here, weight_there, own, other):
-    values = block_products(at, here, there, weight_here, weight_there)
-    rows = values.shape[0] // 2
-    low, high = values[:rows], values[rows:]
+    values = dot_nt(here[...], weight_here[...]) + dot_nt(there[...], weight_there[...])
+    planes, rows, columns = own.shape
+    values = values.astype(jnp.bfloat16).reshape(planes, 2, rows, columns)
     first = at[1] == 0
 
     @pl.when(first)
     def _():
-        own[0] = low
-        other[0] = high
+        own[...] = values[:, 0]
+        other[...] = values[:, 1]
 
     @pl.when(jnp.logical_not(first))
     def _():
-        own[0] = high
-        other[0] = low
+        own[...] = values[:, 1]
+        other[...] = values[:, 0]
 
 
 def cross_products(part, at, features, features_there, cross_weight, weight_there):
     batch, block = features.shape
     columns = weight_there.shape[0] // 2
-    tile = batch // Z_N
+    steps = 2
+    tile = batch // steps
     rows = pl.BlockSpec((tile, block), lambda i, at: (i, 0))
     in_specs = [
         rows,
@@ -69,18 +68,88 @@
         out_shape = jax.ShapeDtypeStruct((batch, columns), jnp.bfloat16)
     else:
         kernel = late_kernel
-        out_specs = [pl.BlockSpec((1, tile // 2, columns), lambda i, at: (i, 0, 0))] * 2
-        out_shape = [jax.ShapeDtypeStruct((Z_N, tile // 2, columns), jnp.bfloat16)] * 2
+        planes, half_plane = Z_N // steps, batch // Z_N // 2
+        out_specs = [pl.BlockSpec((planes, half_plane, columns), lambda i, at: (i, 0, 0))] * 2
+        out_shape = [jax.ShapeDtypeStruct((Z_N, half_plane, columns), jnp.bfloat16)] * 2
     return pl.pallas_call(
         kernel,
         grid_spec=pltpu.PrefetchScalarGridSpec(
-            num_scalar_prefetch=1, grid=(Z_N,), in_specs=in_specs, out_specs=out_specs
+            num_scalar_prefetch=1, grid=(steps,), in_specs=in_specs, out_specs=out_specs
         ),
         out_shape=out_shape,
+        compiler_params=pltpu.CompilerParams(vmem_limit_bytes=GRANT),
         cost_estimate=pl.CostEstimate(
             flops=4 * batch * columns * block, bytes_accessed=7 << 20, transcendentals=0
         ),
     )(at, features, features_there, cross_weight, weight_there)
+
+
+def forward_kernel(routed, weight, out):
+    shares, slots, share = out.shape
+    half = routed.shape[3]
+    low = routed[:, 0].reshape(slots, half)
+    high = routed[:, 1].reshape(slots, half)
+    values = jnp.dot(low, weight[:half], preferred_element_type=jnp.float32)
+    values += jnp.dot(high, weight[half:], preferred_element_type=jnp.float32)
+    values = values.astype(jnp.bfloat16)
+    for index in range(shares):
+        out[index] = values[:, index * share : (index + 1) * share]
+
+
+def expert_forward(routed, weight):
+    width, out_width = weight.shape
+    share = out_width // ROWS_N
+    slots = COL_N * CAP
+    shares = 2
+    return pl.pallas_call(
+        forward_kernel,
+        grid=(ROWS_N // shares,),
+        in_specs=[
+            pl.BlockSpec(routed.shape, lambda i: (0, 0, 0, 0)),
+            pl.BlockSpec((width, shares * share), lambda i: (0, i)),
+        ],
+        out_specs=pl.BlockSpec((shares, slots, share), lambda i: (i, 0, 0)),
+        out_shape=jax.ShapeDtypeStruct((ROWS_N, slots, share), jnp.bfloat16),
+        compiler_params=pltpu.CompilerParams(vmem_limit_bytes=GRANT),
+        cost_estimate=pl.CostEstimate(
+            flops=2 * slots * weight.size, bytes_accessed=10 << 20, transcendentals=0
+        ),
+    )(routed, weight)
+
+
+def back_kernel(slopes, activated, weight, out):
+    shares, slots, share = slopes.shape
+    tile = weight.shape[0]
+    step = pl.program_id(0)
+    values = jnp.zeros((slots, tile), jnp.float32)
+    for index in range(shares):
+        values += dot_nt(slopes[index], weight[:, index * share : (index + 1) * share])
+    out[:, pl.ds(pl.multiple_of(step * tile, tile), tile)] = values.astype(jnp.bfloat16)
+
+    @pl.when(step == 0)
+    def _():
+        out[:, out.shape[1] - share :] = activated[...]
+
+
+def expert_back(slopes, activated, weight):
+    width, out_width = weight.shape
+    slots, share = activated.shape
+    steps = 4
+    return pl.pallas_call(
+        back_kernel,
+        grid=(steps,),
+        in_specs=[
+            pl.BlockSpec(slopes.shape, lambda i: (0, 0, 0)),
+            pl.BlockSpec(activated.shape, lambda i: (0, 0)),
+            pl.BlockSpec((width // steps, out_width), lambda i: (i, 0)),
+        ],
+        out_specs=pl.BlockSpec((slots, width + share), lambda i: (0, 0)),
+        out_shape=jax.ShapeDtypeStruct((slots, width + share), jnp.bfloat16),
+        compiler_params=pltpu.CompilerParams(vmem_limit_bytes=GRANT),
+        cost_estimate=pl.CostEstimate(
+            flops=2 * slots * weight.size, bytes_accessed=10 << 20, transcendentals=0
+        ),
+    )(slopes, activated, weight)
 
 
 def slot_targets(expert_ids):
@@ -113,13 +182,12 @@
 
     features_there = swap(features, "core")
     weight_there = swap(piece(cross_weight, 1 - core_at, half), "core")
-    contract = (((1,), (1,)), ((), ()))
     at = jnp.stack([core_at, xh_at]).astype(jnp.int32)
-    operands = (at, features, features_there, cross_weight, weight_there)
+    operands = (features, features_there, cross_weight, weight_there)
     part = lax.psum_scatter(
-        cross_products(0, *operands), "z", scatter_dimension=0, tiled=True
-    )
-    late_own, late_other = cross_products(1, *operands)
+        cross_products(0, at, *operands), "z", scatter_dimension=0, tiled=True
+    )
+    late_own, late_other = cross_products(1, at, *operands)
     late_sum = (
         late_own.astype(jnp.float32) + swap(late_other, "xh").astype(jnp.float32)
     ).astype(jnp.bfloat16)
@@ -169,13 +237,13 @@
         send_grad.reshape(COL_N, CAP, share), COL, split_axis=0, concat_axis=0, tiled=True
     ).reshape(slots, share)
 
-    late_sum, plane, routed_grad = lax.optimization_barrier((late_sum, plane, routed_grad))
+    late_sum, routed_grad = lax.optimization_barrier((late_sum, routed_grad))
     late_parts = lax.all_to_all(late_sum, "z", split_axis=0, concat_axis=0, tiled=True)
+    part_there = swap(piece(part, 1 - xh_at, 2 * rows), "xh")
+    late_parts, part_there, base, chip_chooser, chooser, table = lax.optimization_barrier(
+        (late_parts, part_there, base, chip_chooser, chooser, table)
+    )
     crossed_late = jnp.sum(late_parts.astype(jnp.float32), axis=0)
-    part, crossed_late, base, chip_chooser, chooser, table = lax.optimization_barrier(
-        (part, crossed_late, base, chip_chooser, chooser, table)
-    )
-    part_there = swap(piece(part, 1 - xh_at, 2 * rows), "xh")
     crossed_early = piece(part, xh_at, 2 * rows).astype(jnp.float32) + part_there.astype(
         jnp.float32
     )
@@ -190,12 +258,7 @@
     ).reshape(COL_N // 2, 2, 2 * CAP, half)
 
     weight = expert_weight[0]
-    pre = jnp.dot(
-        routed[:, 0].reshape(slots, half), weight[:half], preferred_element_type=jnp.float32
-    ) + jnp.dot(
-        routed[:, 1].reshape(slots, half), weight[half:], preferred_element_type=jnp.float32
-    )
-    pre = pre.astype(jnp.bfloat16).reshape(slots, ROWS_N, share).transpose(1, 0, 2)
+    pre = expert_forward(routed, weight)
     parts = lax.all_to_all(pre, "row", split_axis=0, concat_axis=0, tiled=True)
     preact = jnp.sum(parts.astype(jnp.float32), axis=0)
     sigma = jax.nn.sigmoid(preact)
@@ -210,15 +273,11 @@
         concat_axis=0,
         tiled=True,
     )
-    slope_grad = slopes.transpose(1, 0, 2).reshape(slots, out_width)
-    back = lax.dot_general(
-        slope_grad, weight, contract, preferred_element_type=jnp.float32
-    ).astype(jnp.bfloat16)
-
-    answer = jnp.concatenate([back, activated], axis=1).reshape(COL_N, CAP, width + share)
-    returned = lax.all_to_all(answer, COL, split_axis=0, concat_axis=0, tiled=True).reshape(
-        slots, width + share
-    )
+    answer = expert_back(slopes, activated, weight)
+
+    returned = lax.all_to_all(
+        answer.reshape(COL_N, CAP, width + share), COL, split_axis=0, concat_axis=0, tiled=True
+    ).reshape(slots, width + share)
     pull = (((0,), (0,)), ((), ()))
     pair_act = lax.dot_general(
         table, returned[:, width:], pull, preferred_element_type=jnp.float32

time: 252 us -> 237 us (0.940)
  waiting for transfers between devices: 45.7 us -> 32.3 us
  matrix products: 15.3 us -> 2.54 us
  blocking collectives: 108 us -> 118 us
  Pallas kernels: 17.7 us -> 26 us
  starting transfers between devices: 35.6 us -> 29.6 us
    all_to_all x1, waiting for transfers between devices: 22.5 us -> 7.58 us  [local(): lax.all_to_all(late_sum, 'z', split_axis=0, concat_axis=0, tiled=True)]
    pallas_call x0 -> x2, Pallas kernels: none -> 13.5 us  [the longest x1 6.89 us: expert_back(): pl.pallas_call(back_kernel, grid=(steps,), in_specs=[pl.BlockSpec(slopes....]
    dot_general x3 -> x0, matrix products: 12.7 us -> none  [the longest x1 5.77 us: local(): lax.dot_general(slope_grad, weight, contract, preferred_element_type=jnp....]
    all_to_all x1, blocking collectives: 32.2 us -> 39.1 us  [local(): lax.all_to_all(send_rows.reshape(COL_N, 2 * CAP, half), COL, split_axis=0...]
    all_to_all x1, starting transfers between devices: 13 us -> 6.44 us  [local(): lax.all_to_all(late_sum, 'z', split_axis=0, concat_axis=0, tiled=True)]
    reduce_scatter x1, waiting for transfers between devices: 0.02 us -> 6.18 us  [local(): lax.psum_scatter(cross_products(0, at, *operands), 'z', scatter_dimension...]
    all_to_all x1, waiting for transfers between devices: 5.4 us -> 0.01 us  [local(): lax.all_to_all(send_grad.reshape(COL_N, CAP, share), COL, split_axis=0, c...]
    pallas_call x2, Pallas kernels: 17.7 us -> 12.6 us  [cross_products(): pl.pallas_call(kernel, grid_spec=pltpu.PrefetchScalarGridSpec(num_scalar_...]
  transfers between devices with their start and end apart: 11 -> 11, of which waited for: 6 -> 5; matrix products, arithmetic and copies ran while one was open for 4% -> 4% of each run, Pallas kernels for 4% -> 3%
where the time goes in v4:
time: 237 us; the launch traced here: 236 us
  blocking collectives  118 us (50%)
  waiting for transfers between devices  32.3 us (14%)
  starting transfers between devices  29.6 us (12%)
  Pallas kernels  26 us (11%)
  between operations  14.3 us (6%)
  local copies, waits for them, and re-layouts  8.42 us (4%)
  other arithmetic  5.27 us (2%)
  matrix products  2.54 us (1%)
    all_to_all x1, blocking collectives, local(): lax.all_to_all(answer.reshape(COL_N, CAP, width + share), COL, split_axis...  43.7 us
    all_to_all x1, blocking collectives, local(): lax.all_to_all(send_rows.reshape(COL_N, 2 * CAP, half), COL, split_axis=0...  39.1 us
    all_to_all x1, blocking collectives, local(): parts = lax.all_to_all(pre, 'row', split_axis=0, concat_axis=0, tiled=True)  18.9 us
    all_to_all x1, blocking collectives, local(): lax.all_to_all(jnp.broadcast_to(slope[None], (ROWS_N, slots, share)), 'ro...  15.9 us
    ppermute x6, waiting for transfers between devices, swap(): return lax.ppermute(values, axis, [(0, 1), (1, 0)])  14.9 us
    pallas_call x2, Pallas kernels, cross_products(): pl.pallas_call(kernel, grid_spec=pltpu.PrefetchScalarGridSpec(num_scalar_...  12.6 us
    all_to_all x1, starting transfers between devices, local(): lax.all_to_all(send_grad.reshape(COL_N, CAP, share), COL, split_axis=0, c...  8.74 us
    ppermute x6, starting transfers between devices, swap(): return lax.ppermute(values, axis, [(0, 1), (1, 0)])  7.6 us
  transfers between devices with their start and end apart: 11, of which 5 were waited for; matrix products, arithmetic and copies ran while one was open for 4% of the time, Pallas kernels for 3%

profile of v4, /device:TPU:1, one launch (start us, length us, event | category | flops | bytes accessed | tf_op | source)
XLA Modules:
  0.0 236.1 jit_solution(3607001399681649031)
XLA Ops:
  7.2 3.3 %collective-permute-start = (bf16[2048,512]{1,0:T(8,128)(2,1)}, bf16[2048,512]{1,0:T(8,128)(2,1)S(1)}, u32[]{:S(2)}, u32[]{:S(2)}) collective-permute-start(bf16[2048,512]{1,0:T(8,128)(2,1)} %here.3), channel_id=1, source_target_pairs={{0,1},{1,0},{2,3},{3,2},{4,5},{5,4},{6,7},{7,6},{8,9},{9,8},{10,11... | collective-permute-start | bytes 6291464 | tf_op jit(solution)/shard_map/ppermute | solution.py:16
  10.5 2.3 constant_dynamic-slice_fusion.3
  13.4 2.6 %collective-permute-done.1.weight_there = bf16[1024,512]{1,0:T(8,128)(2,1)S(1)} collective-permute-done((bf16[1024,512]{1,0:T(8,128)(2,1)}, bf16[1024,512]{1,0:T(8,128)(2,1)S(1)}, u32[]{:S(2)}, u32[]{:S(2)}) %collective-permute-start.1) | collective-permute-done | bytes 1048608 | tf_op jit(solution)/shard_map/ppermute | solution.py:16
  17.0 1.3 copy-done
  18.3 6.1 %shard_map.87 = bf16[2048,512]{1,0:T(8,128)(2,1)} custom-call(s32[2]{0:T(128)} %pad_add_fusion.at, bf16[2048,512]{1,0:T(8,128)(2,1)} %here.3, bf16[2048,512]{1,0:T(8,128)(2,1)} %copy-done, bf16[2048,512]{1,0:T(8,128)(2,1)} %weight_here.3, bf16[1024,512]{1,0:T(8,128)(2,1)} %copy-done.2), custom_call_target="tpu_custom_call" | custom-call | flops 2147483648 | bytes 7340032 | tf_op jit(solution)/shard_map/pallas_call | solution.py:74
  24.5 6.5 %shard_map.86 = (bf16[8,128,512]{2,1,0:T(8,128)(2,1)}, bf16[8,128,512]{2,1,0:T(8,128)(2,1)}) custom-call(s32[2]{0:T(128)} %pad_add_fusion.at, bf16[2048,512]{1,0:T(8,128)(2,1)} %here.3, bf16[2048,512]{1,0:T(8,128)(2,1)} %copy-done, bf16[2048,512]{1,0:T(8,128)(2,1)} %weight_here.3, bf16[1024,512]{1,0:T(8,128)(2,1)} %copy-done.2), custom_call_target="tpu_custom_call" | custom-call | flops 2147483648 | bytes 7340032 | tf_op jit(solution)/shard_map/pallas_call | solution.py:74
  30.9 1.0 collective-permute-start.2
  35.1 8.7 %all-to-all-start = ((bf16[32,8,256]{2,1,0:T(8,128)(2,1)}), bf16[32,8,256]{2,1,0:T(8,128)(2,1)S(1)}, u32[]{:S(2)}, u32[]{:S(2)}) async-start(bf16[32,8,256]{2,1,0:T(8,128)(2,1)} %fusion), calls=%async_computation | async-start | bytes 262144 | tf_op jit(solution)/shard_map/all_to_all | solution.py:236
  46.0 12.3 %collective-permute-done.2 = bf16[8,128,512]{2,1,0:T(8,128)(2,1)S(1)} collective-permute-done((bf16[8,128,512]{2,1,0:T(8,128)(2,1)}, bf16[8,128,512]{2,1,0:T(8,128)(2,1)S(1)}, u32[]{:S(2)}, u32[]{:S(2)}) %collective-permute-start.2) | collective-permute-done | bytes 1048608 | tf_op jit(solution)/shard_map/ppermute | solution.py:16
  58.3 1.3 add_convert_fusion
  59.6 6.4 %all-to-all-start.1 = ((bf16[8,128,512]{2,1,0:T(8,128)(2,1)}), bf16[8,128,512]{2,1,0:T(8,128)(2,1)S(1)}, u32[]{:S(2)}, u32[]{:S(2)}) async-start(bf16[8,128,512]{2,1,0:T(8,128)(2,1)} %add_convert_fusion), calls=%async_computation.1 | async-start | bytes 2097152 | tf_op jit(solution)/shard_map/all_to_all | solution.py:241
  66.4 6.1 %collective-permute-start.5 = (bf16[256,512]{1,0:T(8,128)(2,1)S(1)}, bf16[256,512]{1,0:T(8,128)(2,1)S(1)}, u32[]{:S(2)}, u32[]{:S(2)}) collective-permute-start(bf16[256,512]{1,0:T(8,128)(2,1)S(1)} %collective-permute-done.4), channel_id=1, source_target_pairs={{0,0},{1,2},{2,1},{3,3},{4,100},{5,102},{6,101},{7,103},{8,200},{9... | collective-permute-start | bytes 786440 | tf_op jit(solution)/shard_map/ppermute | solution.py:203
  73.2 3.7 %collective-permute-done.5 = bf16[256,512]{1,0:T(8,128)(2,1)S(1)} collective-permute-done((bf16[256,512]{1,0:T(8,128)(2,1)S(1)}, bf16[256,512]{1,0:T(8,128)(2,1)S(1)}, u32[]{:S(2)}, u32[]{:S(2)}) %collective-permute-start.5) | collective-permute-done | bytes 262176 | tf_op jit(solution)/shard_map/ppermute | solution.py:203
  77.1 6.2 %reduce-scatter.2.cloned.1.call-done = bf16[256,512]{1,0:T(8,128)(2,1)} async-done(((bf16[2048,512]{1,0:T(8,128)(2,1)}), bf16[256,512]{1,0:T(8,128)(2,1)}) %reduce-scatter.2.cloned.1.call-update) | async-done | bytes 262160 | tf_op jit(solution)/shard_map/reduce_scatter | solution.py:187
  83.3 1.0 constant_dynamic-slice_fusion.2
  84.2 2.5 %collective-permute-start.3 = (bf16[128,512]{1,0:T(8,128)(2,1)S(1)}, bf16[128,512]{1,0:T(8,128)(2,1)S(1)}, u32[]{:S(2)}, u32[]{:S(2)}) collective-permute-start(bf16[128,512]{1,0:T(8,128)(2,1)S(1)} %constant_dynamic-slice_fusion.2), channel_id=1, source_target_pairs={{0,2},{2,0},{1,3},{3,1},{4,6},{6,4},{5,7},{7,5},{8,10},{10,8},{9,1... | collective-permute-start | bytes 393224 | tf_op jit(solution)/shard_map/ppermute | solution.py:16
  86.9 7.6 %all-to-all-done.1 = bf16[8,128,512]{2,1,0:T(8,128)(2,1)S(1)} async-done(((bf16[8,128,512]{2,1,0:T(8,128)(2,1)}), bf16[8,128,512]{2,1,0:T(8,128)(2,1)S(1)}, u32[]{:S(2)}, u32[]{:S(2)}) %all-to-all-start.1) | async-done | bytes 1048608 | tf_op jit(solution)/shard_map/all_to_all | solution.py:241
  95.1 39.1 %all_to_all.30 = bf16[32,16,1024]{2,1,0:T(8,128)(2,1)} all-to-all(bf16[32,16,1024]{2,1,0:T(8,128)(2,1)S(1)} %bitcast.23), channel_id=1, replica_groups=mesh['row'=8,'z'=8,'xh'=2,'core'=2] {'z','xh','core'}, dimensions={0} | all-to-all | bytes 2097152 | tf_op jit(solution)/shard_map/all_to_all | solution.py:256
  134.2 6.6 %shard_map.88 = bf16[8,256,256]{2,1,0:T(8,128)(2,1)} custom-call(bf16[16,2,16,1024]{3,2,1,0:T(8,128)(2,1)} %bitcast.22, bf16[2048,2048]{1,0:T(8,128)(2,1)} %bitcast.17), custom_call_target="tpu_custom_call" | custom-call | flops 2147483648 | bytes 10485760 | tf_op jit(solution)/shard_map/pallas_call | solution.py:104
  140.7 18.9 %all_to_all.31 = bf16[8,256,256]{2,1,0:T(8,128)(2,1)S(1)} all-to-all(bf16[8,256,256]{2,1,0:T(8,128)(2,1)} %shard_map.88), channel_id=1, replica_groups=mesh['row'=8,'z'=8,'xh'=2,'core'=2] {'row'}, dimensions={0} | all-to-all | bytes 2097152 | tf_op jit(solution)/shard_map/all_to_all | solution.py:262
  160.6 15.9 %all_to_all.32.slopes = bf16[8,256,256]{2,1,0:T(8,128)(2,1)} all-to-all(bf16[8,256,256]{2,1,0:T(8,128)(2,1)S(1)} %broadcast_in_dim.2), channel_id=1, replica_groups=mesh['row'=8,'z'=8,'xh'=2,'core'=2] {'row'}, dimensions={0} | all-to-all | bytes 2097152 | tf_op jit(solution)/shard_map/all_to_all | solution.py:269
  176.5 6.9 %shard_map.89 = bf16[256,2304]{1,0:T(8,128)(2,1)} custom-call(bf16[8,256,256]{2,1,0:T(8,128)(2,1)} %all_to_all.32.slopes, bf16[256,256]{1,0:T(8,128)(2,1)} %get-tuple-element.24.activated, bf16[2048,2048]{1,0:T(8,128)(2,1)} %bitcast.18), custom_call_target="tpu_custom_call" | custom-call | flops 2147483648 | bytes 10485760 | tf_op jit(solution)/shard_map/pallas_call | solution.py:138
  183.4 43.7 %all_to_all.33 = bf16[32,8,2304]{2,1,0:T(8,128)(2,1)S(1)} all-to-all(bf16[32,8,2304]{2,1,0:T(8,128)(2,1)} %bitcast.21), channel_id=1, replica_groups=mesh['row'=8,'z'=8,'xh'=2,'core'=2] {'z','xh','core'}, dimensions={0} | all-to-all | bytes 2359296 | tf_op jit(solution)/shard_map/all_to_all | solution.py:278
  228.3 1.0 convolution_convert_fusion
  (68 shorter events, 10.9 us)
Async XLA Ops:
  7.2 76.1 %reduce-scatter.2.cloned.1.call-start = ((), (), s32[]{:S(2)}) async-start(), calls=%async_computation.7 | async-start | bytes 2359296 | tf_op jit(solution)/shard_map/reduce_scatter | solution.py:187
  7.2 8.8 %collective-permute-start = (bf16[2048,512]{1,0:T(8,128)(2,1)}, bf16[2048,512]{1,0:T(8,128)(2,1)S(1)}, u32[]{:S(2)}, u32[]{:S(2)}) collective-permute-start(bf16[2048,512]{1,0:T(8,128)(2,1)} %here.3), channel_id=1, source_target_pairs={{0,1},{1,0},{2,3},{3,2},{4,5},{5,4},{6,7},{7,6},{8,9},{9,8},{10,11... | collective-permute-start | bytes 6291464 | tf_op jit(solution)/shard_map/ppermute | solution.py:16
  12.8 3.2 %collective-permute-start.1 = (bf16[1024,512]{1,0:T(8,128)(2,1)}, bf16[1024,512]{1,0:T(8,128)(2,1)S(1)}, u32[]{:S(2)}, u32[]{:S(2)}) collective-permute-start(bf16[1024,512]{1,0:T(8,128)(2,1)} %constant_dynamic-slice_fusion.3), channel_id=1, source_target_pairs={{0,1},{1,0},{2,3},{3,2},{4,5},{5,4},{6,7},{7,6},{8,9},{9,8},{10,11... | collective-permute-start | bytes 3145736 | tf_op jit(solution)/shard_map/ppermute | solution.py:16
  16.0 1.0 copy-start.2
  17.0 1.3 copy-start
  24.5 7.5 %copy-start.4 = (s32[64,2]{0,1:T(2,128)S(1)}, s32[64,2]{0,1:T(2,128)}, u32[]{:S(2)}) copy-start(s32[64,2]{0,1:T(2,128)} %param.10) | copy-start | bytes 1540
  24.5 9.1 %copy-start.5 = (f32[64,2]{0,1:T(2,128)S(1)}, f32[64,2]{0,1:T(2,128)}, u32[]{:S(2)}) copy-start(f32[64,2]{0,1:T(2,128)} %param.11) | copy-start | bytes 1540
  30.9 27.3 %copy-start.1 = (bf16[8,128,512]{2,1,0:T(8,128)(2,1)S(1)}, bf16[8,128,512]{2,1,0:T(8,128)(2,1)}, u32[]{:S(2)}) copy-start(bf16[8,128,512]{2,1,0:T(8,128)(2,1)} %get-tuple-element.12) | copy-start | bytes 3145732
  30.9 27.3 %collective-permute-start.2 = (bf16[8,128,512]{2,1,0:T(8,128)(2,1)}, bf16[8,128,512]{2,1,0:T(8,128)(2,1)S(1)}, u32[]{:S(2)}, u32[]{:S(2)}) collective-permute-start(bf16[8,128,512]{2,1,0:T(8,128)(2,1)} %get-tuple-element.13), channel_id=1, source_target_pairs={{0,2},{2,0},{1,3},{3,1},{4,6},{6,4},{5,7},{7,5},{8,10},{10,8},{9,1... | collective-permute-start | bytes 3145736 | tf_op jit(solution)/shard_map/ppermute | solution.py:16
  31.9 34.2 %collective-permute-start.7 = (s32[64,2]{0,1:T(2,128)S(1)}, s32[64,2]{0,1:T(2,128)S(1)}, u32[]{:S(2)}, u32[]{:S(2)}) collective-permute-start(s32[64,2]{0,1:T(2,128)S(1)} %copy-done.4), channel_id=1, source_target_pairs={{0,1},{1,0},{2,3},{3,2},{4,5},{5,4},{6,7},{7,6},{8,9},{9,8},{10,11... | collective-permute-start | bytes 1544 | tf_op jit(solution)/shard_map/ppermute | solution.py:16
  35.1 24.5 %all-to-all-start = ((bf16[32,8,256]{2,1,0:T(8,128)(2,1)}), bf16[32,8,256]{2,1,0:T(8,128)(2,1)S(1)}, u32[]{:S(2)}, u32[]{:S(2)}) async-start(bf16[32,8,256]{2,1,0:T(8,128)(2,1)} %fusion), calls=%async_computation | async-start | bytes 262144 | tf_op jit(solution)/shard_map/all_to_all | solution.py:236
  44.8 21.6 %collective-permute-start.4 = (bf16[256,512]{1,0:T(8,128)(2,1)S(1)}, bf16[256,512]{1,0:T(8,128)(2,1)S(1)}, u32[]{:S(2)}, u32[]{:S(2)}) collective-permute-start(bf16[256,512]{1,0:T(8,128)(2,1)S(1)} %constant_dynamic-slice_fusion.1), channel_id=1, source_target_pairs={{0,0},{4,12},{8,24},{12,4},{16,16},{20,28},{24,8},{28,20},{32,36},... | collective-permute-start | bytes 786440 | tf_op jit(solution)/shard_map/ppermute | solution.py:181
  59.6 34.9 %all-to-all-start.1 = ((bf16[8,128,512]{2,1,0:T(8,128)(2,1)}), bf16[8,128,512]{2,1,0:T(8,128)(2,1)S(1)}, u32[]{:S(2)}, u32[]{:S(2)}) async-start(bf16[8,128,512]{2,1,0:T(8,128)(2,1)} %add_convert_fusion), calls=%async_computation.1 | async-start | bytes 2097152 | tf_op jit(solution)/shard_map/all_to_all | solution.py:241
  66.2 28.5 %dynamic-slice-start = ((f32[2048]{0:T(1024)}, s32[]{:T(128)}), f32[1024]{0:T(1024)S(1)}, s32[]{:S(2)}) async-start(f32[2048]{0:T(1024)} %param.9, s32[]{:T(128)} %select_n.66), calls=%async_computation.8 | async-start | bytes 8704 | tf_op jit(solution)/shard_map/dynamic_slice | solution.py:20
  66.4 10.5 %collective-permute-start.5 = (bf16[256,512]{1,0:T(8,128)(2,1)S(1)}, bf16[256,512]{1,0:T(8,128)(2,1)S(1)}, u32[]{:S(2)}, u32[]{:S(2)}) collective-permute-start(bf16[256,512]{1,0:T(8,128)(2,1)S(1)} %collective-permute-done.4), channel_id=1, source_target_pairs={{0,0},{1,2},{2,1},{3,3},{4,100},{5,102},{6,101},{7,103},{8,200},{9... | collective-permute-start | bytes 786440 | tf_op jit(solution)/shard_map/ppermute | solution.py:203
  76.9 9.8 %collective-permute-start.6 = (bf16[128,512]{1,0:T(8,128)(2,1)S(1)}, bf16[128,512]{1,0:T(8,128)(2,1)S(1)}, u32[]{:S(2)}, u32[]{:S(2)}) collective-permute-start(bf16[128,512]{1,0:T(8,128)(2,1)S(1)} %constant_dynamic-slice_fusion), channel_id=1, source_target_pairs={{0,2},{2,0},{1,3},{3,1},{4,6},{6,4},{5,7},{7,5},{8,10},{10,8},{9,1... | collective-permute-start | bytes 393224 | tf_op jit(solution)/shard_map/ppermute | solution.py:16
  83.3 11.3 %copy-start.3 = (bf16[256,512]{1,0:T(8,128)(2,1)S(1)}, bf16[256,512]{1,0:T(8,128)(2,1)}, u32[]{:S(2)}) copy-start(bf16[256,512]{1,0:T(8,128)(2,1)} %reduce-scatter.2.cloned.1.call-done) | copy-start | bytes 786436
  84.2 10.2 %collective-permute-start.3 = (bf16[128,512]{1,0:T(8,128)(2,1)S(1)}, bf16[128,512]{1,0:T(8,128)(2,1)S(1)}, u32[]{:S(2)}, u32[]{:S(2)}) collective-permute-start(bf16[128,512]{1,0:T(8,128)(2,1)S(1)} %constant_dynamic-slice_fusion.2), channel_id=1, source_target_pairs={{0,2},{2,0},{1,3},{3,1},{4,6},{6,4},{5,7},{7,5},{8,10},{10,8},{9,1... | collective-permute-start | bytes 393224 | tf_op jit(solution)/shard_map/ppermute | solution.py:16
Sparse Core Ops, SparseCore 0:
  24.6 58.6 reduce-scatter.1

commit v5 on v2

--- a/solution.py
+++ b/solution.py
@@ -1,6 +1,8 @@
 import jax
 import jax.numpy as jnp
 from jax import lax
+from jax.experimental import pallas as pl
+from jax.experimental.pallas import tpu as pltpu
 from jax.sharding import Mesh, PartitionSpec as P
 
 COL = ("z", "xh", "core")
@@ -16,6 +18,140 @@
 
 def piece(values, index, size, axis=0):
     return lax.dynamic_slice_in_dim(values, index * size, size, axis)
+
+
+EARLY = 640
+GRANT = 56 << 20
+CHUNKS, CUTS = 4, 4
+NT = (((1,), (1,)), ((), ()))
+VMEM = pl.BlockSpec(memory_space=pltpu.VMEM)
+
+
+def dot_nt(left, right):
+    return lax.dot_general(left, right, NT, preferred_element_type=jnp.float32)
+
+
+def products_kernel(at, here, there, weight_here, weight_there, early, own, other):
+    values = dot_nt(here[...], weight_here[...]) + dot_nt(there[...], weight_there[...])
+    values = values.astype(jnp.bfloat16)
+    first_width = early.shape[1]
+    planes, rows, columns = own.shape
+    early[...] = values[:, :first_width]
+    late = values[:, first_width:].reshape(planes, 2, rows, columns)
+    first = at[1] == 0
+
+    @pl.when(first)
+    def _():
+        own[...] = late[:, 0]
+        other[...] = late[:, 1]
+
+    @pl.when(jnp.logical_not(first))
+    def _():
+        own[...] = late[:, 1]
+        other[...] = late[:, 0]
+
+
+def cross_products(at, features, features_there, weight_here, weight_there):
+    batch, block = features.shape
+    columns = weight_here.shape[0] // 2
+    late = columns - EARLY
+    steps = 4
+    tile = batch // steps
+    planes, half_plane = Z_N // steps, batch // Z_N // 2
+    rows = pl.BlockSpec((tile, block), lambda i, at: (i, 0))
+    weights = pl.BlockSpec((columns, block), lambda i, at: (at[0], 0))
+    late_spec = pl.BlockSpec((planes, half_plane, late), lambda i, at: (i, 0, 0))
+    late_shape = jax.ShapeDtypeStruct((Z_N, half_plane, late), jnp.bfloat16)
+    return pl.pallas_call(
+        products_kernel,
+        grid_spec=pltpu.PrefetchScalarGridSpec(
+            num_scalar_prefetch=1,
+            grid=(steps,),
+            in_specs=[rows, rows, weights, weights],
+            out_specs=[pl.BlockSpec((tile, EARLY), lambda i, at: (i, 0)), late_spec, late_spec],
+        ),
+        out_shape=[jax.ShapeDtypeStruct((batch, EARLY), jnp.bfloat16), late_shape, late_shape],
+        compiler_params=pltpu.CompilerParams(vmem_limit_bytes=GRANT),
+        cost_estimate=pl.CostEstimate(
+            flops=4 * batch * columns * block, bytes_accessed=10 << 20, transcendentals=0
+        ),
+    )(at, features, features_there, weight_here, weight_there)
+
+
+def weight_copies(source, held, semaphores, by_columns):
+    rows, columns = source.shape
+    copies = []
+    for chunk in range(CHUNKS):
+        for cut in range(CUTS):
+            if by_columns:
+                part = (
+                    pl.ds(cut * (rows // CUTS), rows // CUTS),
+                    pl.ds(chunk * (columns // CHUNKS), columns // CHUNKS),
+                )
+            else:
+                part = (pl.ds((chunk * CUTS + cut) * (rows // CHUNKS // CUTS), rows // CHUNKS // CUTS),)
+            copies.append(
+                pltpu.make_async_copy(
+                    source.at[part], held.at[part], semaphores.at[chunk * CUTS + cut]
+                )
+            )
+    return copies
+
+
+def forward_kernel(routed, weight, out, held, semaphores):
+    copies = weight_copies(weight, held, semaphores, True)
+    for copy in copies:
+        copy.start()
+    shares, slots, share = out.shape
+    half = routed.shape[3]
+    wide = held.shape[1] // CHUNKS
+    low = routed[:, 0].reshape(slots, half)
+    high = routed[:, 1].reshape(slots, half)
+    for chunk in range(CHUNKS):
+        for copy in copies[chunk * CUTS : (chunk + 1) * CUTS]:
+            copy.wait()
+        columns = slice(chunk * wide, (chunk + 1) * wide)
+        values = jnp.dot(low, held[:half, columns], preferred_element_type=jnp.float32)
+        values += jnp.dot(high, held[half:, columns], preferred_element_type=jnp.float32)
+        values = values.astype(jnp.bfloat16)
+        for index in range(wide // share):
+            out[chunk * (wide // share) + index] = values[:, index * share : (index + 1) * share]
+
+
+def back_kernel(slopes, activated, weight, out, held, semaphores):
+    copies = weight_copies(weight, held, semaphores, False)
+    for copy in copies:
+        copy.start()
+    shares, slots, share = slopes.shape
+    width = held.shape[0]
+    tall = width // CHUNKS
+    out[:, width:] = activated[...]
+    for chunk in range(CHUNKS):
+        for copy in copies[chunk * CUTS : (chunk + 1) * CUTS]:
+            copy.wait()
+        rows = slice(chunk * tall, (chunk + 1) * tall)
+        values = jnp.zeros((slots, tall), jnp.float32)
+        for index in range(shares):
+            values += dot_nt(slopes[index], held[rows, index * share : (index + 1) * share])
+        out[:, rows] = values.astype(jnp.bfloat16)
+
+
+def expert_call(kernel, out_shape, *operands):
+    weight = operands[-1]
+    return pl.pallas_call(
+        kernel,
+        in_specs=[VMEM] * (len(operands) - 1) + [pl.BlockSpec(memory_space=pl.ANY)],
+        out_specs=VMEM,
+        out_shape=jax.ShapeDtypeStruct(out_shape, jnp.bfloat16),
+        scratch_shapes=[
+            pltpu.VMEM(weight.shape, weight.dtype),
+            pltpu.SemaphoreType.DMA((CHUNKS * CUTS,)),
+        ],
+        compiler_params=pltpu.CompilerParams(vmem_limit_bytes=GRANT),
+        cost_estimate=pl.CostEstimate(
+            flops=2 * COL_N * CAP * weight.size, bytes_accessed=10 << 20, transcendentals=0
+        ),
+    )(*operands)
 
 
 def slot_targets(expert_ids):
@@ -47,16 +183,15 @@
     plane = lax.ppermute(piece(features, plane_there, 4 * rows), ("row", "z"), perm)
 
     features_there = swap(features, "core")
-    weight_there = swap(piece(cross_weight, 1 - core_at, half), "core")
-    contract = (((1,), (1,)), ((), ()))
-    products = lax.dot_general(
-        features, piece(cross_weight, core_at, half), contract, preferred_element_type=jnp.float32
-    )
-    products = products + lax.dot_general(
-        features_there, weight_there, contract, preferred_element_type=jnp.float32
-    )
-    products, plane = lax.optimization_barrier((products.astype(jnp.bfloat16), plane))
-    part = lax.psum_scatter(products, "z", scatter_dimension=0, tiled=True)
+    weight_there = swap(cross_weight, "core")
+    at = jnp.stack([core_at, xh_at]).astype(jnp.int32)
+    early, late_own, late_other = cross_products(
+        at, features, features_there, cross_weight, weight_there
+    )
+    part = lax.psum_scatter(early, "z", scatter_dimension=0, tiled=True)
+    late_sum = (
+        late_own.astype(jnp.float32) + swap(late_other, "xh").astype(jnp.float32)
+    ).astype(jnp.bfloat16)
 
     perm = []
     for r in range(ROWS_N):
@@ -99,15 +234,21 @@
     send_grad = jnp.dot(
         table, route_grad.reshape(2 * rows, share), preferred_element_type=jnp.float32
     ).astype(jnp.bfloat16)
+
+    late_parts = lax.all_to_all(late_sum, "z", split_axis=0, concat_axis=0, tiled=True)
+    send_grad, late_parts = lax.optimization_barrier((send_grad, late_parts))
     routed_grad = lax.all_to_all(
         send_grad.reshape(COL_N, CAP, share), COL, split_axis=0, concat_axis=0, tiled=True
     ).reshape(slots, share)
-
-    part, base, routed_grad, chip_chooser, chooser, table = lax.optimization_barrier(
-        (part, base, routed_grad, chip_chooser, chooser, table)
-    )
     part_there = swap(piece(part, 1 - xh_at, 2 * rows), "xh")
-    crossed = piece(part, xh_at, 2 * rows).astype(jnp.float32) + part_there.astype(jnp.float32)
+    part_there, routed_grad, base, chip_chooser, chooser, table = lax.optimization_barrier(
+        (part_there, routed_grad, base, chip_chooser, chooser, table)
+    )
+    crossed_late = jnp.sum(late_parts.astype(jnp.float32), axis=0)
+    crossed_early = piece(part, xh_at, 2 * rows).astype(jnp.float32) + part_there.astype(
+        jnp.float32
+    )
+    crossed = jnp.concatenate([crossed_early, crossed_late], axis=1)
     bias = piece(cross_bias, core_at, half)
     hidden = (base * (crossed + bias) + base).astype(jnp.bfloat16)
     send_rows = jnp.dot(chip_chooser, hidden, preferred_element_type=jnp.float32).astype(
@@ -118,12 +259,7 @@
     ).reshape(COL_N // 2, 2, 2 * CAP, half)
 
     weight = expert_weight[0]
-    pre = jnp.dot(
-        routed[:, 0].reshape(slots, half), weight[:half], preferred_element_type=jnp.float32
-    ) + jnp.dot(
-        routed[:, 1].reshape(slots, half), weight[half:], preferred_element_type=jnp.float32
-    )
-    pre = pre.astype(jnp.bfloat16).reshape(slots, ROWS_N, share).transpose(1, 0, 2)
+    pre = expert_call(forward_kernel, (ROWS_N, slots, share), routed, weight)
     parts = lax.all_to_all(pre, "row", split_axis=0, concat_axis=0, tiled=True)
     preact = jnp.sum(parts.astype(jnp.float32), axis=0)
     sigma = jax.nn.sigmoid(preact)
@@ -138,15 +274,11 @@
         concat_axis=0,
         tiled=True,
     )
-    slope_grad = slopes.transpose(1, 0, 2).reshape(slots, out_width)
-    back = lax.dot_general(
-        slope_grad, weight, contract, preferred_element_type=jnp.float32
-    ).astype(jnp.bfloat16)
-
-    answer = jnp.concatenate([back, activated], axis=1).reshape(COL_N, CAP, width + share)
-    returned = lax.all_to_all(answer, COL, split_axis=0, concat_axis=0, tiled=True).reshape(
-        slots, width + share
-    )
+    answer = expert_call(back_kernel, (slots, width + share), slopes, activated, weight)
+
+    returned = lax.all_to_all(
+        answer.reshape(COL_N, CAP, width + share), COL, split_axis=0, concat_axis=0, tiled=True
+    ).reshape(slots, width + share)
     pull = (((0,), (0,)), ((), ()))
     pair_act = lax.dot_general(
         table, returned[:, width:], pull, preferred_element_type=jnp.float32

time: 240 us -> 247 us (1.029)
  matrix products: 27.3 us -> 2.53 us
  Pallas kernels: 0 us -> 22.8 us
  waiting for transfers between devices: 45.8 us -> 51.6 us
    reduce_scatter x1, waiting for transfers between devices: 28.9 us -> 0.02 us  [local(): part = lax.psum_scatter(early, 'z', scatter_dimension=0, tiled=True)]
    dot_general x5 -> x0, matrix products: 22.9 us -> none  [the longest x1 6.22 us: local(): lax.dot_general(features_there, weight_there, contract, preferred_element...]
    pallas_call x0 -> x3, Pallas kernels: none -> 22.8 us  [the longest x2 13.7 us: expert_call(): pl.pallas_call(kernel, in_specs=[VMEM] * (len(operands) - 1) + [pl.BlockS...]
    ppermute x5 -> x6, waiting for transfers between devices: 12.3 us -> 32.2 us  [swap(): return lax.ppermute(values, axis, [(0, 1), (1, 0)])]
    all_to_all x0 -> x1, starting transfers between devices: none -> 9.45 us  [local(): lax.all_to_all(late_sum, 'z', split_axis=0, concat_axis=0, tiled=True)]
    all_to_all x0 -> x1, waiting for transfers between devices: none -> 9.1 us  [local(): lax.all_to_all(late_sum, 'z', split_axis=0, concat_axis=0, tiled=True)]
    all_to_all x1, starting transfers between devices: 14.5 us -> 7.22 us  [local(): lax.all_to_all(send_grad.reshape(COL_N, CAP, share), COL, split_axis=0, c...]
    all_to_all x1, waiting for transfers between devices: 0.01 us -> 6.59 us  [local(): lax.all_to_all(send_grad.reshape(COL_N, CAP, share), COL, split_axis=0, c...]
  transfers between devices with their start and end apart: 9 -> 11, of which waited for: 4 -> 7; matrix products, arithmetic and copies ran while one was open for 7% -> 3% of each run, Pallas kernels for 0% -> 0%
where the time goes in v5:
time: 247 us; the launch traced here: 246 us
  blocking collectives  114 us (46%)
  waiting for transfers between devices  51.6 us (21%)
  starting transfers between devices  31 us (13%)
  Pallas kernels  22.8 us (9%)
  between operations  14.3 us (6%)
  other arithmetic  5.03 us (2%)
  local copies, waits for them, and re-layouts  4.14 us (2%)
  matrix products  2.53 us (1%)
    all_to_all x1, blocking collectives, local(): lax.all_to_all(answer.reshape(COL_N, CAP, width + share), COL, split_axis...  43.7 us
    all_to_all x1, blocking collectives, local(): lax.all_to_all(send_rows.reshape(COL_N, 2 * CAP, half), COL, split_axis=0...  35.9 us
    ppermute x6, waiting for transfers between devices, swap(): return lax.ppermute(values, axis, [(0, 1), (1, 0)])  32.2 us
    all_to_all x1, blocking collectives, local(): parts = lax.all_to_all(pre, 'row', split_axis=0, concat_axis=0, tiled=True)  18.9 us
    all_to_all x1, blocking collectives, local(): lax.all_to_all(jnp.broadcast_to(slope[None], (ROWS_N, slots, share)), 'ro...  15.9 us
    pallas_call x2, Pallas kernels, expert_call(): pl.pallas_call(kernel, in_specs=[VMEM] * (len(operands) - 1) + [pl.BlockS...  13.7 us
    all_to_all x1, starting transfers between devices, local(): lax.all_to_all(late_sum, 'z', split_axis=0, concat_axis=0, tiled=True)  9.45 us
    pallas_call x1, Pallas kernels, cross_products(): pl.pallas_call(products_kernel, grid_spec=pltpu.PrefetchScalarGridSpec(nu...  9.18 us
  transfers between devices with their start and end apart: 11, of which 7 were waited for; matrix products, arithmetic and copies ran while one was open for 3% of the time, Pallas kernels for 0%

profile of v5, /device:TPU:1, one launch (start us, length us, event | category | flops | bytes accessed | tf_op | source)
XLA Modules:
  0.0 245.9 jit_solution(1642658271679191681)
XLA Ops:
  7.2 3.3 %collective-permute-start = (bf16[2048,512]{1,0:T(8,128)(2,1)}, bf16[2048,512]{1,0:T(8,128)(2,1)S(1)}, u32[]{:S(2)}, u32[]{:S(2)}) collective-permute-start(bf16[2048,512]{1,0:T(8,128)(2,1)} %here.1), channel_id=1, source_target_pairs={{0,1},{1,0},{2,3},{3,2},{4,5},{5,4},{6,7},{7,6},{8,9},{9,8},{10,11... | collective-permute-start | bytes 6291464 | tf_op jit(solution)/shard_map/ppermute | solution.py:16
  11.2 5.3 %collective-permute-done.there = bf16[2048,512]{1,0:T(8,128)(2,1)S(1)} collective-permute-done((bf16[2048,512]{1,0:T(8,128)(2,1)}, bf16[2048,512]{1,0:T(8,128)(2,1)S(1)}, u32[]{:S(2)}, u32[]{:S(2)}) %collective-permute-start) | collective-permute-done | bytes 2097184 | tf_op jit(solution)/shard_map/ppermute | solution.py:16
  16.5 1.2 collective-permute-done.1.weight_there
  17.8 9.2 %shard_map.86 = (bf16[2048,640]{1,0:T(8,128)(2,1)}, bf16[8,128,384]{2,1,0:T(8,128)(2,1)}, bf16[8,128,384]{2,1,0:T(8,128)(2,1)}) custom-call(s32[2]{0:T(128)} %pad_add_fusion.at, bf16[2048,512]{1,0:T(8,128)(2,1)} %here.1, bf16[2048,512]{1,0:T(8,128)(2,1)} %copy-done.4, bf16[2048,512]{1,0:T(8,128)(2,1)} %weight_here.1, ...), custom_call_target="tpu_custom_call" | custom-call | flops 4294967296 | bytes 10485760 | tf_op jit(solution)/shard_map/pallas_call | solution.py:65
  27.1 1.1 constant_dynamic-slice_fusion.1
  29.9 1.0 collective-permute-start.3
  31.1 19.4 %collective-permute-done.3 = bf16[8,128,384]{2,1,0:T(8,128)(2,1)S(1)} collective-permute-done((bf16[8,128,384]{2,1,0:T(8,128)(2,1)S(1)}, bf16[8,128,384]{2,1,0:T(8,128)(2,1)S(1)}, u32[]{:S(2)}, u32[]{:S(2)}) %collective-permute-start.3) | collective-permute-done | bytes 786464 | tf_op jit(solution)/shard_map/ppermute | solution.py:16
  50.5 1.1 add_convert_fusion
  51.6 9.4 %all-to-all-start = ((bf16[8,128,384]{2,1,0:T(8,128)(2,1)}), bf16[8,128,384]{2,1,0:T(8,128)(2,1)S(1)}, u32[]{:S(2)}, u32[]{:S(2)}) async-start(bf16[8,128,384]{2,1,0:T(8,128)(2,1)} %add_convert_fusion), calls=%async_computation.1 | async-start | bytes 1572864 | tf_op jit(solution)/shard_map/all_to_all | solution.py:238
  63.3 5.6 %collective-permute-start.5 = (bf16[256,512]{1,0:T(8,128)(2,1)S(1)}, bf16[256,512]{1,0:T(8,128)(2,1)S(1)}, u32[]{:S(2)}, u32[]{:S(2)}) collective-permute-start(bf16[256,512]{1,0:T(8,128)(2,1)S(1)} %collective-permute-done.4), channel_id=1, source_target_pairs={{0,0},{1,2},{2,1},{3,3},{4,100},{5,102},{6,101},{7,103},{8,200},{9... | collective-permute-start | bytes 786440 | tf_op jit(solution)/shard_map/ppermute | solution.py:204
  69.6 3.7 %collective-permute-done.5 = bf16[256,512]{1,0:T(8,128)(2,1)S(1)} collective-permute-done((bf16[256,512]{1,0:T(8,128)(2,1)S(1)}, bf16[256,512]{1,0:T(8,128)(2,1)S(1)}, u32[]{:S(2)}, u32[]{:S(2)}) %collective-permute-start.5) | collective-permute-done | bytes 262176 | tf_op jit(solution)/shard_map/ppermute | solution.py:204
  73.7 6.4 %collective-permute-done.6 = bf16[128,512]{1,0:T(8,128)(2,1)S(1)} collective-permute-done((bf16[128,512]{1,0:T(8,128)(2,1)S(1)}, bf16[128,512]{1,0:T(8,128)(2,1)S(1)}, u32[]{:S(2)}, u32[]{:S(2)}) %collective-permute-start.6) | collective-permute-done | bytes 131104 | tf_op jit(solution)/shard_map/ppermute | solution.py:16
  80.2 9.1 %all-to-all-done = bf16[8,128,384]{2,1,0:T(8,128)(2,1)S(1)} async-done(((bf16[8,128,384]{2,1,0:T(8,128)(2,1)}), bf16[8,128,384]{2,1,0:T(8,128)(2,1)S(1)}, u32[]{:S(2)}, u32[]{:S(2)}) %all-to-all-start) | async-done | bytes 786464 | tf_op jit(solution)/shard_map/all_to_all | solution.py:238
  89.3 7.2 %all-to-all-start.1 = ((bf16[32,8,256]{2,1,0:T(8,128)(2,1)}), bf16[32,8,256]{2,1,0:T(8,128)(2,1)S(1)}, u32[]{:S(2)}, u32[]{:S(2)}) async-start(bf16[32,8,256]{2,1,0:T(8,128)(2,1)} %bitcast.2), calls=%async_computation.2 | async-start | bytes 262144 | tf_op jit(solution)/shard_map/all_to_all | solution.py:240
  96.6 1.0 constant_dynamic-slice_fusion.2
  97.6 3.0 %collective-permute-start.2 = (bf16[128,640]{1,0:T(8,128)(2,1)S(1)}, bf16[128,640]{1,0:T(8,128)(2,1)S(1)}, u32[]{:S(2)}, u32[]{:S(2)}) collective-permute-start(bf16[128,640]{1,0:T(8,128)(2,1)S(1)} %constant_dynamic-slice_fusion.2), channel_id=1, source_target_pairs={{0,2},{2,0},{1,3},{3,1},{4,6},{6,4},{5,7},{7,5},{8,10},{10,8},{9,1... | collective-permute-start | bytes 491528 | tf_op jit(solution)/shard_map/ppermute | solution.py:16
  100.7 6.6 %all-to-all-done.1 = bf16[32,8,256]{2,1,0:T(8,128)(2,1)S(1)} async-done(((bf16[32,8,256]{2,1,0:T(8,128)(2,1)}), bf16[32,8,256]{2,1,0:T(8,128)(2,1)S(1)}, u32[]{:S(2)}, u32[]{:S(2)}) %all-to-all-start.1) | async-done | bytes 131104 | tf_op jit(solution)/shard_map/all_to_all | solution.py:240
  107.8 35.9 %all_to_all.30 = bf16[32,16,1024]{2,1,0:T(8,128)(2,1)} all-to-all(bf16[32,16,1024]{2,1,0:T(8,128)(2,1)S(1)} %bitcast.22), channel_id=1, replica_groups=mesh['row'=8,'z'=8,'xh'=2,'core'=2] {'z','xh','core'}, dimensions={0} | all-to-all | bytes 2097152 | tf_op jit(solution)/shard_map/all_to_all | solution.py:257
  143.7 6.8 %shard_map.87 = bf16[8,256,256]{2,1,0:T(8,128)(2,1)} custom-call(bf16[16,2,16,1024]{3,2,1,0:T(8,128)(2,1)} %bitcast.21, bf16[2048,2048]{1,0:T(8,128)(2,1)} %bitcast.16), custom_call_target="tpu_custom_call" | custom-call | flops 2147483648 | bytes 10485760 | tf_op jit(solution)/shard_map/pallas_call | solution.py:141
  150.5 18.9 %all_to_all.31 = bf16[8,256,256]{2,1,0:T(8,128)(2,1)S(1)} all-to-all(bf16[8,256,256]{2,1,0:T(8,128)(2,1)} %shard_map.87), channel_id=1, replica_groups=mesh['row'=8,'z'=8,'xh'=2,'core'=2] {'row'}, dimensions={0} | all-to-all | bytes 2097152 | tf_op jit(solution)/shard_map/all_to_all | solution.py:263
  170.4 15.9 %all_to_all.32.slopes = bf16[8,256,256]{2,1,0:T(8,128)(2,1)} all-to-all(bf16[8,256,256]{2,1,0:T(8,128)(2,1)S(1)} %broadcast_in_dim.2), channel_id=1, replica_groups=mesh['row'=8,'z'=8,'xh'=2,'core'=2] {'row'}, dimensions={0} | all-to-all | bytes 2097152 | tf_op jit(solution)/shard_map/all_to_all | solution.py:270
  186.3 6.9 %shard_map.88 = bf16[256,2304]{1,0:T(8,128)(2,1)} custom-call(bf16[8,256,256]{2,1,0:T(8,128)(2,1)} %all_to_all.32.slopes, bf16[256,256]{1,0:T(8,128)(2,1)} %get-tuple-element.26.activated, bf16[2048,2048]{1,0:T(8,128)(2,1)} %bitcast.17), custom_call_target="tpu_custom_call" | custom-call | flops 2147483648 | bytes 10485760 | tf_op jit(solution)/shard_map/pallas_call | solution.py:141
  193.2 43.7 %all_to_all.33 = bf16[32,8,2304]{2,1,0:T(8,128)(2,1)S(1)} all-to-all(bf16[32,8,2304]{2,1,0:T(8,128)(2,1)} %bitcast.20), channel_id=1, replica_groups=mesh['row'=8,'z'=8,'xh'=2,'core'=2] {'z','xh','core'}, dimensions={0} | all-to-all | bytes 2359296 | tf_op jit(solution)/shard_map/all_to_all | solution.py:279
  238.0 1.0 convolution_convert_fusion
  (65 shorter events, 9.0 us)
Async XLA Ops:
  7.2 89.4 %reduce-scatter.2.cloned.1.call-start = ((), (), s32[]{:S(2)}) async-start(), calls=%async_computation.7 | async-start | bytes 2949120 | tf_op jit(solution)/shard_map/reduce_scatter | solution.py:191
  7.2 9.3 %collective-permute-start = (bf16[2048,512]{1,0:T(8,128)(2,1)}, bf16[2048,512]{1,0:T(8,128)(2,1)S(1)}, u32[]{:S(2)}, u32[]{:S(2)}) collective-permute-start(bf16[2048,512]{1,0:T(8,128)(2,1)} %here.1), channel_id=1, source_target_pairs={{0,1},{1,0},{2,3},{3,2},{4,5},{5,4},{6,7},{7,6},{8,9},{9,8},{10,11... | collective-permute-start | bytes 6291464 | tf_op jit(solution)/shard_map/ppermute | solution.py:16
  10.5 7.1 %collective-permute-start.1 = (bf16[2048,512]{1,0:T(8,128)(2,1)}, bf16[2048,512]{1,0:T(8,128)(2,1)}, u32[]{:S(2)}, u32[]{:S(2)}) collective-permute-start(bf16[2048,512]{1,0:T(8,128)(2,1)} %weight_here.1), channel_id=1, source_target_pairs={{0,1},{1,0},{2,3},{3,2},{4,5},{5,4},{6,7},{7,6},{8,9},{9,8},{10,11... | collective-permute-start | bytes 6291464 | tf_op jit(solution)/shard_map/ppermute | solution.py:16
  16.5 1.3 copy-start.4
  27.0 1.8 copy-start.2
  27.0 2.9 %copy-start.5 = (bf16[8,128,384]{2,1,0:T(8,128)(2,1)S(1)}, bf16[8,128,384]{2,1,0:T(8,128)(2,1)}, u32[]{:S(2)}) copy-start(bf16[8,128,384]{2,1,0:T(8,128)(2,1)} %get-tuple-element.15) | copy-start | bytes 2359300
  27.0 23.5 %copy-start = (bf16[8,128,384]{2,1,0:T(8,128)(2,1)S(1)}, bf16[8,128,384]{2,1,0:T(8,128)(2,1)}, u32[]{:S(2)}) copy-start(bf16[8,128,384]{2,1,0:T(8,128)(2,1)} %get-tuple-element.14) | copy-start | bytes 2359300
  28.2 35.2 %collective-permute-start.4 = (bf16[256,512]{1,0:T(8,128)(2,1)S(1)}, bf16[256,512]{1,0:T(8,128)(2,1)S(1)}, u32[]{:S(2)}, u32[]{:S(2)}) collective-permute-start(bf16[256,512]{1,0:T(8,128)(2,1)S(1)} %constant_dynamic-slice_fusion.1), channel_id=1, source_target_pairs={{0,0},{4,12},{8,24},{12,4},{16,16},{20,28},{24,8},{28,20},{32,36},... | collective-permute-start | bytes 786440 | tf_op jit(solution)/shard_map/ppermute | solution.py:183
  28.8 40.1 %collective-permute-start.7 = (s32[64,2]{0,1:T(2,128)S(1)}, s32[64,2]{0,1:T(2,128)S(1)}, u32[]{:S(2)}, u32[]{:S(2)}) collective-permute-start(s32[64,2]{0,1:T(2,128)S(1)} %copy-done.2), channel_id=1, source_target_pairs={{0,1},{1,0},{2,3},{3,2},{4,5},{5,4},{6,7},{7,6},{8,9},{9,8},{10,11... | collective-permute-start | bytes 1544 | tf_op jit(solution)/shard_map/ppermute | solution.py:16
  29.9 20.5 %collective-permute-start.3 = (bf16[8,128,384]{2,1,0:T(8,128)(2,1)S(1)}, bf16[8,128,384]{2,1,0:T(8,128)(2,1)S(1)}, u32[]{:S(2)}, u32[]{:S(2)}) collective-permute-start(bf16[8,128,384]{2,1,0:T(8,128)(2,1)S(1)} %copy-done.5), channel_id=1, source_target_pairs={{0,2},{2,0},{1,3},{3,1},{4,6},{6,4},{5,7},{7,5},{8,10},{10,8},{9,1... | collective-permute-start | bytes 2359304 | tf_op jit(solution)/shard_map/ppermute | solution.py:16
  51.6 10.4 %copy-start.3 = (f32[64,2]{0,1:T(2,128)S(1)}, f32[64,2]{0,1:T(2,128)}, u32[]{:S(2)}) copy-start(f32[64,2]{0,1:T(2,128)} %param.11) | copy-start | bytes 1540
  51.6 37.7 %all-to-all-start = ((bf16[8,128,384]{2,1,0:T(8,128)(2,1)}), bf16[8,128,384]{2,1,0:T(8,128)(2,1)S(1)}, u32[]{:S(2)}, u32[]{:S(2)}) async-start(bf16[8,128,384]{2,1,0:T(8,128)(2,1)} %add_convert_fusion), calls=%async_computation.1 | async-start | bytes 1572864 | tf_op jit(solution)/shard_map/all_to_all | solution.py:238
  63.3 9.9 %collective-permute-start.5 = (bf16[256,512]{1,0:T(8,128)(2,1)S(1)}, bf16[256,512]{1,0:T(8,128)(2,1)S(1)}, u32[]{:S(2)}, u32[]{:S(2)}) collective-permute-start(bf16[256,512]{1,0:T(8,128)(2,1)S(1)} %collective-permute-done.4), channel_id=1, source_target_pairs={{0,0},{1,2},{2,1},{3,3},{4,100},{5,102},{6,101},{7,103},{8,200},{9... | collective-permute-start | bytes 786440 | tf_op jit(solution)/shard_map/ppermute | solution.py:204
  73.3 6.8 %collective-permute-start.6 = (bf16[128,512]{1,0:T(8,128)(2,1)S(1)}, bf16[128,512]{1,0:T(8,128)(2,1)S(1)}, u32[]{:S(2)}, u32[]{:S(2)}) collective-permute-start(bf16[128,512]{1,0:T(8,128)(2,1)S(1)} %constant_dynamic-slice_fusion), channel_id=1, source_target_pairs={{0,2},{2,0},{1,3},{3,1},{4,6},{6,4},{5,7},{7,5},{8,10},{10,8},{9,1... | collective-permute-start | bytes 393224 | tf_op jit(solution)/shard_map/ppermute | solution.py:16
  80.2 27.2 %dynamic-slice-start = ((f32[2048]{0:T(1024)}, s32[]{:T(128)}), f32[1024]{0:T(1024)S(1)}, s32[]{:S(2)}) async-start(f32[2048]{0:T(1024)} %param.9, s32[]{:T(128)} %select_n.62), calls=%async_computation.8 | async-start | bytes 8704 | tf_op jit(solution)/shard_map/dynamic_slice | solution.py:20
  89.3 18.0 %all-to-all-start.1 = ((bf16[32,8,256]{2,1,0:T(8,128)(2,1)}), bf16[32,8,256]{2,1,0:T(8,128)(2,1)S(1)}, u32[]{:S(2)}, u32[]{:S(2)}) async-start(bf16[32,8,256]{2,1,0:T(8,128)(2,1)} %bitcast.2), calls=%async_computation.2 | async-start | bytes 262144 | tf_op jit(solution)/shard_map/all_to_all | solution.py:240
  96.6 10.7 %copy-start.1 = (bf16[256,640]{1,0:T(8,128)(2,1)S(1)}, bf16[256,640]{1,0:T(8,128)(2,1)}, u32[]{:S(2)}) copy-start(bf16[256,640]{1,0:T(8,128)(2,1)} %reduce-scatter.2.cloned.1.call-done) | copy-start | bytes 983044
  97.6 9.7 %collective-permute-start.2 = (bf16[128,640]{1,0:T(8,128)(2,1)S(1)}, bf16[128,640]{1,0:T(8,128)(2,1)S(1)}, u32[]{:S(2)}, u32[]{:S(2)}) collective-permute-start(bf16[128,640]{1,0:T(8,128)(2,1)S(1)} %constant_dynamic-slice_fusion.2), channel_id=1, source_target_pairs={{0,2},{2,0},{1,3},{3,1},{4,6},{6,4},{5,7},{7,5},{8,10},{10,8},{9,1... | collective-permute-start | bytes 491528 | tf_op jit(solution)/shard_map/ppermute | solution.py:16
Sparse Core Ops, SparseCore 0:
  27.2 56.5 reduce-scatter.1

commit v6 on v5

--- a/solution.py
+++ b/solution.py
@@ -20,7 +20,7 @@
     return lax.dynamic_slice_in_dim(values, index * size, size, axis)
 
 
-EARLY = 640
+EARLY = 512
 GRANT = 56 << 20
 CHUNKS, CUTS = 4, 4
 NT = (((1,), (1,)), ((), ()))
@@ -103,10 +103,10 @@
     for copy in copies:
         copy.start()
     shares, slots, share = out.shape
-    half = routed.shape[3]
+    half = held.shape[0] // 2
     wide = held.shape[1] // CHUNKS
-    low = routed[:, 0].reshape(slots, half)
-    high = routed[:, 1].reshape(slots, half)
+    low = routed[:, 0, :, :half].reshape(slots, half)
+    high = routed[:, 1, :, :half].reshape(slots, half)
     for chunk in range(CHUNKS):
         for copy in copies[chunk * CUTS : (chunk + 1) * CUTS]:
             copy.wait()
@@ -176,12 +176,6 @@
     share = out_width // ROWS_N
     slots = COL_N * CAP
 
-    plane_there = (3 * z_at + row_at) % Z_N
-    perm = [
-        (r * Z_N + z, r * Z_N + (3 * z + r) % Z_N) for r in range(ROWS_N) for z in range(Z_N)
-    ]
-    plane = lax.ppermute(piece(features, plane_there, 4 * rows), ("row", "z"), perm)
-
     features_there = swap(features, "core")
     weight_there = swap(cross_weight, "core")
     at = jnp.stack([core_at, xh_at]).astype(jnp.int32)
@@ -193,20 +187,23 @@
         late_own.astype(jnp.float32) + swap(late_other, "xh").astype(jnp.float32)
     ).astype(jnp.bfloat16)
 
-    perm = []
-    for r in range(ROWS_N):
-        for z in range(Z_N):
-            for u in range(XH_N):
-                for v in range(CORE_N):
-                    src = ((r * Z_N + z) * XH_N + u) * CORE_N + v
-                    dst = ((3 * (z - r) % Z_N * Z_N + z) * XH_N + v) * CORE_N + u
-                    perm.append((src, dst))
-    plane = lax.ppermute(plane, ALL, perm)
-    base_own = piece(plane, xh_at, 2 * rows)
-    base_other = swap(piece(plane, 1 - xh_at, 2 * rows), "xh")
+    held_features, late_sum = lax.optimization_barrier((features, late_sum))
+    plane_there = (3 * z_at + row_at) % Z_N
+    pieces = []
+    for turn in range(2):
+        perm = []
+        for r in range(ROWS_N):
+            for z in range(Z_N):
+                for u in range(XH_N):
+                    for v in range(CORE_N):
+                        src = ((r * Z_N + z) * XH_N + u) * CORE_N + v
+                        dst = ((z * Z_N + (3 * z + r) % Z_N) * XH_N + (v ^ turn)) * CORE_N + u
+                        perm.append((src, dst))
+        chip_there = plane_there * XH_N + (core_at ^ turn)
+        pieces.append(lax.ppermute(piece(held_features, chip_there, 2 * rows), ALL, perm))
     first = xh_at == 0
     base = jnp.concatenate(
-        [jnp.where(first, base_own, base_other), jnp.where(first, base_other, base_own)], axis=1
+        [jnp.where(first, pieces[0], pieces[1]), jnp.where(first, pieces[1], pieces[0])], axis=1
     ).astype(jnp.float32)
 
     ids_there = swap(expert_ids, "core")
@@ -234,15 +231,16 @@
     send_grad = jnp.dot(
         table, route_grad.reshape(2 * rows, share), preferred_element_type=jnp.float32
     ).astype(jnp.bfloat16)
+    lanes = share // 2
+    send_grad = send_grad.reshape(COL_N, CAP, share)
+    send_grad = jnp.concatenate([send_grad[:, :, :lanes], send_grad[:, :, lanes:]], axis=1)
 
     late_parts = lax.all_to_all(late_sum, "z", split_axis=0, concat_axis=0, tiled=True)
-    send_grad, late_parts = lax.optimization_barrier((send_grad, late_parts))
-    routed_grad = lax.all_to_all(
-        send_grad.reshape(COL_N, CAP, share), COL, split_axis=0, concat_axis=0, tiled=True
-    ).reshape(slots, share)
     part_there = swap(piece(part, 1 - xh_at, 2 * rows), "xh")
-    part_there, routed_grad, base, chip_chooser, chooser, table = lax.optimization_barrier(
-        (part_there, routed_grad, base, chip_chooser, chooser, table)
+    late_parts, part_there, base, chip_chooser, chooser, table, send_grad = (
+        lax.optimization_barrier(
+            (late_parts, part_there, base, chip_chooser, chooser, table, send_grad)
+        )
     )
     crossed_late = jnp.sum(late_parts.astype(jnp.float32), axis=0)
     crossed_early = piece(part, xh_at, 2 * rows).astype(jnp.float32) + part_there.astype(
@@ -254,9 +252,11 @@
     send_rows = jnp.dot(chip_chooser, hidden, preferred_element_type=jnp.float32).astype(
         jnp.bfloat16
     )
-    routed = lax.all_to_all(
-        send_rows.reshape(COL_N, 2 * CAP, half), COL, split_axis=0, concat_axis=0, tiled=True
-    ).reshape(COL_N // 2, 2, 2 * CAP, half)
+    send = jnp.concatenate([send_rows.reshape(COL_N, 2 * CAP, half), send_grad], axis=2)
+    routed = lax.all_to_all(send, COL, split_axis=0, concat_axis=0, tiled=True)
+    grad = routed[:, :, half:]
+    routed_grad = jnp.concatenate([grad[:, :CAP], grad[:, CAP:]], axis=2).reshape(slots, share)
+    routed = routed.reshape(COL_N // 2, 2, 2 * CAP, half + lanes)
 
     weight = expert_weight[0]
     pre = expert_call(forward_kernel, (ROWS_N, slots, share), routed, weight)

time: 247 us -> 244 us (0.988)
  starting transfers between devices: 31 us -> 24.4 us
  waiting for transfers between devices: 51.6 us -> 57.3 us
  blocking collectives: 114 us -> 111 us
    all_to_all x1, waiting for transfers between devices: 6.59 us -> 13.6 us  [local(): parts = lax.all_to_all(pre, 'row', split_axis=0, concat_axis=0, tiled=True)]
    all_to_all x1, waiting for transfers between devices: 9.1 us -> 13.7 us  [local(): lax.all_to_all(late_sum, 'z', split_axis=0, concat_axis=0, tiled=True)]
    ppermute x6 -> x5, waiting for transfers between devices: 32.2 us -> 28.5 us  [swap(): return lax.ppermute(values, axis, [(0, 1), (1, 0)])]
    all_to_all x1, starting transfers between devices: 7.22 us -> 3.66 us  [local(): parts = lax.all_to_all(pre, 'row', split_axis=0, concat_axis=0, tiled=True)]
    all_to_all x1, blocking collectives: 43.7 us -> 40.2 us  [local(): lax.all_to_all(answer.reshape(COL_N, CAP, width + share), COL, split_axis...]
    all_to_all x1, starting transfers between devices: 9.45 us -> 6.45 us  [local(): lax.all_to_all(late_sum, 'z', split_axis=0, concat_axis=0, tiled=True)]
    all_to_all x2 -> x1, blocking collectives: 54.8 us -> 53.3 us  [local(): routed = lax.all_to_all(send, COL, split_axis=0, concat_axis=0, tiled=True)]
    ppermute x6 -> x5, starting transfers between devices: 8 us -> 8.13 us  [swap(): return lax.ppermute(values, axis, [(0, 1), (1, 0)])]
  transfers between devices with their start and end apart: 11 -> 10, of which waited for: 7 -> 6; matrix products, arithmetic and copies ran while one was open for 3% -> 3% of each run, Pallas kernels for 0% -> 0%
where the time goes in v6:
time: 244 us; the launch traced here: 243 us
  blocking collectives  111 us (45%)
  waiting for transfers between devices  57.3 us (23%)
  starting transfers between devices  24.4 us (10%)
  Pallas kernels  22.9 us (9%)
  between operations  14.3 us (6%)
  local copies, waits for them, and re-layouts  6.09 us (2%)
  other arithmetic  5.34 us (2%)
    all_to_all x1, blocking collectives, local(): routed = lax.all_to_all(send, COL, split_axis=0, concat_axis=0, tiled=True)  53.3 us
    all_to_all x1, blocking collectives, local(): lax.all_to_all(answer.reshape(COL_N, CAP, width + share), COL, split_axis...  40.2 us
    ppermute x5, waiting for transfers between devices, swap(): return lax.ppermute(values, axis, [(0, 1), (1, 0)])  28.5 us
    all_to_all x1, blocking collectives, local(): lax.all_to_all(jnp.broadcast_to(slope[None], (ROWS_N, slots, share)), 'ro...  17.4 us
    pallas_call x2, Pallas kernels, expert_call(): pl.pallas_call(kernel, in_specs=[VMEM] * (len(operands) - 1) + [pl.BlockS...  13.7 us
    all_to_all x1, waiting for transfers between devices, local(): lax.all_to_all(late_sum, 'z', split_axis=0, concat_axis=0, tiled=True)  13.7 us
    all_to_all x1, waiting for transfers between devices, local(): parts = lax.all_to_all(pre, 'row', split_axis=0, concat_axis=0, tiled=True)  13.6 us
    pallas_call x1, Pallas kernels, cross_products(): pl.pallas_call(products_kernel, grid_spec=pltpu.PrefetchScalarGridSpec(nu...  9.23 us
  transfers between devices with their start and end apart: 10, of which 6 were waited for; matrix products, arithmetic and copies ran while one was open for 3% of the time, Pallas kernels for 0%

profile of v6, /device:TPU:1, one launch (start us, length us, event | category | flops | bytes accessed | tf_op | source)
XLA Modules:
  0.0 243.2 jit_solution(7211807978453934379)
XLA Ops:
  7.2 3.3 %collective-permute-start = (bf16[2048,512]{1,0:T(8,128)(2,1)}, bf16[2048,512]{1,0:T(8,128)(2,1)S(1)}, u32[]{:S(2)}, u32[]{:S(2)}) collective-permute-start(bf16[2048,512]{1,0:T(8,128)(2,1)} %here.1), channel_id=1, source_target_pairs={{0,1},{1,0},{2,3},{3,2},{4,5},{5,4},{6,7},{7,6},{8,9},{9,8},{10,11... | collective-permute-start | bytes 6291464 | tf_op jit(solution)/shard_map/ppermute | solution.py:16
  11.2 5.3 %collective-permute-done.there = bf16[2048,512]{1,0:T(8,128)(2,1)S(1)} collective-permute-done((bf16[2048,512]{1,0:T(8,128)(2,1)}, bf16[2048,512]{1,0:T(8,128)(2,1)S(1)}, u32[]{:S(2)}, u32[]{:S(2)}) %collective-permute-start) | collective-permute-done | bytes 2097184 | tf_op jit(solution)/shard_map/ppermute | solution.py:16
  16.5 1.2 collective-permute-done.1.weight_there
  17.8 9.2 %shard_map.86 = (bf16[2048,512]{1,0:T(8,128)(2,1)}, bf16[8,128,512]{2,1,0:T(8,128)(2,1)}, bf16[8,128,512]{2,1,0:T(8,128)(2,1)}) custom-call(s32[2]{0:T(128)} %pad_add_fusion.at, bf16[2048,512]{1,0:T(8,128)(2,1)} %here.1, bf16[2048,512]{1,0:T(8,128)(2,1)} %copy-done.4, bf16[2048,512]{1,0:T(8,128)(2,1)} %weight_here.1, ...), custom_call_target="tpu_custom_call" | custom-call | flops 4294967296 | bytes 10485760 | tf_op jit(solution)/shard_map/pallas_call | solution.py:65
  27.1 1.2 copy-done.5
  28.3 1.0 collective-permute-start.2
  32.1 22.0 %collective-permute-done.2 = bf16[8,128,512]{2,1,0:T(8,128)(2,1)S(1)} collective-permute-done((bf16[8,128,512]{2,1,0:T(8,128)(2,1)S(1)}, bf16[8,128,512]{2,1,0:T(8,128)(2,1)S(1)}, u32[]{:S(2)}, u32[]{:S(2)}) %collective-permute-start.2) | collective-permute-done | bytes 1048608 | tf_op jit(solution)/shard_map/ppermute | solution.py:16
  54.1 1.3 add_convert_fusion
  55.5 6.4 %all-to-all-start = ((bf16[8,128,512]{2,1,0:T(8,128)(2,1)}), bf16[8,128,512]{2,1,0:T(8,128)(2,1)S(1)}, u32[]{:S(2)}, u32[]{:S(2)}) async-start(bf16[8,128,512]{2,1,0:T(8,128)(2,1)} %add_convert_fusion), calls=%async_computation | async-start | bytes 2097152 | tf_op jit(solution)/shard_map/all_to_all | solution.py:238
  63.1 1.0 constant_dynamic-slice_fusion.1
  64.2 6.0 %collective-permute-start.4 = (bf16[128,512]{1,0:T(8,128)(2,1)S(1)}, bf16[128,512]{1,0:T(8,128)(2,1)S(1)}, u32[]{:S(2)}, u32[]{:S(2)}) collective-permute-start(bf16[128,512]{1,0:T(8,128)(2,1)S(1)} %get-tuple-element.26), channel_id=1, source_target_pairs={{0,0},{1,2},{2,1},{3,3},{4,44},{5,46},{6,45},{7,47},{8,88},{9,90},... | collective-permute-start | bytes 393224 | tf_op jit(solution)/shard_map/ppermute | solution.py:203
  70.4 1.0 constant_dynamic-slice_fusion.2
  71.4 3.0 %collective-permute-start.3 = (bf16[128,512]{1,0:T(8,128)(2,1)S(1)}, bf16[128,512]{1,0:T(8,128)(2,1)S(1)}, u32[]{:S(2)}, u32[]{:S(2)}) collective-permute-start(bf16[128,512]{1,0:T(8,128)(2,1)S(1)} %constant_dynamic-slice_fusion.2), channel_id=1, source_target_pairs={{0,2},{2,0},{1,3},{3,1},{4,6},{6,4},{5,7},{7,5},{8,10},{10,8},{9,1... | collective-permute-start | bytes 393224 | tf_op jit(solution)/shard_map/ppermute | solution.py:16
  74.4 1.5 collective-permute-done.5
  76.0 13.7 %all-to-all-done = bf16[8,128,512]{2,1,0:T(8,128)(2,1)S(1)} async-done(((bf16[8,128,512]{2,1,0:T(8,128)(2,1)}), bf16[8,128,512]{2,1,0:T(8,128)(2,1)S(1)}, u32[]{:S(2)}, u32[]{:S(2)}) %all-to-all-start) | async-done | bytes 1048608 | tf_op jit(solution)/shard_map/all_to_all | solution.py:238
  90.4 53.3 %all_to_all.25 = bf16[32,16,1152]{2,1,0:T(8,128)(2,1)} all-to-all(bf16[32,16,1152]{2,1,0:T(8,128)(2,1)S(1)} %pad_maximum_fusion), channel_id=1, replica_groups=mesh['row'=8,'z'=8,'xh'=2,'core'=2] {'z','xh','core'}, dimensions={0} | all-to-all | bytes 2359296 | tf_op jit(solution)/shard_map/all_to_all | solution.py:256
  143.7 6.8 %shard_map.87 = bf16[8,256,256]{2,1,0:T(8,128)(2,1)} custom-call(bf16[16,2,16,1152]{3,2,1,0:T(8,128)(2,1)} %bitcast.23, bf16[2048,2048]{1,0:T(8,128)(2,1)} %bitcast.21), custom_call_target="tpu_custom_call" | custom-call | flops 2147483648 | bytes 10485760 | tf_op jit(solution)/shard_map/pallas_call | solution.py:141
  150.6 3.7 %all-to-all-start.2 = ((bf16[8,256,256]{2,1,0:T(8,128)(2,1)}), bf16[8,256,256]{2,1,0:T(8,128)(2,1)S(1)}, u32[]{:S(2)}, u32[]{:S(2)}) async-start(bf16[8,256,256]{2,1,0:T(8,128)(2,1)} %shard_map.87), calls=%async_computation.3 | async-start | bytes 2097152 | tf_op jit(solution)/shard_map/all_to_all | solution.py:263
  154.2 0.9 fusion.19
  155.1 13.6 %all-to-all-done.2 = bf16[8,256,256]{2,1,0:T(8,128)(2,1)S(1)} async-done(((bf16[8,256,256]{2,1,0:T(8,128)(2,1)}), bf16[8,256,256]{2,1,0:T(8,128)(2,1)S(1)}, u32[]{:S(2)}, u32[]{:S(2)}) %all-to-all-start.2) | async-done | bytes 1048608 | tf_op jit(solution)/shard_map/all_to_all | solution.py:263
  169.7 17.4 %all_to_all.26.slopes = bf16[8,256,256]{2,1,0:T(8,128)(2,1)} all-to-all(bf16[8,256,256]{2,1,0:T(8,128)(2,1)S(1)} %broadcast_in_dim.2), channel_id=1, replica_groups=mesh['row'=8,'z'=8,'xh'=2,'core'=2] {'row'}, dimensions={0} | all-to-all | bytes 2097152 | tf_op jit(solution)/shard_map/all_to_all | solution.py:270
  187.1 6.9 %shard_map.88 = bf16[256,2304]{1,0:T(8,128)(2,1)} custom-call(bf16[8,256,256]{2,1,0:T(8,128)(2,1)} %all_to_all.26.slopes, bf16[256,256]{1,0:T(8,128)(2,1)} %get-tuple-element.30.activated, bf16[2048,2048]{1,0:T(8,128)(2,1)} %bitcast.22), custom_call_target="tpu_custom_call" | custom-call | flops 2147483648 | bytes 10485760 | tf_op jit(solution)/shard_map/pallas_call | solution.py:141
  194.0 40.2 %all_to_all.27 = bf16[32,8,2304]{2,1,0:T(8,128)(2,1)S(1)} all-to-all(bf16[32,8,2304]{2,1,0:T(8,128)(2,1)} %bitcast.26), channel_id=1, replica_groups=mesh['row'=8,'z'=8,'xh'=2,'core'=2] {'z','xh','core'}, dimensions={0} | all-to-all | bytes 2359296 | tf_op jit(solution)/shard_map/all_to_all | solution.py:279
  235.3 1.0 convolution_convert_fusion
  (65 shorter events, 7.9 us)
Async XLA Ops:
  7.2 63.2 %reduce-scatter.2.cloned.1.call-start = ((), (), s32[]{:S(2)}) async-start(), calls=%async_computation.6 | async-start | bytes 2359296 | tf_op jit(solution)/shard_map/reduce_scatter | solution.py:185
  7.2 9.3 %collective-permute-start = (bf16[2048,512]{1,0:T(8,128)(2,1)}, bf16[2048,512]{1,0:T(8,128)(2,1)S(1)}, u32[]{:S(2)}, u32[]{:S(2)}) collective-permute-start(bf16[2048,512]{1,0:T(8,128)(2,1)} %here.1), channel_id=1, source_target_pairs={{0,1},{1,0},{2,3},{3,2},{4,5},{5,4},{6,7},{7,6},{8,9},{9,8},{10,11... | collective-permute-start | bytes 6291464 | tf_op jit(solution)/shard_map/ppermute | solution.py:16
  10.5 7.1 %collective-permute-start.1 = (bf16[2048,512]{1,0:T(8,128)(2,1)}, bf16[2048,512]{1,0:T(8,128)(2,1)}, u32[]{:S(2)}, u32[]{:S(2)}) collective-permute-start(bf16[2048,512]{1,0:T(8,128)(2,1)} %weight_here.1), channel_id=1, source_target_pairs={{0,1},{1,0},{2,3},{3,2},{4,5},{5,4},{6,7},{7,6},{8,9},{9,8},{10,11... | collective-permute-start | bytes 6291464 | tf_op jit(solution)/shard_map/ppermute | solution.py:16
  16.5 1.3 copy-start.4
  27.0 1.2 copy-start.5
  27.0 2.2 copy-start.2
  27.0 4.5 %copy-start.3 = (f32[64,2]{0,1:T(2,128)S(1)}, f32[64,2]{0,1:T(2,128)}, u32[]{:S(2)}) copy-start(f32[64,2]{0,1:T(2,128)} %param.11) | copy-start | bytes 1540
  27.1 27.1 %copy-start = (bf16[8,128,512]{2,1,0:T(8,128)(2,1)S(1)}, bf16[8,128,512]{2,1,0:T(8,128)(2,1)}, u32[]{:S(2)}) copy-start(bf16[8,128,512]{2,1,0:T(8,128)(2,1)} %get-tuple-element.14) | copy-start | bytes 3145732
  28.3 25.9 %collective-permute-start.2 = (bf16[8,128,512]{2,1,0:T(8,128)(2,1)S(1)}, bf16[8,128,512]{2,1,0:T(8,128)(2,1)S(1)}, u32[]{:S(2)}, u32[]{:S(2)}) collective-permute-start(bf16[8,128,512]{2,1,0:T(8,128)(2,1)S(1)} %copy-done.5), channel_id=1, source_target_pairs={{0,2},{2,0},{1,3},{3,1},{4,6},{6,4},{5,7},{7,5},{8,10},{10,8},{9,1... | collective-permute-start | bytes 3145736 | tf_op jit(solution)/shard_map/ppermute | solution.py:16
  29.3 32.9 %collective-permute-start.6 = (s32[64,2]{0,1:T(2,128)S(1)}, s32[64,2]{0,1:T(2,128)S(1)}, u32[]{:S(2)}, u32[]{:S(2)}) collective-permute-start(s32[64,2]{0,1:T(2,128)S(1)} %copy-done.2), channel_id=1, source_target_pairs={{0,1},{1,0},{2,3},{3,2},{4,5},{5,4},{6,7},{7,6},{8,9},{9,8},{10,11... | collective-permute-start | bytes 1544 | tf_op jit(solution)/shard_map/ppermute | solution.py:16
  55.5 34.2 %all-to-all-start = ((bf16[8,128,512]{2,1,0:T(8,128)(2,1)}), bf16[8,128,512]{2,1,0:T(8,128)(2,1)S(1)}, u32[]{:S(2)}, u32[]{:S(2)}) async-start(bf16[8,128,512]{2,1,0:T(8,128)(2,1)} %add_convert_fusion), calls=%async_computation | async-start | bytes 2097152 | tf_op jit(solution)/shard_map/all_to_all | solution.py:238
  62.9 26.9 %dynamic-slice-start = ((f32[2048]{0:T(1024)}, s32[]{:T(128)}), f32[1024]{0:T(1024)S(1)}, s32[]{:S(2)}) async-start(f32[2048]{0:T(1024)} %param.9, s32[]{:T(128)} %select_n.64), calls=%async_computation.7 | async-start | bytes 8704 | tf_op jit(solution)/shard_map/dynamic_slice | solution.py:20
  64.2 10.3 %collective-permute-start.4 = (bf16[128,512]{1,0:T(8,128)(2,1)S(1)}, bf16[128,512]{1,0:T(8,128)(2,1)S(1)}, u32[]{:S(2)}, u32[]{:S(2)}) collective-permute-start(bf16[128,512]{1,0:T(8,128)(2,1)S(1)} %get-tuple-element.26), channel_id=1, source_target_pairs={{0,0},{1,2},{2,1},{3,3},{4,44},{5,46},{6,45},{7,47},{8,88},{9,90},... | collective-permute-start | bytes 393224 | tf_op jit(solution)/shard_map/ppermute | solution.py:203
  70.2 5.7 %collective-permute-start.5 = (bf16[128,512]{1,0:T(8,128)(2,1)S(1)}, bf16[128,512]{1,0:T(8,128)(2,1)S(1)}, u32[]{:S(2)}, u32[]{:S(2)}) collective-permute-start(bf16[128,512]{1,0:T(8,128)(2,1)S(1)} %get-tuple-element.27), channel_id=1, source_target_pairs={{0,2},{1,0},{2,3},{3,1},{4,46},{5,44},{6,47},{7,45},{8,90},{9,88},... | collective-permute-start | bytes 393224 | tf_op jit(solution)/shard_map/ppermute | solution.py:203
  70.4 19.4 %copy-start.1 = (bf16[256,512]{1,0:T(8,128)(2,1)S(1)}, bf16[256,512]{1,0:T(8,128)(2,1)}, u32[]{:S(2)}) copy-start(bf16[256,512]{1,0:T(8,128)(2,1)} %reduce-scatter.2.cloned.1.call-done) | copy-start | bytes 786436
  71.4 18.3 %collective-permute-start.3 = (bf16[128,512]{1,0:T(8,128)(2,1)S(1)}, bf16[128,512]{1,0:T(8,128)(2,1)S(1)}, u32[]{:S(2)}, u32[]{:S(2)}) collective-permute-start(bf16[128,512]{1,0:T(8,128)(2,1)S(1)} %constant_dynamic-slice_fusion.2), channel_id=1, source_target_pairs={{0,2},{2,0},{1,3},{3,1},{4,6},{6,4},{5,7},{7,5},{8,10},{10,8},{9,1... | collective-permute-start | bytes 393224 | tf_op jit(solution)/shard_map/ppermute | solution.py:16
  150.6 18.2 %all-to-all-start.2 = ((bf16[8,256,256]{2,1,0:T(8,128)(2,1)}), bf16[8,256,256]{2,1,0:T(8,128)(2,1)S(1)}, u32[]{:S(2)}, u32[]{:S(2)}) async-start(bf16[8,256,256]{2,1,0:T(8,128)(2,1)} %shard_map.87), calls=%async_computation.3 | async-start | bytes 2097152 | tf_op jit(solution)/shard_map/all_to_all | solution.py:263
Sparse Core Ops, SparseCore 0:
  27.2 38.6 reduce-scatter.1

commit v7 on v6

--- a/solution.py
+++ b/solution.py
@@ -176,18 +176,6 @@
     share = out_width // ROWS_N
     slots = COL_N * CAP
 
-    features_there = swap(features, "core")
-    weight_there = swap(cross_weight, "core")
-    at = jnp.stack([core_at, xh_at]).astype(jnp.int32)
-    early, late_own, late_other = cross_products(
-        at, features, features_there, cross_weight, weight_there
-    )
-    part = lax.psum_scatter(early, "z", scatter_dimension=0, tiled=True)
-    late_sum = (
-        late_own.astype(jnp.float32) + swap(late_other, "xh").astype(jnp.float32)
-    ).astype(jnp.bfloat16)
-
-    held_features, late_sum = lax.optimization_barrier((features, late_sum))
     plane_there = (3 * z_at + row_at) % Z_N
     pieces = []
     for turn in range(2):
@@ -200,7 +188,20 @@
                         dst = ((z * Z_N + (3 * z + r) % Z_N) * XH_N + (v ^ turn)) * CORE_N + u
                         perm.append((src, dst))
         chip_there = plane_there * XH_N + (core_at ^ turn)
-        pieces.append(lax.ppermute(piece(held_features, chip_there, 2 * rows), ALL, perm))
+        pieces.append(lax.ppermute(piece(features, chip_there, 2 * rows), ALL, perm))
+
+    features_there = swap(features, "core")
+    weight_there = swap(cross_weight, "core")
+    at = jnp.stack([core_at, xh_at]).astype(jnp.int32)
+    early, late_own, late_other = cross_products(
+        at, features, features_there, cross_weight, weight_there
+    )
+    early, pieces = lax.optimization_barrier((early, pieces))
+    part = lax.psum_scatter(early, "z", scatter_dimension=0, tiled=True)
+    late_sum = (
+        late_own.astype(jnp.float32) + swap(late_other, "xh").astype(jnp.float32)
+    ).astype(jnp.bfloat16)
+
     first = xh_at == 0
     base = jnp.concatenate(
         [jnp.where(first, pieces[0], pieces[1]), jnp.where(first, pieces[1], pieces[0])], axis=1

time: 244 us -> 236 us (0.967)
  blocking collectives: 111 us -> 97.8 us
  starting transfers between devices: 24.4 us -> 28.6 us
    all_to_all x1, blocking collectives: 53.3 us -> 40.4 us  [local(): routed = lax.all_to_all(send, COL, split_axis=0, concat_axis=0, tiled=True)]
    all_to_all x1, starting transfers between devices: 6.45 us -> 13.1 us  [local(): lax.all_to_all(late_sum, 'z', split_axis=0, concat_axis=0, tiled=True)]
    all_to_all x1, waiting for transfers between devices: 13.7 us -> 20.1 us  [local(): lax.all_to_all(late_sum, 'z', split_axis=0, concat_axis=0, tiled=True)]
    ppermute x5, waiting for transfers between devices: 28.5 us -> 24.5 us  [swap(): return lax.ppermute(values, axis, [(0, 1), (1, 0)])]
    ppermute x2, starting transfers between devices: 6.12 us -> 3.3 us  [local(): lax.ppermute(piece(features, chip_there, 2 * rows), ALL, perm)]
  transfers between devices with their start and end apart: 10 -> 10, of which waited for: 6 -> 5; matrix products, arithmetic and copies ran while one was open for 3% -> 3% of each run, Pallas kernels for 0% -> 4%
where the time goes in v7:
time: 236 us; the launch traced here: 235 us
  blocking collectives  97.8 us (41%)
  waiting for transfers between devices  59.7 us (25%)
  starting transfers between devices  28.6 us (12%)
  Pallas kernels  22.9 us (10%)
  between operations  14.3 us (6%)
  other arithmetic  5.4 us (2%)
  local copies, waits for them, and re-layouts  4.75 us (2%)
    all_to_all x1, blocking collectives, local(): routed = lax.all_to_all(send, COL, split_axis=0, concat_axis=0, tiled=True)  40.4 us
    all_to_all x1, blocking collectives, local(): lax.all_to_all(answer.reshape(COL_N, CAP, width + share), COL, split_axis...  39 us
    ppermute x5, waiting for transfers between devices, swap(): return lax.ppermute(values, axis, [(0, 1), (1, 0)])  24.5 us
    all_to_all x1, waiting for transfers between devices, local(): lax.all_to_all(late_sum, 'z', split_axis=0, concat_axis=0, tiled=True)  20.1 us
    all_to_all x1, blocking collectives, local(): lax.all_to_all(jnp.broadcast_to(slope[None], (ROWS_N, slots, share)), 'ro...  18.4 us
    pallas_call x2, Pallas kernels, expert_call(): pl.pallas_call(kernel, in_specs=[VMEM] * (len(operands) - 1) + [pl.BlockS...  13.7 us
    all_to_all x1, waiting for transfers between devices, local(): parts = lax.all_to_all(pre, 'row', split_axis=0, concat_axis=0, tiled=True)  13.6 us
    all_to_all x1, starting transfers between devices, local(): lax.all_to_all(late_sum, 'z', split_axis=0, concat_axis=0, tiled=True)  13.1 us
  transfers between devices with their start and end apart: 10, of which 5 were waited for; matrix products, arithmetic and copies ran while one was open for 3% of the time, Pallas kernels for 4%

profile of v7, /device:TPU:1, one launch (start us, length us, event | category | flops | bytes accessed | tf_op | source)
XLA Modules:
  0.0 235.4 jit_solution(9559668654507136480)
XLA Ops:
  7.2 3.3 %collective-permute-start = (bf16[2048,512]{1,0:T(8,128)(2,1)}, bf16[2048,512]{1,0:T(8,128)(2,1)}, u32[]{:S(2)}, u32[]{:S(2)}) collective-permute-start(bf16[2048,512]{1,0:T(8,128)(2,1)} %here.1), channel_id=1, source_target_pairs={{0,1},{1,0},{2,3},{3,2},{4,5},{5,4},{6,7},{7,6},{8,9},{9,8},{10,11... | collective-permute-start | bytes 6291464 | tf_op jit(solution)/shard_map/ppermute | solution.py:16
  10.6 1.0 constant_dynamic-slice_fusion.1
  11.6 3.2 %collective-permute-start.3 = (bf16[128,512]{1,0:T(8,128)(2,1)S(1)}, bf16[128,512]{1,0:T(8,128)(2,1)S(1)}, u32[]{:S(2)}, u32[]{:S(2)}) collective-permute-start(bf16[128,512]{1,0:T(8,128)(2,1)S(1)} %get-tuple-element.29), channel_id=1, source_target_pairs={{0,0},{1,2},{2,1},{3,3},{4,44},{5,46},{6,45},{7,47},{8,88},{9,90},... | collective-permute-start | bytes 393224 | tf_op jit(solution)/shard_map/ppermute | solution.py:191
  15.5 2.1 collective-permute-done.1.weight_there
  17.7 9.2 %shard_map.86 = (bf16[2048,512]{1,0:T(8,128)(2,1)}, bf16[8,128,512]{2,1,0:T(8,128)(2,1)}, bf16[8,128,512]{2,1,0:T(8,128)(2,1)}) custom-call(s32[2]{0:T(128)} %pad_add_fusion.at, bf16[2048,512]{1,0:T(8,128)(2,1)} %here.1, bf16[2048,512]{1,0:T(8,128)(2,1)} %collective-permute-done.there, bf16[2048,512]{1,0:T(8,128)(2,1)} %weight_here.1, ...), custom_call_target="tpu_custom_call" | custom-call | flops 4294967296 | bytes 10485760 | tf_op jit(solution)/shard_map/pallas_call | solution.py:65
  26.9 1.1 collective-permute-start.2
  29.3 0.8 dynamic-slice_convert_fusion
  30.8 22.3 %collective-permute-done.2 = bf16[8,128,512]{2,1,0:T(8,128)(2,1)S(1)} collective-permute-done((bf16[8,128,512]{2,1,0:T(8,128)(2,1)}, bf16[8,128,512]{2,1,0:T(8,128)(2,1)S(1)}, u32[]{:S(2)}, u32[]{:S(2)}) %collective-permute-start.2) | collective-permute-done | bytes 1048608 | tf_op jit(solution)/shard_map/ppermute | solution.py:16
  53.1 1.3 add_convert_fusion
  54.4 13.1 %all-to-all-start = ((bf16[8,128,512]{2,1,0:T(8,128)(2,1)}), bf16[8,128,512]{2,1,0:T(8,128)(2,1)S(1)}, u32[]{:S(2)}, u32[]{:S(2)}) async-start(bf16[8,128,512]{2,1,0:T(8,128)(2,1)} %add_convert_fusion), calls=%async_computation | async-start | bytes 2097152 | tf_op jit(solution)/shard_map/all_to_all | solution.py:239
  69.0 1.4 reduce-scatter.2.cloned.1.call-done
  70.4 1.0 constant_dynamic-slice_fusion
  71.4 3.4 %collective-permute-start.5 = (bf16[128,512]{1,0:T(8,128)(2,1)S(1)}, bf16[128,512]{1,0:T(8,128)(2,1)S(1)}, u32[]{:S(2)}, u32[]{:S(2)}) collective-permute-start(bf16[128,512]{1,0:T(8,128)(2,1)S(1)} %constant_dynamic-slice_fusion), channel_id=1, source_target_pairs={{0,2},{2,0},{1,3},{3,1},{4,6},{6,4},{5,7},{7,5},{8,10},{10,8},{9,1... | collective-permute-start | bytes 393224 | tf_op jit(solution)/shard_map/ppermute | solution.py:16
  74.8 20.1 %all-to-all-done = bf16[8,128,512]{2,1,0:T(8,128)(2,1)S(1)} async-done(((bf16[8,128,512]{2,1,0:T(8,128)(2,1)}), bf16[8,128,512]{2,1,0:T(8,128)(2,1)S(1)}, u32[]{:S(2)}, u32[]{:S(2)}) %all-to-all-start) | async-done | bytes 1048608 | tf_op jit(solution)/shard_map/all_to_all | solution.py:239
  95.7 40.4 %all_to_all.25 = bf16[32,16,1152]{2,1,0:T(8,128)(2,1)} all-to-all(bf16[32,16,1152]{2,1,0:T(8,128)(2,1)S(1)} %pad_maximum_fusion), channel_id=1, replica_groups=mesh['row'=8,'z'=8,'xh'=2,'core'=2] {'z','xh','core'}, dimensions={0} | all-to-all | bytes 2359296 | tf_op jit(solution)/shard_map/all_to_all | solution.py:257
  136.2 6.8 %shard_map.87 = bf16[8,256,256]{2,1,0:T(8,128)(2,1)} custom-call(bf16[16,2,16,1152]{3,2,1,0:T(8,128)(2,1)} %bitcast.23, bf16[2048,2048]{1,0:T(8,128)(2,1)} %bitcast.21), custom_call_target="tpu_custom_call" | custom-call | flops 2147483648 | bytes 10485760 | tf_op jit(solution)/shard_map/pallas_call | solution.py:141
  143.0 3.7 %all-to-all-start.2 = ((bf16[8,256,256]{2,1,0:T(8,128)(2,1)}), bf16[8,256,256]{2,1,0:T(8,128)(2,1)S(1)}, u32[]{:S(2)}, u32[]{:S(2)}) async-start(bf16[8,256,256]{2,1,0:T(8,128)(2,1)} %shard_map.87), calls=%async_computation.3 | async-start | bytes 2097152 | tf_op jit(solution)/shard_map/all_to_all | solution.py:264
  146.7 0.9 fusion.19
  147.5 13.6 %all-to-all-done.2 = bf16[8,256,256]{2,1,0:T(8,128)(2,1)S(1)} async-done(((bf16[8,256,256]{2,1,0:T(8,128)(2,1)}), bf16[8,256,256]{2,1,0:T(8,128)(2,1)S(1)}, u32[]{:S(2)}, u32[]{:S(2)}) %all-to-all-start.2) | async-done | bytes 1048608 | tf_op jit(solution)/shard_map/all_to_all | solution.py:264
  162.1 18.4 %all_to_all.26.slopes = bf16[8,256,256]{2,1,0:T(8,128)(2,1)} all-to-all(bf16[8,256,256]{2,1,0:T(8,128)(2,1)S(1)} %broadcast_in_dim.2), channel_id=1, replica_groups=mesh['row'=8,'z'=8,'xh'=2,'core'=2] {'row'}, dimensions={0} | all-to-all | bytes 2097152 | tf_op jit(solution)/shard_map/all_to_all | solution.py:271
  180.5 6.9 %shard_map.88 = bf16[256,2304]{1,0:T(8,128)(2,1)} custom-call(bf16[8,256,256]{2,1,0:T(8,128)(2,1)} %all_to_all.26.slopes, bf16[256,256]{1,0:T(8,128)(2,1)} %get-tuple-element.32.activated, bf16[2048,2048]{1,0:T(8,128)(2,1)} %bitcast.22), custom_call_target="tpu_custom_call" | custom-call | flops 2147483648 | bytes 10485760 | tf_op jit(solution)/shard_map/pallas_call | solution.py:141
  187.4 39.0 %all_to_all.27 = bf16[32,8,2304]{2,1,0:T(8,128)(2,1)S(1)} all-to-all(bf16[32,8,2304]{2,1,0:T(8,128)(2,1)} %bitcast.26), channel_id=1, replica_groups=mesh['row'=8,'z'=8,'xh'=2,'core'=2] {'z','xh','core'}, dimensions={0} | all-to-all | bytes 2359296 | tf_op jit(solution)/shard_map/all_to_all | solution.py:280
  226.7 0.9 multiply_reduce_fusion
  227.6 1.0 convolution_convert_fusion
  (61 shorter events, 6.1 us)
Async XLA Ops:
  7.2 63.2 %reduce-scatter.2.cloned.1.call-start = ((), (), s32[]{:S(2)}) async-start(), calls=%async_computation.6 | async-start | bytes 2359296 | tf_op jit(solution)/shard_map/reduce_scatter | solution.py:200
  7.2 8.3 %collective-permute-start = (bf16[2048,512]{1,0:T(8,128)(2,1)}, bf16[2048,512]{1,0:T(8,128)(2,1)}, u32[]{:S(2)}, u32[]{:S(2)}) collective-permute-start(bf16[2048,512]{1,0:T(8,128)(2,1)} %here.1), channel_id=1, source_target_pairs={{0,1},{1,0},{2,3},{3,2},{4,5},{5,4},{6,7},{7,6},{8,9},{9,8},{10,11... | collective-permute-start | bytes 6291464 | tf_op jit(solution)/shard_map/ppermute | solution.py:16
  10.5 7.1 %collective-permute-start.1 = (bf16[2048,512]{1,0:T(8,128)(2,1)}, bf16[2048,512]{1,0:T(8,128)(2,1)}, u32[]{:S(2)}, u32[]{:S(2)}) collective-permute-start(bf16[2048,512]{1,0:T(8,128)(2,1)} %weight_here.1), channel_id=1, source_target_pairs={{0,1},{1,0},{2,3},{3,2},{4,5},{5,4},{6,7},{7,6},{8,9},{9,8},{10,11... | collective-permute-start | bytes 6291464 | tf_op jit(solution)/shard_map/ppermute | solution.py:16
  11.6 15.3 %collective-permute-start.3 = (bf16[128,512]{1,0:T(8,128)(2,1)S(1)}, bf16[128,512]{1,0:T(8,128)(2,1)S(1)}, u32[]{:S(2)}, u32[]{:S(2)}) collective-permute-start(bf16[128,512]{1,0:T(8,128)(2,1)S(1)} %get-tuple-element.29), channel_id=1, source_target_pairs={{0,0},{1,2},{2,1},{3,3},{4,44},{5,46},{6,45},{7,47},{8,88},{9,90},... | collective-permute-start | bytes 393224 | tf_op jit(solution)/shard_map/ppermute | solution.py:191
  14.8 12.1 %collective-permute-start.4 = (bf16[128,512]{1,0:T(8,128)(2,1)S(1)}, bf16[128,512]{1,0:T(8,128)(2,1)S(1)}, u32[]{:S(2)}, u32[]{:S(2)}) collective-permute-start(bf16[128,512]{1,0:T(8,128)(2,1)S(1)} %get-tuple-element.28), channel_id=1, source_target_pairs={{0,2},{1,0},{2,3},{3,1},{4,46},{5,44},{6,47},{7,45},{8,90},{9,88},... | collective-permute-start | bytes 393224 | tf_op jit(solution)/shard_map/ppermute | solution.py:191
  26.9 1.2 copy-start.2
  26.9 3.4 %copy-start.3 = (f32[64,2]{0,1:T(2,128)S(1)}, f32[64,2]{0,1:T(2,128)}, u32[]{:S(2)}) copy-start(f32[64,2]{0,1:T(2,128)} %param.11) | copy-start | bytes 1540
  26.9 26.2 %copy-start = (bf16[8,128,512]{2,1,0:T(8,128)(2,1)S(1)}, bf16[8,128,512]{2,1,0:T(8,128)(2,1)}, u32[]{:S(2)}) copy-start(bf16[8,128,512]{2,1,0:T(8,128)(2,1)} %get-tuple-element.15) | copy-start | bytes 3145732
  26.9 26.2 %collective-permute-start.2 = (bf16[8,128,512]{2,1,0:T(8,128)(2,1)}, bf16[8,128,512]{2,1,0:T(8,128)(2,1)S(1)}, u32[]{:S(2)}, u32[]{:S(2)}) collective-permute-start(bf16[8,128,512]{2,1,0:T(8,128)(2,1)} %get-tuple-element.16), channel_id=1, source_target_pairs={{0,2},{2,0},{1,3},{3,1},{4,6},{6,4},{5,7},{7,5},{8,10},{10,8},{9,1... | collective-permute-start | bytes 3145736 | tf_op jit(solution)/shard_map/ppermute | solution.py:16
  28.0 39.9 %collective-permute-start.6 = (s32[64,2]{0,1:T(2,128)S(1)}, s32[64,2]{0,1:T(2,128)S(1)}, u32[]{:S(2)}, u32[]{:S(2)}) collective-permute-start(s32[64,2]{0,1:T(2,128)S(1)} %copy-done.2), channel_id=1, source_target_pairs={{0,1},{1,0},{2,3},{3,2},{4,5},{5,4},{6,7},{7,6},{8,9},{9,8},{10,11... | collective-permute-start | bytes 1544 | tf_op jit(solution)/shard_map/ppermute | solution.py:16
  54.4 40.6 %all-to-all-start = ((bf16[8,128,512]{2,1,0:T(8,128)(2,1)}), bf16[8,128,512]{2,1,0:T(8,128)(2,1)S(1)}, u32[]{:S(2)}, u32[]{:S(2)}) async-start(bf16[8,128,512]{2,1,0:T(8,128)(2,1)} %add_convert_fusion), calls=%async_computation | async-start | bytes 2097152 | tf_op jit(solution)/shard_map/all_to_all | solution.py:239
  67.9 27.2 %dynamic-slice-start = ((f32[2048]{0:T(1024)}, s32[]{:T(128)}), f32[1024]{0:T(1024)S(1)}, s32[]{:S(2)}) async-start(f32[2048]{0:T(1024)} %param.9, s32[]{:T(128)} %select_n.64), calls=%async_computation.7 | async-start | bytes 8704 | tf_op jit(solution)/shard_map/dynamic_slice | solution.py:20
  70.4 24.7 %copy-start.1 = (bf16[256,512]{1,0:T(8,128)(2,1)S(1)}, bf16[256,512]{1,0:T(8,128)(2,1)}, u32[]{:S(2)}) copy-start(bf16[256,512]{1,0:T(8,128)(2,1)} %reduce-scatter.2.cloned.1.call-done) | copy-start | bytes 786436
  71.4 23.6 %collective-permute-start.5 = (bf16[128,512]{1,0:T(8,128)(2,1)S(1)}, bf16[128,512]{1,0:T(8,128)(2,1)S(1)}, u32[]{:S(2)}, u32[]{:S(2)}) collective-permute-start(bf16[128,512]{1,0:T(8,128)(2,1)S(1)} %constant_dynamic-slice_fusion), channel_id=1, source_target_pairs={{0,2},{2,0},{1,3},{3,1},{4,6},{6,4},{5,7},{7,5},{8,10},{10,8},{9,1... | collective-permute-start | bytes 393224 | tf_op jit(solution)/shard_map/ppermute | solution.py:16
  143.0 18.2 %all-to-all-start.2 = ((bf16[8,256,256]{2,1,0:T(8,128)(2,1)}), bf16[8,256,256]{2,1,0:T(8,128)(2,1)S(1)}, u32[]{:S(2)}, u32[]{:S(2)}) async-start(bf16[8,256,256]{2,1,0:T(8,128)(2,1)} %shard_map.87), calls=%async_computation.3 | async-start | bytes 2097152 | tf_op jit(solution)/shard_map/all_to_all | solution.py:264
Sparse Core Ops, SparseCore 0:
  27.1 43.2 reduce-scatter.1

commit v8 on v6

--- a/solution.py
+++ b/solution.py
@@ -20,7 +20,6 @@
     return lax.dynamic_slice_in_dim(values, index * size, size, axis)
 
 
-EARLY = 512
 GRANT = 56 << 20
 CHUNKS, CUTS = 4, 4
 NT = (((1,), (1,)), ((), ()))
@@ -31,51 +30,31 @@
     return lax.dot_general(left, right, NT, preferred_element_type=jnp.float32)
 
 
-def products_kernel(at, here, there, weight_here, weight_there, early, own, other):
-    values = dot_nt(here[...], weight_here[...]) + dot_nt(there[...], weight_there[...])
-    values = values.astype(jnp.bfloat16)
-    first_width = early.shape[1]
-    planes, rows, columns = own.shape
-    early[...] = values[:, :first_width]
-    late = values[:, first_width:].reshape(planes, 2, rows, columns)
-    first = at[1] == 0
-
-    @pl.when(first)
-    def _():
-        own[...] = late[:, 0]
-        other[...] = late[:, 1]
-
-    @pl.when(jnp.logical_not(first))
-    def _():
-        own[...] = late[:, 1]
-        other[...] = late[:, 0]
-
-
-def cross_products(at, features, features_there, weight_here, weight_there):
-    batch, block = features.shape
-    columns = weight_here.shape[0] // 2
-    late = columns - EARLY
-    steps = 4
-    tile = batch // steps
-    planes, half_plane = Z_N // steps, batch // Z_N // 2
-    rows = pl.BlockSpec((tile, block), lambda i, at: (i, 0))
-    weights = pl.BlockSpec((columns, block), lambda i, at: (at[0], 0))
-    late_spec = pl.BlockSpec((planes, half_plane, late), lambda i, at: (i, 0, 0))
-    late_shape = jax.ShapeDtypeStruct((Z_N, half_plane, late), jnp.bfloat16)
+def send_kernel(first, left, right, here, there, bias, chooser, out):
+    block = left.shape[1]
+    swapped = first[0] == 0
+    for index in range(2):
+        columns = slice(index * block, (index + 1) * block)
+        straight, crosswise = (left, right) if index == 0 else (right, left)
+        base = jnp.where(swapped, crosswise[...], straight[...]).astype(jnp.float32)
+        crossed = here[:, columns].astype(jnp.float32) + there[:, columns].astype(jnp.float32)
+        hidden = (base * (crossed + bias[:, columns]) + base).astype(jnp.bfloat16)
+        out[:, columns] = jnp.dot(
+            chooser[...], hidden, preferred_element_type=jnp.float32
+        ).astype(jnp.bfloat16)
+
+
+def send_rows_of(first, left, right, here, there, bias, chooser):
     return pl.pallas_call(
-        products_kernel,
-        grid_spec=pltpu.PrefetchScalarGridSpec(
-            num_scalar_prefetch=1,
-            grid=(steps,),
-            in_specs=[rows, rows, weights, weights],
-            out_specs=[pl.BlockSpec((tile, EARLY), lambda i, at: (i, 0)), late_spec, late_spec],
+        send_kernel,
+        in_specs=[pl.BlockSpec(memory_space=pltpu.SMEM)] + [VMEM] * 6,
+        out_specs=VMEM,
+        out_shape=jax.ShapeDtypeStruct((chooser.shape[0], here.shape[1]), jnp.bfloat16),
+        cost_estimate=pl.CostEstimate(
+            flops=2 * chooser.size * here.shape[1], bytes_accessed=2 << 20, transcendentals=0
         ),
-        out_shape=[jax.ShapeDtypeStruct((batch, EARLY), jnp.bfloat16), late_shape, late_shape],
-        compiler_params=pltpu.CompilerParams(vmem_limit_bytes=GRANT),
-        cost_estimate=pl.CostEstimate(
-            flops=4 * batch * columns * block, bytes_accessed=10 << 20, transcendentals=0
-        ),
-    )(at, features, features_there, weight_here, weight_there)
+        compiler_params=pltpu.CompilerParams(vmem_limit_bytes=24 << 20),
+    )(first, left, right, here, there, bias, chooser)
 
 
 def weight_copies(source, held, semaphores, by_columns):
@@ -177,17 +156,18 @@
     slots = COL_N * CAP
 
     features_there = swap(features, "core")
-    weight_there = swap(cross_weight, "core")
-    at = jnp.stack([core_at, xh_at]).astype(jnp.int32)
-    early, late_own, late_other = cross_products(
-        at, features, features_there, cross_weight, weight_there
-    )
-    part = lax.psum_scatter(early, "z", scatter_dimension=0, tiled=True)
-    late_sum = (
-        late_own.astype(jnp.float32) + swap(late_other, "xh").astype(jnp.float32)
-    ).astype(jnp.bfloat16)
-
-    held_features, late_sum = lax.optimization_barrier((features, late_sum))
+    weight_there = swap(piece(cross_weight, 1 - core_at, half), "core")
+    products = lax.dot_general(
+        features, piece(cross_weight, core_at, half), NT, preferred_element_type=jnp.float32
+    )
+    products = products + lax.dot_general(
+        features_there, weight_there, NT, preferred_element_type=jnp.float32
+    )
+    products, held_features, held_grad = lax.optimization_barrier(
+        (products.astype(jnp.bfloat16), features, mixed_grad)
+    )
+    part = lax.psum_scatter(products, "z", scatter_dimension=0, tiled=True)
+
     plane_there = (3 * z_at + row_at) % Z_N
     pieces = []
     for turn in range(2):
@@ -201,10 +181,6 @@
                         perm.append((src, dst))
         chip_there = plane_there * XH_N + (core_at ^ turn)
         pieces.append(lax.ppermute(piece(held_features, chip_there, 2 * rows), ALL, perm))
-    first = xh_at == 0
-    base = jnp.concatenate(
-        [jnp.where(first, pieces[0], pieces[1]), jnp.where(first, pieces[1], pieces[0])], axis=1
-    ).astype(jnp.float32)
 
     ids_there = swap(expert_ids, "core")
     flat, position = slot_targets(expert_ids)
@@ -226,37 +202,26 @@
         axis=2,
     )
 
-    grad_share = piece(mixed_grad, row_at, share, 1).astype(jnp.float32)
+    grad_share = piece(held_grad, row_at, share, 1).astype(jnp.float32)
     route_grad = (route_gates[:, :, None] * grad_share[:, None, :]).astype(jnp.bfloat16)
     send_grad = jnp.dot(
         table, route_grad.reshape(2 * rows, share), preferred_element_type=jnp.float32
     ).astype(jnp.bfloat16)
-    lanes = share // 2
-    send_grad = send_grad.reshape(COL_N, CAP, share)
-    send_grad = jnp.concatenate([send_grad[:, :, :lanes], send_grad[:, :, lanes:]], axis=1)
-
-    late_parts = lax.all_to_all(late_sum, "z", split_axis=0, concat_axis=0, tiled=True)
+    routed_grad = lax.all_to_all(
+        send_grad.reshape(COL_N, CAP, share), COL, split_axis=0, concat_axis=0, tiled=True
+    ).reshape(slots, share)
+
+    part, pieces, chip_chooser, chooser, table, routed_grad = lax.optimization_barrier(
+        (part, pieces, chip_chooser, chooser, table, routed_grad)
+    )
     part_there = swap(piece(part, 1 - xh_at, 2 * rows), "xh")
-    late_parts, part_there, base, chip_chooser, chooser, table, send_grad = (
-        lax.optimization_barrier(
-            (late_parts, part_there, base, chip_chooser, chooser, table, send_grad)
-        )
-    )
-    crossed_late = jnp.sum(late_parts.astype(jnp.float32), axis=0)
-    crossed_early = piece(part, xh_at, 2 * rows).astype(jnp.float32) + part_there.astype(
-        jnp.float32
-    )
-    crossed = jnp.concatenate([crossed_early, crossed_late], axis=1)
-    bias = piece(cross_bias, core_at, half)
-    hidden = (base * (crossed + bias) + base).astype(jnp.bfloat16)
-    send_rows = jnp.dot(chip_chooser, hidden, preferred_element_type=jnp.float32).astype(
-        jnp.bfloat16
-    )
-    send = jnp.concatenate([send_rows.reshape(COL_N, 2 * CAP, half), send_grad], axis=2)
-    routed = lax.all_to_all(send, COL, split_axis=0, concat_axis=0, tiled=True)
-    grad = routed[:, :, half:]
-    routed_grad = jnp.concatenate([grad[:, :CAP], grad[:, CAP:]], axis=2).reshape(slots, share)
-    routed = routed.reshape(COL_N // 2, 2, 2 * CAP, half + lanes)
+    part_here = piece(part, xh_at, 2 * rows)
+    bias = piece(cross_bias, core_at, half).reshape(1, half)
+    first = (xh_at == 0).astype(jnp.int32).reshape(1)
+    send_rows = send_rows_of(first, *pieces, part_here, part_there, bias, chip_chooser)
+    routed = lax.all_to_all(
+        send_rows.reshape(COL_N, 2 * CAP, half), COL, split_axis=0, concat_axis=0, tiled=True
+    ).reshape(COL_N // 2, 2, 2 * CAP, half)
 
     weight = expert_weight[0]
     pre = expert_call(forward_kernel, (ROWS_N, slots, share), routed, weight)

time: 244 us -> 241 us (0.988)
  matrix products: 1.87 us -> 13.3 us
  waiting for transfers between devices: 57.3 us -> 48.5 us
  Pallas kernels: 22.9 us -> 14.2 us
  blocking collectives: 111 us -> 114 us
    reduce_scatter x1, waiting for transfers between devices: 0.02 us -> 29.4 us  [local(): part = lax.psum_scatter(products, 'z', scatter_dimension=0, tiled=True)]
    ppermute x5 -> x4, waiting for transfers between devices: 28.5 us -> 6.92 us  [swap(): return lax.ppermute(values, axis, [(0, 1), (1, 0)])]
    all_to_all x2 -> x1, waiting for transfers between devices: 27.3 us -> 12.1 us  [local(): lax.all_to_all(send_grad.reshape(COL_N, CAP, share), COL, split_axis=0, c...]
    dot_general x1 -> x2, matrix products: 0.44 us -> 10.4 us  [the longest x1 6.35 us: local(): lax.dot_general(features_there, weight_there, NT, preferred_element_type=...]
    pallas_call x1, Pallas kernels: 9.23 us -> 0.49 us  [send_rows_of(): pl.pallas_call(send_kernel, in_specs=[pl.BlockSpec(memory_space=pltpu.SME...]
    all_to_all x2 -> x1, starting transfers between devices: 10.1 us -> 16.3 us  [local(): lax.all_to_all(send_grad.reshape(COL_N, CAP, share), COL, split_axis=0, c...]
    all_to_all x1, blocking collectives: 40.2 us -> 44 us  [local(): lax.all_to_all(answer.reshape(COL_N, CAP, width + share), COL, split_axis...]
    ppermute x2, starting transfers between devices: 6.12 us -> 3.33 us  [local(): lax.ppermute(piece(held_features, chip_there, 2 * rows), ALL, perm)]
  transfers between devices with their start and end apart: 10 -> 8, of which waited for: 6 -> 3; matrix products, arithmetic and copies ran while one was open for 3% -> 4% of each run, Pallas kernels for 0% -> 0%
where the time goes in v8:
time: 241 us; the launch traced here: 240 us
  blocking collectives  114 us (47%)
  waiting for transfers between devices  48.5 us (20%)
  starting transfers between devices  26.2 us (11%)
  between operations  14.3 us (6%)
  Pallas kernels  14.2 us (6%)
  matrix products  13.3 us (6%)
  other arithmetic  5.1 us (2%)
  local copies, waits for them, and re-layouts  4.68 us (2%)
    all_to_all x1, blocking collectives, local(): lax.all_to_all(answer.reshape(COL_N, CAP, width + share), COL, split_axis...  44 us
    all_to_all x1, blocking collectives, local(): lax.all_to_all(send_rows.reshape(COL_N, 2 * CAP, half), COL, split_axis=0...  35.9 us
    reduce_scatter x1, waiting for transfers between devices, local(): part = lax.psum_scatter(products, 'z', scatter_dimension=0, tiled=True)  29.4 us
    all_to_all x1, blocking collectives, local(): parts = lax.all_to_all(pre, 'row', split_axis=0, concat_axis=0, tiled=True)  17.6 us
    all_to_all x1, starting transfers between devices, local(): lax.all_to_all(send_grad.reshape(COL_N, CAP, share), COL, split_axis=0, c...  16.3 us
    all_to_all x1, blocking collectives, local(): lax.all_to_all(jnp.broadcast_to(slope[None], (ROWS_N, slots, share)), 'ro...  16.1 us
    pallas_call x2, Pallas kernels, expert_call(): pl.pallas_call(kernel, in_specs=[VMEM] * (len(operands) - 1) + [pl.BlockS...  13.7 us
    all_to_all x1, waiting for transfers between devices, local(): lax.all_to_all(send_grad.reshape(COL_N, CAP, share), COL, split_axis=0, c...  12.1 us
  transfers between devices with their start and end apart: 8, of which 3 were waited for; matrix products, arithmetic and copies ran while one was open for 4% of the time, Pallas kernels for 0%

profile of v8, /device:TPU:1, one launch (start us, length us, event | category | flops | bytes accessed | tf_op | source)
XLA Modules:
  0.0 239.8 jit_solution(11910828331377491502)
XLA Ops:
  7.2 3.3 %collective-permute-start.1 = (bf16[2048,512]{1,0:T(8,128)(2,1)}, bf16[2048,512]{1,0:T(8,128)(2,1)}, u32[]{:S(2)}, u32[]{:S(2)}) collective-permute-start(bf16[2048,512]{1,0:T(8,128)(2,1)} %param.7), channel_id=1, source_target_pairs={{0,1},{1,0},{2,3},{3,2},{4,5},{5,4},{6,7},{7,6},{8,9},{9,8},{10,11... | collective-permute-start | bytes 6291464 | tf_op jit(solution)/shard_map/ppermute | solution.py:16
  10.6 1.5 collective-permute-start
  12.2 4.1 %fusion.3 = f32[1024,2048]{0,1:T(8,128)S(1)} fusion(bf16[2048,512]{1,0:T(8,128)(2,1)} %param.7, bf16[2048,512]{1,0:T(8,128)(2,1)S(1)} %copy-done, s32[]{:T(128)S(6)} %select_n.44), kind=kOutput, calls=%fused_computation.7 | convolution fusion | flops 2147483648 | bytes 11534340 | tf_op jit(solution)/shard_map/dot_general | solution.py:160
  16.3 6.3 %fusion = bf16[2048,1024]{1,0:T(8,128)(2,1)} fusion(f32[1024,2048]{0,1:T(8,128)S(1)} %fusion.3, bf16[1024,512]{1,0:T(8,128)(2,1)} %collective-permute-done, bf16[2048,512]{1,0:T(8,128)(2,1)} %collective-permute-done.1), kind=kOutput, calls=%fused_computation.1 | convolution fusion | flops 2151677952 | bytes 15728640 | tf_op jit(solution)/shard_map/dot_general | solution.py:163
  24.3 0.7 fusion.11
  26.5 1.0 constant_dynamic-slice_fusion.2
  27.6 3.2 %collective-permute-start.2 = (bf16[128,512]{1,0:T(8,128)(2,1)S(1)}, bf16[128,512]{1,0:T(8,128)(2,1)S(1)}, u32[]{:S(2)}, u32[]{:S(2)}) collective-permute-start(bf16[128,512]{1,0:T(8,128)(2,1)S(1)} %get-tuple-element.23), channel_id=1, source_target_pairs={{0,0},{1,2},{2,1},{3,3},{4,44},{5,46},{6,45},{7,47},{8,88},{9,90},... | collective-permute-start | bytes 393224 | tf_op jit(solution)/shard_map/ppermute | solution.py:183
  30.9 0.8 dynamic-slice_convert_fusion
  31.8 0.9 fusion.1
  32.7 16.3 %all-to-all-start = ((bf16[32,8,256]{2,1,0:T(8,128)(2,1)}), bf16[32,8,256]{2,1,0:T(8,128)(2,1)S(1)}, u32[]{:S(2)}, u32[]{:S(2)}) async-start(bf16[32,8,256]{2,1,0:T(8,128)(2,1)} %fusion.1), calls=%async_computation.1 | async-start | bytes 262144 | tf_op jit(solution)/shard_map/all_to_all | solution.py:210
  49.4 12.1 %all-to-all-done = bf16[32,8,256]{2,1,0:T(8,128)(2,1)S(1)} async-done(((bf16[32,8,256]{2,1,0:T(8,128)(2,1)}), bf16[32,8,256]{2,1,0:T(8,128)(2,1)S(1)}, u32[]{:S(2)}, u32[]{:S(2)}) %all-to-all-start) | async-done | bytes 131104 | tf_op jit(solution)/shard_map/all_to_all | solution.py:210
  61.5 29.4 %reduce-scatter.2.cloned.1.call-done = bf16[256,1024]{1,0:T(8,128)(2,1)} async-done(((bf16[2048,1024]{1,0:T(8,128)(2,1)}), bf16[256,1024]{1,0:T(8,128)(2,1)}) %reduce-scatter.2.cloned.1.call-update) | async-done | bytes 524304 | tf_op jit(solution)/shard_map/reduce_scatter | solution.py:169
  90.9 1.1 constant_dynamic-slice_fusion
  92.0 1.6 collective-permute-start.5
  93.6 6.9 %collective-permute-done.5.there = bf16[128,1024]{1,0:T(8,128)(2,1)S(1)} collective-permute-done((bf16[128,1024]{1,0:T(8,128)(2,1)S(1)}, bf16[128,1024]{1,0:T(8,128)(2,1)S(1)}, u32[]{:S(2)}, u32[]{:S(2)}) %collective-permute-start.5) | collective-permute-done | bytes 262176 | tf_op jit(solution)/shard_map/ppermute | solution.py:16
  101.0 35.9 %all_to_all.25 = bf16[32,16,1024]{2,1,0:T(8,128)(2,1)} all-to-all(bf16[32,16,1024]{2,1,0:T(8,128)(2,1)S(1)} %bitcast.21), channel_id=1, replica_groups=mesh['row'=8,'z'=8,'xh'=2,'core'=2] {'z','xh','core'}, dimensions={0} | all-to-all | bytes 2097152 | tf_op jit(solution)/shard_map/all_to_all | solution.py:222
  136.9 6.8 %shard_map.87 = bf16[8,256,256]{2,1,0:T(8,128)(2,1)} custom-call(bf16[16,2,16,1024]{3,2,1,0:T(8,128)(2,1)} %bitcast.28, bf16[2048,2048]{1,0:T(8,128)(2,1)} %bitcast.23), custom_call_target="tpu_custom_call" | custom-call | flops 2147483648 | bytes 10485760 | tf_op jit(solution)/shard_map/pallas_call | solution.py:120
  143.7 17.6 %all_to_all.26 = bf16[8,256,256]{2,1,0:T(8,128)(2,1)S(1)} all-to-all(bf16[8,256,256]{2,1,0:T(8,128)(2,1)} %shard_map.87), channel_id=1, replica_groups=mesh['row'=8,'z'=8,'xh'=2,'core'=2] {'row'}, dimensions={0} | all-to-all | bytes 2097152 | tf_op jit(solution)/shard_map/all_to_all | solution.py:228
  161.4 0.8 multiply_convert_fusion
  162.3 16.1 %all_to_all.27.slopes = bf16[8,256,256]{2,1,0:T(8,128)(2,1)} all-to-all(bf16[8,256,256]{2,1,0:T(8,128)(2,1)S(1)} %broadcast_in_dim.2), channel_id=1, replica_groups=mesh['row'=8,'z'=8,'xh'=2,'core'=2] {'row'}, dimensions={0} | all-to-all | bytes 2097152 | tf_op jit(solution)/shard_map/all_to_all | solution.py:235
  178.4 6.9 %shard_map.88 = bf16[256,2304]{1,0:T(8,128)(2,1)} custom-call(bf16[8,256,256]{2,1,0:T(8,128)(2,1)} %all_to_all.27.slopes, bf16[256,256]{1,0:T(8,128)(2,1)} %get-tuple-element.26.activated, bf16[2048,2048]{1,0:T(8,128)(2,1)} %bitcast.24), custom_call_target="tpu_custom_call" | custom-call | flops 2147483648 | bytes 10485760 | tf_op jit(solution)/shard_map/pallas_call | solution.py:120
  185.3 44.0 %all_to_all.28 = bf16[32,8,2304]{2,1,0:T(8,128)(2,1)S(1)} all-to-all(bf16[32,8,2304]{2,1,0:T(8,128)(2,1)} %bitcast.27), channel_id=1, replica_groups=mesh['row'=8,'z'=8,'xh'=2,'core'=2] {'z','xh','core'}, dimensions={0} | all-to-all | bytes 2359296 | tf_op jit(solution)/shard_map/all_to_all | solution.py:244
  229.5 1.6 multiply_reduce_fusion
  231.2 1.8 convolution_convert_fusion
  (54 shorter events, 4.8 us)
Async XLA Ops:
  7.2 3.4 %copy-start = (bf16[2048,512]{1,0:T(8,128)(2,1)S(1)}, bf16[2048,512]{1,0:T(8,128)(2,1)}, u32[]{:S(2)}) copy-start(bf16[2048,512]{1,0:T(8,128)(2,1)} %param.8) | copy-start | bytes 6291460
  7.2 83.8 %reduce-scatter.2.cloned.1.call-start = ((), (), s32[]{:S(2)}) async-start(), calls=%async_computation.6 | async-start | bytes 4718592 | tf_op jit(solution)/shard_map/reduce_scatter | solution.py:169
  7.2 9.0 %collective-permute-start.1 = (bf16[2048,512]{1,0:T(8,128)(2,1)}, bf16[2048,512]{1,0:T(8,128)(2,1)}, u32[]{:S(2)}, u32[]{:S(2)}) collective-permute-start(bf16[2048,512]{1,0:T(8,128)(2,1)} %param.7), channel_id=1, source_target_pairs={{0,1},{1,0},{2,3},{3,2},{4,5},{5,4},{6,7},{7,6},{8,9},{9,8},{10,11... | collective-permute-start | bytes 6291464 | tf_op jit(solution)/shard_map/ppermute | solution.py:16
  10.6 5.6 %collective-permute-start = (bf16[1024,512]{1,0:T(8,128)(2,1)S(1)}, bf16[1024,512]{1,0:T(8,128)(2,1)}, u32[]{:S(2)}, u32[]{:S(2)}) collective-permute-start(bf16[1024,512]{1,0:T(8,128)(2,1)S(1)} %constant_dynamic-slice_fusion.4), channel_id=1, source_target_pairs={{0,1},{1,0},{2,3},{3,2},{4,5},{5,4},{6,7},{7,6},{8,9},{9,8},{10,11... | collective-permute-start | bytes 3145736 | tf_op jit(solution)/shard_map/ppermute | solution.py:16
  22.6 0.7 copy-start.3
  22.6 3.0 %copy-start.5 = (f32[64,2]{0,1:T(2,128)S(1)}, f32[64,2]{0,1:T(2,128)}, u32[]{:S(2)}) copy-start(f32[64,2]{0,1:T(2,128)} %param.11) | copy-start | bytes 1540
  23.3 70.3 %copy-start.4 = (f32[2048]{0:T(1024)S(1)}, f32[2048]{0:T(1024)}, u32[]{:S(2)}) copy-start(f32[2048]{0:T(1024)} %param.9) | copy-start | bytes 24580
  23.3 2.6 %collective-permute-start.4 = (s32[64,2]{0,1:T(2,128)S(1)}, s32[64,2]{0,1:T(2,128)S(1)}, u32[]{:S(2)}, u32[]{:S(2)}) collective-permute-start(s32[64,2]{0,1:T(2,128)S(1)} %copy-done.3), channel_id=1, source_target_pairs={{0,1},{1,0},{2,3},{3,2},{4,5},{5,4},{6,7},{7,6},{8,9},{9,8},{10,11... | collective-permute-start | bytes 1544 | tf_op jit(solution)/shard_map/ppermute | solution.py:16
  25.7 1.8 copy-start.1
  27.6 21.8 %collective-permute-start.2 = (bf16[128,512]{1,0:T(8,128)(2,1)S(1)}, bf16[128,512]{1,0:T(8,128)(2,1)S(1)}, u32[]{:S(2)}, u32[]{:S(2)}) collective-permute-start(bf16[128,512]{1,0:T(8,128)(2,1)S(1)} %get-tuple-element.23), channel_id=1, source_target_pairs={{0,0},{1,2},{2,1},{3,3},{4,44},{5,46},{6,45},{7,47},{8,88},{9,90},... | collective-permute-start | bytes 393224 | tf_op jit(solution)/shard_map/ppermute | solution.py:183
  30.8 18.6 %collective-permute-start.3 = (bf16[128,512]{1,0:T(8,128)(2,1)S(1)}, bf16[128,512]{1,0:T(8,128)(2,1)S(1)}, u32[]{:S(2)}, u32[]{:S(2)}) collective-permute-start(bf16[128,512]{1,0:T(8,128)(2,1)S(1)} %get-tuple-element.22), channel_id=1, source_target_pairs={{0,2},{1,0},{2,3},{3,1},{4,46},{5,44},{6,47},{7,45},{8,90},{9,88},... | collective-permute-start | bytes 393224 | tf_op jit(solution)/shard_map/ppermute | solution.py:183
  32.7 28.8 %all-to-all-start = ((bf16[32,8,256]{2,1,0:T(8,128)(2,1)}), bf16[32,8,256]{2,1,0:T(8,128)(2,1)S(1)}, u32[]{:S(2)}, u32[]{:S(2)}) async-start(bf16[32,8,256]{2,1,0:T(8,128)(2,1)} %fusion.1), calls=%async_computation.1 | async-start | bytes 262144 | tf_op jit(solution)/shard_map/all_to_all | solution.py:210
  92.0 8.5 %collective-permute-start.5 = (bf16[128,1024]{1,0:T(8,128)(2,1)S(1)}, bf16[128,1024]{1,0:T(8,128)(2,1)S(1)}, u32[]{:S(2)}, u32[]{:S(2)}) collective-permute-start(bf16[128,1024]{1,0:T(8,128)(2,1)S(1)} %get-tuple-element.24), channel_id=1, source_target_pairs={{0,2},{2,0},{1,3},{3,1},{4,6},{6,4},{5,7},{7,5},{8,10},{10,8},{9,1... | collective-permute-start | bytes 786440 | tf_op jit(solution)/shard_map/ppermute | solution.py:16
  185.3 44.0 %copy-start.2 = (bf16[256,128]{1,0:T(8,128)(2,1)S(1)}, bf16[256,128]{1,0:T(8,128)(2,1)}, u32[]{:S(2)}) copy-start(bf16[256,128]{1,0:T(8,128)(2,1)} %fusion.9) | copy-start | bytes 196612
Sparse Core Ops, SparseCore 0:
  22.8 68.1 reduce-scatter.1

commit v9 on v6

--- a/solution.py
+++ b/solution.py
@@ -20,7 +20,7 @@
     return lax.dynamic_slice_in_dim(values, index * size, size, axis)
 
 
-EARLY = 512
+EARLY = 768
 GRANT = 56 << 20
 CHUNKS, CUTS = 4, 4
 NT = (((1,), (1,)), ((), ()))
@@ -78,6 +78,37 @@
     )(at, features, features_there, weight_here, weight_there)
 
 
+def send_kernel(first, left, right, here, there, late, bias, chooser, grad, out):
+    block = left.shape[1]
+    swapped = first[0] == 0
+    late_sum = jnp.sum(late[...].astype(jnp.float32), axis=0)
+    early_sum = here[...].astype(jnp.float32) + there[...].astype(jnp.float32)
+    crossed = jnp.concatenate([early_sum, late_sum], axis=1) + bias[...]
+    experts, amount, _ = out.shape
+    for index in range(2):
+        columns = slice(index * block, (index + 1) * block)
+        straight, crosswise = (left, right) if index == 0 else (right, left)
+        base = jnp.where(swapped, crosswise[...], straight[...]).astype(jnp.float32)
+        hidden = (base * crossed[:, columns] + base).astype(jnp.bfloat16)
+        chosen = jnp.dot(chooser[...], hidden, preferred_element_type=jnp.float32)
+        out[:, :, columns] = chosen.astype(jnp.bfloat16).reshape(experts, amount, block)
+    out[:, :, 2 * block :] = grad[...]
+
+
+def send_rows_of(first, left, right, here, there, late, bias, chooser, grad):
+    width = bias.shape[1] + grad.shape[2]
+    return pl.pallas_call(
+        send_kernel,
+        in_specs=[pl.BlockSpec(memory_space=pltpu.SMEM)] + [VMEM] * 8,
+        out_specs=VMEM,
+        out_shape=jax.ShapeDtypeStruct(grad.shape[:2] + (width,), jnp.bfloat16),
+        cost_estimate=pl.CostEstimate(
+            flops=2 * chooser.size * bias.size, bytes_accessed=2 << 20, transcendentals=0
+        ),
+        compiler_params=pltpu.CompilerParams(vmem_limit_bytes=24 << 20),
+    )(first, left, right, here, there, late, bias, chooser, grad)
+
+
 def weight_copies(source, held, semaphores, by_columns):
     rows, columns = source.shape
     copies = []
@@ -182,12 +213,12 @@
     early, late_own, late_other = cross_products(
         at, features, features_there, cross_weight, weight_there
     )
+    early, held_features = lax.optimization_barrier((early, features))
     part = lax.psum_scatter(early, "z", scatter_dimension=0, tiled=True)
     late_sum = (
         late_own.astype(jnp.float32) + swap(late_other, "xh").astype(jnp.float32)
     ).astype(jnp.bfloat16)
 
-    held_features, late_sum = lax.optimization_barrier((features, late_sum))
     plane_there = (3 * z_at + row_at) % Z_N
     pieces = []
     for turn in range(2):
@@ -201,10 +232,6 @@
                         perm.append((src, dst))
         chip_there = plane_there * XH_N + (core_at ^ turn)
         pieces.append(lax.ppermute(piece(held_features, chip_there, 2 * rows), ALL, perm))
-    first = xh_at == 0
-    base = jnp.concatenate(
-        [jnp.where(first, pieces[0], pieces[1]), jnp.where(first, pieces[1], pieces[0])], axis=1
-    ).astype(jnp.float32)
 
     ids_there = swap(expert_ids, "core")
     flat, position = slot_targets(expert_ids)
@@ -235,24 +262,20 @@
     send_grad = send_grad.reshape(COL_N, CAP, share)
     send_grad = jnp.concatenate([send_grad[:, :, :lanes], send_grad[:, :, lanes:]], axis=1)
 
+    late_sum, pieces = lax.optimization_barrier((late_sum, pieces))
     late_parts = lax.all_to_all(late_sum, "z", split_axis=0, concat_axis=0, tiled=True)
     part_there = swap(piece(part, 1 - xh_at, 2 * rows), "xh")
-    late_parts, part_there, base, chip_chooser, chooser, table, send_grad = (
+    late_parts, part_there, pieces, chip_chooser, chooser, table, send_grad = (
         lax.optimization_barrier(
-            (late_parts, part_there, base, chip_chooser, chooser, table, send_grad)
+            (late_parts, part_there, pieces, chip_chooser, chooser, table, send_grad)
         )
     )
-    crossed_late = jnp.sum(late_parts.astype(jnp.float32), axis=0)
-    crossed_early = piece(part, xh_at, 2 * rows).astype(jnp.float32) + part_there.astype(
-        jnp.float32
-    )
-    crossed = jnp.concatenate([crossed_early, crossed_late], axis=1)
-    bias = piece(cross_bias, core_at, half)
-    hidden = (base * (crossed + bias) + base).astype(jnp.bfloat16)
-    send_rows = jnp.dot(chip_chooser, hidden, preferred_element_type=jnp.float32).astype(
-        jnp.bfloat16
-    )
-    send = jnp.concatenate([send_rows.reshape(COL_N, 2 * CAP, half), send_grad], axis=2)
+    part_here = piece(part, xh_at, 2 * rows)
+    bias = piece(cross_bias, core_at, half).reshape(1, half)
+    first = (xh_at == 0).astype(jnp.int32).reshape(1)
+    send = send_rows_of(
+        first, *pieces, part_here, part_there, late_parts, bias, chip_chooser, send_grad
+    )
     routed = lax.all_to_all(send, COL, split_axis=0, concat_axis=0, tiled=True)
     grad = routed[:, :, half:]
     routed_grad = jnp.concatenate([grad[:, :CAP], grad[:, CAP:]], axis=2).reshape(slots, share)

time: 244 us -> 244 us (level)
  blocking collectives: 111 us -> 97.3 us
  waiting for transfers between devices: 57.3 us -> 65.9 us
  starting transfers between devices: 24.4 us -> 30.6 us
    reduce_scatter x1, waiting for transfers between devices: 0.02 us -> 30.1 us  [local(): part = lax.psum_scatter(early, 'z', scatter_dimension=0, tiled=True)]
    all_to_all x1, waiting for transfers between devices: 13.7 us -> 0.01 us  [local(): lax.all_to_all(late_sum, 'z', split_axis=0, concat_axis=0, tiled=True)]
    all_to_all x1, blocking collectives: 53.3 us -> 39.7 us  [local(): routed = lax.all_to_all(send, COL, split_axis=0, concat_axis=0, tiled=True)]
    all_to_all x1, starting transfers between devices: 6.45 us -> 16 us  [local(): lax.all_to_all(late_sum, 'z', split_axis=0, concat_axis=0, tiled=True)]
    ppermute x5, waiting for transfers between devices: 28.5 us -> 20 us  [swap(): return lax.ppermute(values, axis, [(0, 1), (1, 0)])]
  transfers between devices with their start and end apart: 10 -> 10, of which waited for: 6 -> 7; matrix products, arithmetic and copies ran while one was open for 3% -> 3% of each run, Pallas kernels for 0% -> 0%
where the time goes in v9:
time: 244 us; the launch traced here: 243 us
  blocking collectives  97.3 us (40%)
  waiting for transfers between devices  65.9 us (27%)
  starting transfers between devices  30.6 us (13%)
  Pallas kernels  23.3 us (10%)
  between operations  14.3 us (6%)
  local copies, waits for them, and re-layouts  5.66 us (2%)
  other arithmetic  4.71 us (2%)
    all_to_all x1, blocking collectives, local(): routed = lax.all_to_all(send, COL, split_axis=0, concat_axis=0, tiled=True)  39.7 us
    all_to_all x1, blocking collectives, local(): lax.all_to_all(answer.reshape(COL_N, CAP, width + share), COL, split_axis...  39.2 us
    reduce_scatter x1, waiting for transfers between devices, local(): part = lax.psum_scatter(early, 'z', scatter_dimension=0, tiled=True)  30.1 us
    ppermute x5, waiting for transfers between devices, swap(): return lax.ppermute(values, axis, [(0, 1), (1, 0)])  20 us
    all_to_all x1, blocking collectives, local(): lax.all_to_all(jnp.broadcast_to(slope[None], (ROWS_N, slots, share)), 'ro...  18.4 us
    all_to_all x1, starting transfers between devices, local(): lax.all_to_all(late_sum, 'z', split_axis=0, concat_axis=0, tiled=True)  16 us
    pallas_call x2, Pallas kernels, expert_call(): pl.pallas_call(kernel, in_specs=[VMEM] * (len(operands) - 1) + [pl.BlockS...  13.7 us
    all_to_all x1, waiting for transfers between devices, local(): parts = lax.all_to_all(pre, 'row', split_axis=0, concat_axis=0, tiled=True)  13.6 us
  transfers between devices with their start and end apart: 10, of which 7 were waited for; matrix products, arithmetic and copies ran while one was open for 3% of the time, Pallas kernels for 0%

profile of v9, /device:TPU:1, one launch (start us, length us, event | category | flops | bytes accessed | tf_op | source)
XLA Modules:
  0.0 243.2 jit_solution(2724601594564995095)
XLA Ops:
  7.2 3.3 %collective-permute-start = (bf16[2048,512]{1,0:T(8,128)(2,1)}, bf16[2048,512]{1,0:T(8,128)(2,1)S(1)}, u32[]{:S(2)}, u32[]{:S(2)}) collective-permute-start(bf16[2048,512]{1,0:T(8,128)(2,1)} %here.1), channel_id=1, source_target_pairs={{0,1},{1,0},{2,3},{3,2},{4,5},{5,4},{6,7},{7,6},{8,9},{9,8},{10,11... | collective-permute-start | bytes 6291464 | tf_op jit(solution)/shard_map/ppermute | solution.py:16
  11.3 5.2 %collective-permute-done.there = bf16[2048,512]{1,0:T(8,128)(2,1)S(1)} collective-permute-done((bf16[2048,512]{1,0:T(8,128)(2,1)}, bf16[2048,512]{1,0:T(8,128)(2,1)S(1)}, u32[]{:S(2)}, u32[]{:S(2)}) %collective-permute-start) | collective-permute-done | bytes 2097184 | tf_op jit(solution)/shard_map/ppermute | solution.py:16
  16.5 1.2 collective-permute-done.1.weight_there
  17.9 9.2 %shard_map.86 = (bf16[2048,768]{1,0:T(8,128)(2,1)}, bf16[8,128,256]{2,1,0:T(8,128)(2,1)}, bf16[8,128,256]{2,1,0:T(8,128)(2,1)}) custom-call(s32[2]{0:T(128)} %pad_add_fusion.at, bf16[2048,512]{1,0:T(8,128)(2,1)} %here.1, bf16[2048,512]{1,0:T(8,128)(2,1)} %copy-done.4, bf16[2048,512]{1,0:T(8,128)(2,1)} %weight_here.1, ...), custom_call_target="tpu_custom_call" | custom-call | flops 4294967296 | bytes 10485760 | tf_op jit(solution)/shard_map/pallas_call | solution.py:65
  30.2 1.1 collective-permute-start.2
  31.3 1.0 constant_dynamic-slice_fusion.2
  32.3 4.2 %collective-permute-start.3 = (bf16[128,512]{1,0:T(8,128)(2,1)S(1)}, bf16[128,512]{1,0:T(8,128)(2,1)S(1)}, u32[]{:S(2)}, u32[]{:S(2)}) collective-permute-start(bf16[128,512]{1,0:T(8,128)(2,1)S(1)} %get-tuple-element.35), channel_id=1, source_target_pairs={{0,0},{1,2},{2,1},{3,3},{4,44},{5,46},{6,45},{7,47},{8,88},{9,90},... | collective-permute-start | bytes 393224 | tf_op jit(solution)/shard_map/ppermute | solution.py:234
  36.6 8.6 %collective-permute-done.2 = bf16[8,128,256]{2,1,0:T(8,128)(2,1)S(1)} collective-permute-done((bf16[8,128,256]{2,1,0:T(8,128)(2,1)S(1)}, bf16[8,128,256]{2,1,0:T(8,128)(2,1)S(1)}, u32[]{:S(2)}, u32[]{:S(2)}) %collective-permute-start.2) | collective-permute-done | bytes 524320 | tf_op jit(solution)/shard_map/ppermute | solution.py:16
  45.2 0.9 add_convert_fusion
  46.1 2.2 collective-permute-done.3.left
  48.3 16.0 %all-to-all-start = ((bf16[8,128,256]{2,1,0:T(8,128)(2,1)}), bf16[8,128,256]{2,1,0:T(8,128)(2,1)S(1)}, u32[]{:S(2)}, u32[]{:S(2)}) async-start(bf16[8,128,256]{2,1,0:T(8,128)(2,1)} %add_convert_fusion), calls=%async_computation | async-start | bytes 1048576 | tf_op jit(solution)/shard_map/all_to_all | solution.py:266
  65.3 30.1 %reduce-scatter.2.cloned.1.call-done = bf16[256,768]{1,0:T(8,128)(2,1)} async-done(((bf16[2048,768]{1,0:T(8,128)(2,1)}), bf16[256,768]{1,0:T(8,128)(2,1)}) %reduce-scatter.2.cloned.1.call-update) | async-done | bytes 393232 | tf_op jit(solution)/shard_map/reduce_scatter | solution.py:217
  95.5 1.0 constant_dynamic-slice_fusion
  96.5 1.7 collective-permute-start.5
  98.5 5.0 %collective-permute-done.5.there = bf16[128,768]{1,0:T(8,128)(2,1)S(1)} collective-permute-done((bf16[128,768]{1,0:T(8,128)(2,1)S(1)}, bf16[128,768]{1,0:T(8,128)(2,1)S(1)}, u32[]{:S(2)}, u32[]{:S(2)}) %collective-permute-start.5) | collective-permute-done | bytes 196640 | tf_op jit(solution)/shard_map/ppermute | solution.py:16
  104.1 39.7 %all_to_all.25 = bf16[32,16,1152]{2,1,0:T(8,128)(2,1)} all-to-all(bf16[32,16,1152]{2,1,0:T(8,128)(2,1)S(1)} %shard_map.87), channel_id=1, replica_groups=mesh['row'=8,'z'=8,'xh'=2,'core'=2] {'z','xh','core'}, dimensions={0} | all-to-all | bytes 2359296 | tf_op jit(solution)/shard_map/all_to_all | solution.py:279
  143.8 6.8 %shard_map.88 = bf16[8,256,256]{2,1,0:T(8,128)(2,1)} custom-call(bf16[16,2,16,1152]{3,2,1,0:T(8,128)(2,1)} %bitcast.24, bf16[2048,2048]{1,0:T(8,128)(2,1)} %bitcast.22), custom_call_target="tpu_custom_call" | custom-call | flops 2147483648 | bytes 10485760 | tf_op jit(solution)/shard_map/pallas_call | solution.py:172
  150.6 3.7 %all-to-all-start.2 = ((bf16[8,256,256]{2,1,0:T(8,128)(2,1)}), bf16[8,256,256]{2,1,0:T(8,128)(2,1)S(1)}, u32[]{:S(2)}, u32[]{:S(2)}) async-start(bf16[8,256,256]{2,1,0:T(8,128)(2,1)} %shard_map.88), calls=%async_computation.3 | async-start | bytes 2097152 | tf_op jit(solution)/shard_map/all_to_all | solution.py:286
  154.3 0.9 fusion.15
  155.2 13.6 %all-to-all-done.2 = bf16[8,256,256]{2,1,0:T(8,128)(2,1)S(1)} async-done(((bf16[8,256,256]{2,1,0:T(8,128)(2,1)}), bf16[8,256,256]{2,1,0:T(8,128)(2,1)S(1)}, u32[]{:S(2)}, u32[]{:S(2)}) %all-to-all-start.2) | async-done | bytes 1048608 | tf_op jit(solution)/shard_map/all_to_all | solution.py:286
  169.8 18.4 %all_to_all.26.slopes = bf16[8,256,256]{2,1,0:T(8,128)(2,1)} all-to-all(bf16[8,256,256]{2,1,0:T(8,128)(2,1)S(1)} %broadcast_in_dim.2), channel_id=1, replica_groups=mesh['row'=8,'z'=8,'xh'=2,'core'=2] {'row'}, dimensions={0} | all-to-all | bytes 2097152 | tf_op jit(solution)/shard_map/all_to_all | solution.py:293
  188.2 6.9 %shard_map.89 = bf16[256,2304]{1,0:T(8,128)(2,1)} custom-call(bf16[8,256,256]{2,1,0:T(8,128)(2,1)} %all_to_all.26.slopes, bf16[256,256]{1,0:T(8,128)(2,1)} %get-tuple-element.40.activated, bf16[2048,2048]{1,0:T(8,128)(2,1)} %bitcast.23), custom_call_target="tpu_custom_call" | custom-call | flops 2147483648 | bytes 10485760 | tf_op jit(solution)/shard_map/pallas_call | solution.py:172
  195.1 39.2 %all_to_all.27 = bf16[32,8,2304]{2,1,0:T(8,128)(2,1)S(1)} all-to-all(bf16[32,8,2304]{2,1,0:T(8,128)(2,1)} %bitcast.27), channel_id=1, replica_groups=mesh['row'=8,'z'=8,'xh'=2,'core'=2] {'z','xh','core'}, dimensions={0} | all-to-all | bytes 2359296 | tf_op jit(solution)/shard_map/all_to_all | solution.py:302
  235.4 1.0 convolution_convert_fusion
  (59 shorter events, 8.1 us)
Async XLA Ops:
  7.2 88.3 %reduce-scatter.2.cloned.1.call-start = ((), (), s32[]{:S(2)}) async-start(), calls=%async_computation.6 | async-start | bytes 3538944 | tf_op jit(solution)/shard_map/reduce_scatter | solution.py:217
  7.2 9.3 %collective-permute-start = (bf16[2048,512]{1,0:T(8,128)(2,1)}, bf16[2048,512]{1,0:T(8,128)(2,1)S(1)}, u32[]{:S(2)}, u32[]{:S(2)}) collective-permute-start(bf16[2048,512]{1,0:T(8,128)(2,1)} %here.1), channel_id=1, source_target_pairs={{0,1},{1,0},{2,3},{3,2},{4,5},{5,4},{6,7},{7,6},{8,9},{9,8},{10,11... | collective-permute-start | bytes 6291464 | tf_op jit(solution)/shard_map/ppermute | solution.py:16
  10.5 7.1 %collective-permute-start.1 = (bf16[2048,512]{1,0:T(8,128)(2,1)}, bf16[2048,512]{1,0:T(8,128)(2,1)}, u32[]{:S(2)}, u32[]{:S(2)}) collective-permute-start(bf16[2048,512]{1,0:T(8,128)(2,1)} %weight_here.1), channel_id=1, source_target_pairs={{0,1},{1,0},{2,3},{3,2},{4,5},{5,4},{6,7},{7,6},{8,9},{9,8},{10,11... | collective-permute-start | bytes 6291464 | tf_op jit(solution)/shard_map/ppermute | solution.py:16
  16.5 1.3 copy-start.4
  27.0 0.7 copy-start.1
  27.0 2.6 %copy-start.3 = (f32[64,2]{0,1:T(2,128)S(1)}, f32[64,2]{0,1:T(2,128)}, u32[]{:S(2)}) copy-start(f32[64,2]{0,1:T(2,128)} %param.11) | copy-start | bytes 1540
  27.7 2.5 %copy-start.5 = (bf16[8,128,256]{2,1,0:T(8,128)(2,1)S(1)}, bf16[8,128,256]{2,1,0:T(8,128)(2,1)}, u32[]{:S(2)}) copy-start(bf16[8,128,256]{2,1,0:T(8,128)(2,1)} %get-tuple-element.19) | copy-start | bytes 1572868
  27.7 17.5 %copy-start = (bf16[8,128,256]{2,1,0:T(8,128)(2,1)S(1)}, bf16[8,128,256]{2,1,0:T(8,128)(2,1)}, u32[]{:S(2)}) copy-start(bf16[8,128,256]{2,1,0:T(8,128)(2,1)} %get-tuple-element.18) | copy-start | bytes 1572868
  27.7 37.0 %collective-permute-start.6 = (s32[64,2]{0,1:T(2,128)S(1)}, s32[64,2]{0,1:T(2,128)S(1)}, u32[]{:S(2)}, u32[]{:S(2)}) collective-permute-start(s32[64,2]{0,1:T(2,128)S(1)} %copy-done.1), channel_id=1, source_target_pairs={{0,1},{1,0},{2,3},{3,2},{4,5},{5,4},{6,7},{7,6},{8,9},{9,8},{10,11... | collective-permute-start | bytes 1544 | tf_op jit(solution)/shard_map/ppermute | solution.py:16
  30.2 15.0 %collective-permute-start.2 = (bf16[8,128,256]{2,1,0:T(8,128)(2,1)S(1)}, bf16[8,128,256]{2,1,0:T(8,128)(2,1)S(1)}, u32[]{:S(2)}, u32[]{:S(2)}) collective-permute-start(bf16[8,128,256]{2,1,0:T(8,128)(2,1)S(1)} %copy-done.5), channel_id=1, source_target_pairs={{0,2},{2,0},{1,3},{3,1},{4,6},{6,4},{5,7},{7,5},{8,10},{10,8},{9,1... | collective-permute-start | bytes 1572872 | tf_op jit(solution)/shard_map/ppermute | solution.py:16
  32.3 16.0 %collective-permute-start.3 = (bf16[128,512]{1,0:T(8,128)(2,1)S(1)}, bf16[128,512]{1,0:T(8,128)(2,1)S(1)}, u32[]{:S(2)}, u32[]{:S(2)}) collective-permute-start(bf16[128,512]{1,0:T(8,128)(2,1)S(1)} %get-tuple-element.35), channel_id=1, source_target_pairs={{0,0},{1,2},{2,1},{3,3},{4,44},{5,46},{6,45},{7,47},{8,88},{9,90},... | collective-permute-start | bytes 393224 | tf_op jit(solution)/shard_map/ppermute | solution.py:234
  36.5 11.8 %collective-permute-start.4 = (bf16[128,512]{1,0:T(8,128)(2,1)S(1)}, bf16[128,512]{1,0:T(8,128)(2,1)S(1)}, u32[]{:S(2)}, u32[]{:S(2)}) collective-permute-start(bf16[128,512]{1,0:T(8,128)(2,1)S(1)} %get-tuple-element.34), channel_id=1, source_target_pairs={{0,2},{1,0},{2,3},{3,1},{4,46},{5,44},{6,47},{7,45},{8,90},{9,88},... | collective-permute-start | bytes 393224 | tf_op jit(solution)/shard_map/ppermute | solution.py:234
  45.2 19.5 %copy-start.2 = (f32[2048]{0:T(1024)S(1)}, f32[2048]{0:T(1024)}, u32[]{:S(2)}) copy-start(f32[2048]{0:T(1024)} %param.9) | copy-start | bytes 24580
  48.3 50.2 %all-to-all-start = ((bf16[8,128,256]{2,1,0:T(8,128)(2,1)}), bf16[8,128,256]{2,1,0:T(8,128)(2,1)S(1)}, u32[]{:S(2)}, u32[]{:S(2)}) async-start(bf16[8,128,256]{2,1,0:T(8,128)(2,1)} %add_convert_fusion), calls=%async_computation | async-start | bytes 1048576 | tf_op jit(solution)/shard_map/all_to_all | solution.py:266
  96.5 7.1 %collective-permute-start.5 = (bf16[128,768]{1,0:T(8,128)(2,1)S(1)}, bf16[128,768]{1,0:T(8,128)(2,1)S(1)}, u32[]{:S(2)}, u32[]{:S(2)}) collective-permute-start(bf16[128,768]{1,0:T(8,128)(2,1)S(1)} %get-tuple-element.39), channel_id=1, source_target_pairs={{0,2},{2,0},{1,3},{3,1},{4,6},{6,4},{5,7},{7,5},{8,10},{10,8},{9,1... | collective-permute-start | bytes 589832 | tf_op jit(solution)/shard_map/ppermute | solution.py:16
  150.6 18.2 %all-to-all-start.2 = ((bf16[8,256,256]{2,1,0:T(8,128)(2,1)}), bf16[8,256,256]{2,1,0:T(8,128)(2,1)S(1)}, u32[]{:S(2)}, u32[]{:S(2)}) async-start(bf16[8,256,256]{2,1,0:T(8,128)(2,1)} %shard_map.88), calls=%async_computation.3 | async-start | bytes 2097152 | tf_op jit(solution)/shard_map/all_to_all | solution.py:286
Sparse Core Ops, SparseCore 0:
  27.2 68.2 reduce-scatter.1

commit v10 on v8

--- a/solution.py
+++ b/solution.py
@@ -169,18 +169,20 @@
     part = lax.psum_scatter(products, "z", scatter_dimension=0, tiled=True)
 
     plane_there = (3 * z_at + row_at) % Z_N
-    pieces = []
-    for turn in range(2):
-        perm = []
-        for r in range(ROWS_N):
-            for z in range(Z_N):
-                for u in range(XH_N):
-                    for v in range(CORE_N):
-                        src = ((r * Z_N + z) * XH_N + u) * CORE_N + v
-                        dst = ((z * Z_N + (3 * z + r) % Z_N) * XH_N + (v ^ turn)) * CORE_N + u
-                        perm.append((src, dst))
-        chip_there = plane_there * XH_N + (core_at ^ turn)
-        pieces.append(lax.ppermute(piece(held_features, chip_there, 2 * rows), ALL, perm))
+    perm = [
+        (r * Z_N + z, r * Z_N + (3 * z + r) % Z_N) for r in range(ROWS_N) for z in range(Z_N)
+    ]
+    plane = lax.ppermute(piece(held_features, plane_there, 4 * rows), ("row", "z"), perm)
+    perm = []
+    for r in range(ROWS_N):
+        for z in range(Z_N):
+            for u in range(XH_N):
+                for v in range(CORE_N):
+                    src = ((r * Z_N + z) * XH_N + u) * CORE_N + v
+                    dst = ((3 * (z - r) % Z_N * Z_N + z) * XH_N + v) * CORE_N + u
+                    perm.append((src, dst))
+    plane = lax.ppermute(plane, ALL, perm)
+    pieces = [piece(plane, xh_at, 2 * rows), swap(piece(plane, 1 - xh_at, 2 * rows), "xh")]
 
     ids_there = swap(expert_ids, "core")
     flat, position = slot_targets(expert_ids)

time: 241 us -> 238 us (0.988)
  waiting for transfers between devices: 48.5 us -> 25 us
  starting transfers between devices: 26.2 us -> 44.7 us
    reduce_scatter x1, waiting for transfers between devices: 29.4 us -> 10.6 us  [local(): part = lax.psum_scatter(products, 'z', scatter_dimension=0, tiled=True)]
    all_to_all x1, starting transfers between devices: 16.3 us -> 29.9 us  [local(): lax.all_to_all(send_grad.reshape(COL_N, CAP, share), COL, split_axis=0, c...]
    ppermute x4 -> x5, starting transfers between devices: 6.51 us -> 10.8 us  [swap(): return lax.ppermute(values, axis, [(0, 1), (1, 0)])]
    all_to_all x1, waiting for transfers between devices: 12.1 us -> 8.57 us  [local(): lax.all_to_all(send_grad.reshape(COL_N, CAP, share), COL, split_axis=0, c...]
    ppermute x4 -> x5, waiting for transfers between devices: 6.92 us -> 5.85 us  [swap(): return lax.ppermute(values, axis, [(0, 1), (1, 0)])]
  transfers between devices with their start and end apart: 8 -> 9, of which waited for: 3 -> 3; matrix products, arithmetic and copies ran while one was open for 4% -> 4% of each run, Pallas kernels for 0% -> 0%
where the time goes in v10:
time: 238 us; the launch traced here: 237 us
  blocking collectives  116 us (49%)
  starting transfers between devices  44.7 us (19%)
  waiting for transfers between devices  25 us (11%)
  between operations  14.3 us (6%)
  Pallas kernels  14.2 us (6%)
  matrix products  13.3 us (6%)
  other arithmetic  5.1 us (2%)
  local copies, waits for them, and re-layouts  4.69 us (2%)
    all_to_all x1, blocking collectives, local(): lax.all_to_all(answer.reshape(COL_N, CAP, width + share), COL, split_axis...  44 us
    all_to_all x1, blocking collectives, local(): lax.all_to_all(send_rows.reshape(COL_N, 2 * CAP, half), COL, split_axis=0...  37.7 us
    all_to_all x1, starting transfers between devices, local(): lax.all_to_all(send_grad.reshape(COL_N, CAP, share), COL, split_axis=0, c...  29.9 us
    all_to_all x1, blocking collectives, local(): parts = lax.all_to_all(pre, 'row', split_axis=0, concat_axis=0, tiled=True)  18.1 us
    all_to_all x1, blocking collectives, local(): lax.all_to_all(jnp.broadcast_to(slope[None], (ROWS_N, slots, share)), 'ro...  16.4 us
    pallas_call x2, Pallas kernels, expert_call(): pl.pallas_call(kernel, in_specs=[VMEM] * (len(operands) - 1) + [pl.BlockS...  13.7 us
    ppermute x5, starting transfers between devices, swap(): return lax.ppermute(values, axis, [(0, 1), (1, 0)])  10.8 us
    reduce_scatter x1, waiting for transfers between devices, local(): part = lax.psum_scatter(products, 'z', scatter_dimension=0, tiled=True)  10.6 us
  transfers between devices with their start and end apart: 9, of which 3 were waited for; matrix products, arithmetic and copies ran while one was open for 4% of the time, Pallas kernels for 0%

profile of v10, /device:TPU:1, one launch (start us, length us, event | category | flops | bytes accessed | tf_op | source)
XLA Modules:
  0.0 237.3 jit_solution(15098041508738619947)
XLA Ops:
  7.2 3.3 %collective-permute-start.1 = (bf16[2048,512]{1,0:T(8,128)(2,1)}, bf16[2048,512]{1,0:T(8,128)(2,1)}, u32[]{:S(2)}, u32[]{:S(2)}) collective-permute-start(bf16[2048,512]{1,0:T(8,128)(2,1)} %param.7), channel_id=1, source_target_pairs={{0,1},{1,0},{2,3},{3,2},{4,5},{5,4},{6,7},{7,6},{8,9},{9,8},{10,11... | collective-permute-start | bytes 6291464 | tf_op jit(solution)/shard_map/ppermute | solution.py:16
  10.6 1.5 collective-permute-start
  12.2 4.1 %fusion.3 = f32[1024,2048]{0,1:T(8,128)S(1)} fusion(bf16[2048,512]{1,0:T(8,128)(2,1)} %param.7, bf16[2048,512]{1,0:T(8,128)(2,1)S(1)} %copy-done, s32[]{:T(128)S(6)} %select_n.43), kind=kOutput, calls=%fused_computation.7 | convolution fusion | flops 2147483648 | bytes 11534340 | tf_op jit(solution)/shard_map/dot_general | solution.py:160
  16.3 6.3 %fusion = bf16[2048,1024]{1,0:T(8,128)(2,1)} fusion(f32[1024,2048]{0,1:T(8,128)S(1)} %fusion.3, bf16[1024,512]{1,0:T(8,128)(2,1)} %collective-permute-done, bf16[2048,512]{1,0:T(8,128)(2,1)} %collective-permute-done.1), kind=kOutput, calls=%fused_computation.1 | convolution fusion | flops 2151677952 | bytes 15728640 | tf_op jit(solution)/shard_map/dot_general | solution.py:163
  24.9 1.0 constant_dynamic-slice_fusion.4
  27.8 3.2 %collective-permute-start.3 = (bf16[256,512]{1,0:T(8,128)(2,1)S(1)}, bf16[256,512]{1,0:T(8,128)(2,1)S(1)}, u32[]{:S(2)}, u32[]{:S(2)}) collective-permute-start(bf16[256,512]{1,0:T(8,128)(2,1)S(1)} %collective-permute-done.2), channel_id=1, source_target_pairs={{0,0},{1,2},{2,1},{3,3},{4,100},{5,102},{6,101},{7,103},{8,200},{9... | collective-permute-start | bytes 786440 | tf_op jit(solution)/shard_map/ppermute | solution.py:184
  31.5 0.8 dynamic-slice_convert_fusion
  32.4 0.9 fusion.1
  33.3 29.9 %all-to-all-start = ((bf16[32,8,256]{2,1,0:T(8,128)(2,1)}), bf16[32,8,256]{2,1,0:T(8,128)(2,1)S(1)}, u32[]{:S(2)}, u32[]{:S(2)}) async-start(bf16[32,8,256]{2,1,0:T(8,128)(2,1)} %fusion.1), calls=%async_computation.1 | async-start | bytes 262144 | tf_op jit(solution)/shard_map/all_to_all | solution.py:212
  63.3 3.0 %collective-permute-start.4 = (bf16[128,512]{1,0:T(8,128)(2,1)S(1)}, bf16[128,512]{1,0:T(8,128)(2,1)S(1)}, u32[]{:S(2)}, u32[]{:S(2)}) collective-permute-start(bf16[128,512]{1,0:T(8,128)(2,1)S(1)} %get-tuple-element.26), channel_id=1, source_target_pairs={{0,2},{2,0},{1,3},{3,1},{4,6},{6,4},{5,7},{7,5},{8,10},{10,8},{9,1... | collective-permute-start | bytes 393224 | tf_op jit(solution)/shard_map/ppermute | solution.py:16
  66.6 8.6 %all-to-all-done = bf16[32,8,256]{2,1,0:T(8,128)(2,1)S(1)} async-done(((bf16[32,8,256]{2,1,0:T(8,128)(2,1)}), bf16[32,8,256]{2,1,0:T(8,128)(2,1)S(1)}, u32[]{:S(2)}, u32[]{:S(2)}) %all-to-all-start) | async-done | bytes 131104 | tf_op jit(solution)/shard_map/all_to_all | solution.py:212
  75.2 10.6 %reduce-scatter.2.cloned.1.call-done = bf16[256,1024]{1,0:T(8,128)(2,1)} async-done(((bf16[2048,1024]{1,0:T(8,128)(2,1)}), bf16[256,1024]{1,0:T(8,128)(2,1)}) %reduce-scatter.2.cloned.1.call-update) | async-done | bytes 524304 | tf_op jit(solution)/shard_map/reduce_scatter | solution.py:169
  85.7 1.1 constant_dynamic-slice_fusion
  86.8 2.9 %collective-permute-start.6 = (bf16[128,1024]{1,0:T(8,128)(2,1)S(1)}, bf16[128,1024]{1,0:T(8,128)(2,1)S(1)}, u32[]{:S(2)}, u32[]{:S(2)}) collective-permute-start(bf16[128,1024]{1,0:T(8,128)(2,1)S(1)} %get-tuple-element.22), channel_id=1, source_target_pairs={{0,2},{2,0},{1,3},{3,1},{4,6},{6,4},{5,7},{7,5},{8,10},{10,8},{9,1... | collective-permute-start | bytes 786440 | tf_op jit(solution)/shard_map/ppermute | solution.py:16
  89.7 5.8 %collective-permute-done.6.there = bf16[128,1024]{1,0:T(8,128)(2,1)S(1)} collective-permute-done((bf16[128,1024]{1,0:T(8,128)(2,1)S(1)}, bf16[128,1024]{1,0:T(8,128)(2,1)S(1)}, u32[]{:S(2)}, u32[]{:S(2)}) %collective-permute-start.6) | collective-permute-done | bytes 262176 | tf_op jit(solution)/shard_map/ppermute | solution.py:16
  96.0 37.7 %all_to_all.25 = bf16[32,16,1024]{2,1,0:T(8,128)(2,1)} all-to-all(bf16[32,16,1024]{2,1,0:T(8,128)(2,1)S(1)} %bitcast.21), channel_id=1, replica_groups=mesh['row'=8,'z'=8,'xh'=2,'core'=2] {'z','xh','core'}, dimensions={0} | all-to-all | bytes 2097152 | tf_op jit(solution)/shard_map/all_to_all | solution.py:224
  133.7 6.8 %shard_map.87 = bf16[8,256,256]{2,1,0:T(8,128)(2,1)} custom-call(bf16[16,2,16,1024]{3,2,1,0:T(8,128)(2,1)} %bitcast.28, bf16[2048,2048]{1,0:T(8,128)(2,1)} %bitcast.23), custom_call_target="tpu_custom_call" | custom-call | flops 2147483648 | bytes 10485760 | tf_op jit(solution)/shard_map/pallas_call | solution.py:120
  140.5 18.1 %all_to_all.26 = bf16[8,256,256]{2,1,0:T(8,128)(2,1)S(1)} all-to-all(bf16[8,256,256]{2,1,0:T(8,128)(2,1)} %shard_map.87), channel_id=1, replica_groups=mesh['row'=8,'z'=8,'xh'=2,'core'=2] {'row'}, dimensions={0} | all-to-all | bytes 2097152 | tf_op jit(solution)/shard_map/all_to_all | solution.py:230
  158.7 0.8 multiply_convert_fusion
  159.5 16.4 %all_to_all.27.slopes = bf16[8,256,256]{2,1,0:T(8,128)(2,1)} all-to-all(bf16[8,256,256]{2,1,0:T(8,128)(2,1)S(1)} %broadcast_in_dim.2), channel_id=1, replica_groups=mesh['row'=8,'z'=8,'xh'=2,'core'=2] {'row'}, dimensions={0} | all-to-all | bytes 2097152 | tf_op jit(solution)/shard_map/all_to_all | solution.py:237
  175.9 6.9 %shard_map.88 = bf16[256,2304]{1,0:T(8,128)(2,1)} custom-call(bf16[8,256,256]{2,1,0:T(8,128)(2,1)} %all_to_all.27.slopes, bf16[256,256]{1,0:T(8,128)(2,1)} %get-tuple-element.24.activated, bf16[2048,2048]{1,0:T(8,128)(2,1)} %bitcast.24), custom_call_target="tpu_custom_call" | custom-call | flops 2147483648 | bytes 10485760 | tf_op jit(solution)/shard_map/pallas_call | solution.py:120
  182.8 44.0 %all_to_all.28 = bf16[32,8,2304]{2,1,0:T(8,128)(2,1)S(1)} all-to-all(bf16[32,8,2304]{2,1,0:T(8,128)(2,1)} %bitcast.27), channel_id=1, replica_groups=mesh['row'=8,'z'=8,'xh'=2,'core'=2] {'z','xh','core'}, dimensions={0} | all-to-all | bytes 2359296 | tf_op jit(solution)/shard_map/all_to_all | solution.py:246
  227.1 1.6 multiply_reduce_fusion
  228.7 1.8 convolution_convert_fusion
  (57 shorter events, 6.1 us)
Async XLA Ops:
  7.2 3.4 %copy-start = (bf16[2048,512]{1,0:T(8,128)(2,1)S(1)}, bf16[2048,512]{1,0:T(8,128)(2,1)}, u32[]{:S(2)}) copy-start(bf16[2048,512]{1,0:T(8,128)(2,1)} %param.8) | copy-start | bytes 6291460
  7.2 78.5 %reduce-scatter.2.cloned.1.call-start = ((), (), s32[]{:S(2)}) async-start(), calls=%async_computation.6 | async-start | bytes 4718592 | tf_op jit(solution)/shard_map/reduce_scatter | solution.py:169
  7.2 9.0 %collective-permute-start.1 = (bf16[2048,512]{1,0:T(8,128)(2,1)}, bf16[2048,512]{1,0:T(8,128)(2,1)}, u32[]{:S(2)}, u32[]{:S(2)}) collective-permute-start(bf16[2048,512]{1,0:T(8,128)(2,1)} %param.7), channel_id=1, source_target_pairs={{0,1},{1,0},{2,3},{3,2},{4,5},{5,4},{6,7},{7,6},{8,9},{9,8},{10,11... | collective-permute-start | bytes 6291464 | tf_op jit(solution)/shard_map/ppermute | solution.py:16
  10.6 5.6 %collective-permute-start = (bf16[1024,512]{1,0:T(8,128)(2,1)S(1)}, bf16[1024,512]{1,0:T(8,128)(2,1)}, u32[]{:S(2)}, u32[]{:S(2)}) collective-permute-start(bf16[1024,512]{1,0:T(8,128)(2,1)S(1)} %constant_dynamic-slice_fusion.5), channel_id=1, source_target_pairs={{0,1},{1,0},{2,3},{3,2},{4,5},{5,4},{6,7},{7,6},{8,9},{9,8},{10,11... | collective-permute-start | bytes 3145736 | tf_op jit(solution)/shard_map/ppermute | solution.py:16
  22.6 0.7 copy-start.3
  22.6 4.7 %copy-start.5 = (f32[64,2]{0,1:T(2,128)S(1)}, f32[64,2]{0,1:T(2,128)}, u32[]{:S(2)}) copy-start(f32[64,2]{0,1:T(2,128)} %param.11) | copy-start | bytes 1540
  23.3 66.4 %copy-start.4 = (f32[2048]{0:T(1024)S(1)}, f32[2048]{0:T(1024)}, u32[]{:S(2)}) copy-start(f32[2048]{0:T(1024)} %param.9) | copy-start | bytes 24580
  23.3 4.2 %collective-permute-start.5 = (s32[64,2]{0,1:T(2,128)S(1)}, s32[64,2]{0,1:T(2,128)S(1)}, u32[]{:S(2)}, u32[]{:S(2)}) collective-permute-start(s32[64,2]{0,1:T(2,128)S(1)} %copy-done.3), channel_id=1, source_target_pairs={{0,1},{1,0},{2,3},{3,2},{4,5},{5,4},{6,7},{7,6},{8,9},{9,8},{10,11... | collective-permute-start | bytes 1544 | tf_op jit(solution)/shard_map/ppermute | solution.py:16
  25.9 1.9 collective-permute-start.2
  27.4 4.8 %copy-start.1 = (f32[64,2]{1,0:T(8,128)}, f32[64,2]{1,0:T(8,128)S(1)}, u32[]{:S(2)}) copy-start(f32[64,2]{1,0:T(8,128)S(1)} %copy.41) | copy-start | bytes 1540
  27.8 35.4 %collective-permute-start.3 = (bf16[256,512]{1,0:T(8,128)(2,1)S(1)}, bf16[256,512]{1,0:T(8,128)(2,1)S(1)}, u32[]{:S(2)}, u32[]{:S(2)}) collective-permute-start(bf16[256,512]{1,0:T(8,128)(2,1)S(1)} %collective-permute-done.2), channel_id=1, source_target_pairs={{0,0},{1,2},{2,1},{3,3},{4,100},{5,102},{6,101},{7,103},{8,200},{9... | collective-permute-start | bytes 786440 | tf_op jit(solution)/shard_map/ppermute | solution.py:184
  33.3 41.9 %all-to-all-start = ((bf16[32,8,256]{2,1,0:T(8,128)(2,1)}), bf16[32,8,256]{2,1,0:T(8,128)(2,1)S(1)}, u32[]{:S(2)}, u32[]{:S(2)}) async-start(bf16[32,8,256]{2,1,0:T(8,128)(2,1)} %fusion.1), calls=%async_computation.1 | async-start | bytes 262144 | tf_op jit(solution)/shard_map/all_to_all | solution.py:212
  63.3 11.9 %collective-permute-start.4 = (bf16[128,512]{1,0:T(8,128)(2,1)S(1)}, bf16[128,512]{1,0:T(8,128)(2,1)S(1)}, u32[]{:S(2)}, u32[]{:S(2)}) collective-permute-start(bf16[128,512]{1,0:T(8,128)(2,1)S(1)} %get-tuple-element.26), channel_id=1, source_target_pairs={{0,2},{2,0},{1,3},{3,1},{4,6},{6,4},{5,7},{7,5},{8,10},{10,8},{9,1... | collective-permute-start | bytes 393224 | tf_op jit(solution)/shard_map/ppermute | solution.py:16
  86.8 8.7 %collective-permute-start.6 = (bf16[128,1024]{1,0:T(8,128)(2,1)S(1)}, bf16[128,1024]{1,0:T(8,128)(2,1)S(1)}, u32[]{:S(2)}, u32[]{:S(2)}) collective-permute-start(bf16[128,1024]{1,0:T(8,128)(2,1)S(1)} %get-tuple-element.22), channel_id=1, source_target_pairs={{0,2},{2,0},{1,3},{3,1},{4,6},{6,4},{5,7},{7,5},{8,10},{10,8},{9,1... | collective-permute-start | bytes 786440 | tf_op jit(solution)/shard_map/ppermute | solution.py:16
  182.8 44.0 %copy-start.2 = (bf16[256,128]{1,0:T(8,128)(2,1)S(1)}, bf16[256,128]{1,0:T(8,128)(2,1)}, u32[]{:S(2)}) copy-start(bf16[256,128]{1,0:T(8,128)(2,1)} %fusion.9) | copy-start | bytes 196612
Sparse Core Ops, SparseCore 0:
  22.8 62.9 reduce-scatter.1

commit v11 on v9

--- a/solution.py
+++ b/solution.py
@@ -20,7 +20,7 @@
     return lax.dynamic_slice_in_dim(values, index * size, size, axis)
 
 
-EARLY = 768
+EARLY = 512
 GRANT = 56 << 20
 CHUNKS, CUTS = 4, 4
 NT = (((1,), (1,)), ((), ()))
@@ -220,18 +220,19 @@
     ).astype(jnp.bfloat16)
 
     plane_there = (3 * z_at + row_at) % Z_N
-    pieces = []
-    for turn in range(2):
-        perm = []
-        for r in range(ROWS_N):
-            for z in range(Z_N):
-                for u in range(XH_N):
-                    for v in range(CORE_N):
-                        src = ((r * Z_N + z) * XH_N + u) * CORE_N + v
-                        dst = ((z * Z_N + (3 * z + r) % Z_N) * XH_N + (v ^ turn)) * CORE_N + u
-                        perm.append((src, dst))
-        chip_there = plane_there * XH_N + (core_at ^ turn)
-        pieces.append(lax.ppermute(piece(held_features, chip_there, 2 * rows), ALL, perm))
+    perm = [
+        (r * Z_N + z, r * Z_N + (3 * z + r) % Z_N) for r in range(ROWS_N) for z in range(Z_N)
+    ]
+    plane = lax.ppermute(piece(held_features, plane_there, 4 * rows), ("row", "z"), perm)
+    perm = []
+    for r in range(ROWS_N):
+        for z in range(Z_N):
+            for u in range(XH_N):
+                for v in range(CORE_N):
+                    src = ((r * Z_N + z) * XH_N + u) * CORE_N + v
+                    dst = ((3 * (z - r) % Z_N * Z_N + z) * XH_N + v) * CORE_N + u
+                    perm.append((src, dst))
+    plane = lax.ppermute(plane, ALL, perm)
 
     ids_there = swap(expert_ids, "core")
     flat, position = slot_targets(expert_ids)
@@ -262,7 +263,8 @@
     send_grad = send_grad.reshape(COL_N, CAP, share)
     send_grad = jnp.concatenate([send_grad[:, :, :lanes], send_grad[:, :, lanes:]], axis=1)
 
-    late_sum, pieces = lax.optimization_barrier((late_sum, pieces))
+    late_sum, plane = lax.optimization_barrier((late_sum, plane))
+    pieces = [piece(plane, xh_at, 2 * rows), swap(piece(plane, 1 - xh_at, 2 * rows), "xh")]
     late_parts = lax.all_to_all(late_sum, "z", split_axis=0, concat_axis=0, tiled=True)
     part_there = swap(piece(part, 1 - xh_at, 2 * rows), "xh")
     late_parts, part_there, pieces, chip_chooser, chooser, table, send_grad = (

time: 244 us -> 239 us (0.980)
  blocking collectives: 97.3 us -> 93.6 us
  waiting for transfers between devices: 65.9 us -> 62.8 us
    reduce_scatter x1, waiting for transfers between devices: 30.1 us -> 0.02 us  [local(): part = lax.psum_scatter(early, 'z', scatter_dimension=0, tiled=True)]
    all_to_all x1, waiting for transfers between devices: 0.01 us -> 21.3 us  [local(): lax.all_to_all(late_sum, 'z', split_axis=0, concat_axis=0, tiled=True)]
    ppermute x5 -> x6, waiting for transfers between devices: 20 us -> 25.6 us  [swap(): return lax.ppermute(values, axis, [(0, 1), (1, 0)])]
    all_to_all x1, blocking collectives: 39.7 us -> 36.7 us  [local(): routed = lax.all_to_all(send, COL, split_axis=0, concat_axis=0, tiled=True)]
    ppermute x5 -> x6, starting transfers between devices: 6.6 us -> 8.27 us  [swap(): return lax.ppermute(values, axis, [(0, 1), (1, 0)])]
  transfers between devices with their start and end apart: 10 -> 11, of which waited for: 7 -> 7; matrix products, arithmetic and copies ran while one was open for 3% -> 3% of each run, Pallas kernels for 0% -> 0%
where the time goes in v11:
time: 239 us; the launch traced here: 238 us
  blocking collectives  93.6 us (39%)
  waiting for transfers between devices  62.8 us (26%)
  starting transfers between devices  32.4 us (14%)
  Pallas kernels  23.5 us (10%)
  between operations  14.3 us (6%)
  other arithmetic  5.09 us (2%)
  local copies, waits for them, and re-layouts  4.94 us (2%)
    all_to_all x1, blocking collectives, local(): lax.all_to_all(answer.reshape(COL_N, CAP, width + share), COL, split_axis...  38.8 us
    all_to_all x1, blocking collectives, local(): routed = lax.all_to_all(send, COL, split_axis=0, concat_axis=0, tiled=True)  36.7 us
    ppermute x6, waiting for transfers between devices, swap(): return lax.ppermute(values, axis, [(0, 1), (1, 0)])  25.6 us
    all_to_all x1, waiting for transfers between devices, local(): lax.all_to_all(late_sum, 'z', split_axis=0, concat_axis=0, tiled=True)  21.3 us
    all_to_all x1, blocking collectives, local(): lax.all_to_all(jnp.broadcast_to(slope[None], (ROWS_N, slots, share)), 'ro...  18 us
    all_to_all x1, starting transfers between devices, local(): lax.all_to_all(late_sum, 'z', split_axis=0, concat_axis=0, tiled=True)  16 us
    all_to_all x1, waiting for transfers between devices, local(): parts = lax.all_to_all(pre, 'row', split_axis=0, concat_axis=0, tiled=True)  13.9 us
    pallas_call x2, Pallas kernels, expert_call(): pl.pallas_call(kernel, in_specs=[VMEM] * (len(operands) - 1) + [pl.BlockS...  13.7 us
  transfers between devices with their start and end apart: 11, of which 7 were waited for; matrix products, arithmetic and copies ran while one was open for 3% of the time, Pallas kernels for 0%

profile of v11, /device:TPU:1, one launch (start us, length us, event | category | flops | bytes accessed | tf_op | source)
XLA Modules:
  0.0 238.0 jit_solution(8733584612385676121)
XLA Ops:
  7.2 3.3 %collective-permute-start = (bf16[2048,512]{1,0:T(8,128)(2,1)}, bf16[2048,512]{1,0:T(8,128)(2,1)S(1)}, u32[]{:S(2)}, u32[]{:S(2)}) collective-permute-start(bf16[2048,512]{1,0:T(8,128)(2,1)} %here.1), channel_id=1, source_target_pairs={{0,1},{1,0},{2,3},{3,2},{4,5},{5,4},{6,7},{7,6},{8,9},{9,8},{10,11... | collective-permute-start | bytes 6291464 | tf_op jit(solution)/shard_map/ppermute | solution.py:16
  11.3 5.2 %collective-permute-done.there = bf16[2048,512]{1,0:T(8,128)(2,1)S(1)} collective-permute-done((bf16[2048,512]{1,0:T(8,128)(2,1)}, bf16[2048,512]{1,0:T(8,128)(2,1)S(1)}, u32[]{:S(2)}, u32[]{:S(2)}) %collective-permute-start) | collective-permute-done | bytes 2097184 | tf_op jit(solution)/shard_map/ppermute | solution.py:16
  16.5 1.2 collective-permute-done.1.weight_there
  17.8 9.2 %shard_map.86 = (bf16[2048,512]{1,0:T(8,128)(2,1)}, bf16[8,128,512]{2,1,0:T(8,128)(2,1)}, bf16[8,128,512]{2,1,0:T(8,128)(2,1)}) custom-call(s32[2]{0:T(128)} %pad_add_fusion.at, bf16[2048,512]{1,0:T(8,128)(2,1)} %here.1, bf16[2048,512]{1,0:T(8,128)(2,1)} %copy-done.4, bf16[2048,512]{1,0:T(8,128)(2,1)} %weight_here.1, ...), custom_call_target="tpu_custom_call" | custom-call | flops 4294967296 | bytes 10485760 | tf_op jit(solution)/shard_map/pallas_call | solution.py:65
  27.1 1.1 collective-permute-start.2
  29.4 1.0 constant_dynamic-slice_fusion.4
  31.2 3.8 %collective-permute-start.4 = (bf16[256,512]{1,0:T(8,128)(2,1)S(1)}, bf16[256,512]{1,0:T(8,128)(2,1)S(1)}, u32[]{:S(2)}, u32[]{:S(2)}) collective-permute-start(bf16[256,512]{1,0:T(8,128)(2,1)S(1)} %collective-permute-done.3), channel_id=1, source_target_pairs={{0,0},{1,2},{2,1},{3,3},{4,100},{5,102},{6,101},{7,103},{8,200},{9... | collective-permute-start | bytes 786440 | tf_op jit(solution)/shard_map/ppermute | solution.py:235
  35.0 18.2 %collective-permute-done.2 = bf16[8,128,512]{2,1,0:T(8,128)(2,1)S(1)} collective-permute-done((bf16[8,128,512]{2,1,0:T(8,128)(2,1)}, bf16[8,128,512]{2,1,0:T(8,128)(2,1)S(1)}, u32[]{:S(2)}, u32[]{:S(2)}) %collective-permute-start.2) | collective-permute-done | bytes 1048608 | tf_op jit(solution)/shard_map/ppermute | solution.py:16
  53.2 1.3 add_convert_fusion
  54.6 2.0 collective-permute-done.4
  56.6 16.0 %all-to-all-start = ((bf16[8,128,512]{2,1,0:T(8,128)(2,1)}), bf16[8,128,512]{2,1,0:T(8,128)(2,1)S(1)}, u32[]{:S(2)}, u32[]{:S(2)}) async-start(bf16[8,128,512]{2,1,0:T(8,128)(2,1)} %add_convert_fusion), calls=%async_computation | async-start | bytes 2097152 | tf_op jit(solution)/shard_map/all_to_all | solution.py:268
  75.2 1.0 constant_dynamic-slice_fusion
  76.2 3.0 %collective-permute-start.5 = (bf16[128,512]{1,0:T(8,128)(2,1)S(1)}, bf16[128,512]{1,0:T(8,128)(2,1)S(1)}, u32[]{:S(2)}, u32[]{:S(2)}) collective-permute-start(bf16[128,512]{1,0:T(8,128)(2,1)S(1)} %get-tuple-element.37), channel_id=1, source_target_pairs={{0,2},{2,0},{1,3},{3,1},{4,6},{6,4},{5,7},{7,5},{8,10},{10,8},{9,1... | collective-permute-start | bytes 393224 | tf_op jit(solution)/shard_map/ppermute | solution.py:16
  79.6 1.0 collective-permute-done.6.right
  80.5 21.3 %all-to-all-done.late = bf16[8,128,512]{2,1,0:T(8,128)(2,1)S(1)} async-done(((bf16[8,128,512]{2,1,0:T(8,128)(2,1)}), bf16[8,128,512]{2,1,0:T(8,128)(2,1)S(1)}, u32[]{:S(2)}, u32[]{:S(2)}) %all-to-all-start) | async-done | bytes 1048608 | tf_op jit(solution)/shard_map/all_to_all | solution.py:268
  102.4 36.7 %all_to_all.25 = bf16[32,16,1152]{2,1,0:T(8,128)(2,1)} all-to-all(bf16[32,16,1152]{2,1,0:T(8,128)(2,1)S(1)} %shard_map.87), channel_id=1, replica_groups=mesh['row'=8,'z'=8,'xh'=2,'core'=2] {'z','xh','core'}, dimensions={0} | all-to-all | bytes 2359296 | tf_op jit(solution)/shard_map/all_to_all | solution.py:281
  139.1 6.8 %shard_map.88 = bf16[8,256,256]{2,1,0:T(8,128)(2,1)} custom-call(bf16[16,2,16,1152]{3,2,1,0:T(8,128)(2,1)} %bitcast.24, bf16[2048,2048]{1,0:T(8,128)(2,1)} %bitcast.22), custom_call_target="tpu_custom_call" | custom-call | flops 2147483648 | bytes 10485760 | tf_op jit(solution)/shard_map/pallas_call | solution.py:172
  145.9 3.6 %all-to-all-start.2 = ((bf16[8,256,256]{2,1,0:T(8,128)(2,1)}), bf16[8,256,256]{2,1,0:T(8,128)(2,1)S(1)}, u32[]{:S(2)}, u32[]{:S(2)}) async-start(bf16[8,256,256]{2,1,0:T(8,128)(2,1)} %shard_map.88), calls=%async_computation.3 | async-start | bytes 2097152 | tf_op jit(solution)/shard_map/all_to_all | solution.py:288
  149.5 0.9 fusion.15
  150.4 13.9 %all-to-all-done.2 = bf16[8,256,256]{2,1,0:T(8,128)(2,1)S(1)} async-done(((bf16[8,256,256]{2,1,0:T(8,128)(2,1)}), bf16[8,256,256]{2,1,0:T(8,128)(2,1)S(1)}, u32[]{:S(2)}, u32[]{:S(2)}) %all-to-all-start.2) | async-done | bytes 1048608 | tf_op jit(solution)/shard_map/all_to_all | solution.py:288
  165.2 18.0 %all_to_all.26.slopes = bf16[8,256,256]{2,1,0:T(8,128)(2,1)} all-to-all(bf16[8,256,256]{2,1,0:T(8,128)(2,1)S(1)} %broadcast_in_dim.2), channel_id=1, replica_groups=mesh['row'=8,'z'=8,'xh'=2,'core'=2] {'row'}, dimensions={0} | all-to-all | bytes 2097152 | tf_op jit(solution)/shard_map/all_to_all | solution.py:295
  183.2 6.9 %shard_map.89 = bf16[256,2304]{1,0:T(8,128)(2,1)} custom-call(bf16[8,256,256]{2,1,0:T(8,128)(2,1)} %all_to_all.26.slopes, bf16[256,256]{1,0:T(8,128)(2,1)} %get-tuple-element.34.activated, bf16[2048,2048]{1,0:T(8,128)(2,1)} %bitcast.23), custom_call_target="tpu_custom_call" | custom-call | flops 2147483648 | bytes 10485760 | tf_op jit(solution)/shard_map/pallas_call | solution.py:172
  190.1 38.8 %all_to_all.27 = bf16[32,8,2304]{2,1,0:T(8,128)(2,1)S(1)} all-to-all(bf16[32,8,2304]{2,1,0:T(8,128)(2,1)} %bitcast.27), channel_id=1, replica_groups=mesh['row'=8,'z'=8,'xh'=2,'core'=2] {'z','xh','core'}, dimensions={0} | all-to-all | bytes 2359296 | tf_op jit(solution)/shard_map/all_to_all | solution.py:304
  230.1 1.0 convolution_convert_fusion
  (60 shorter events, 8.5 us)
Async XLA Ops:
  7.2 68.1 %reduce-scatter.2.cloned.1.call-start = ((), (), s32[]{:S(2)}) async-start(), calls=%async_computation.6 | async-start | bytes 2359296 | tf_op jit(solution)/shard_map/reduce_scatter | solution.py:217
  7.2 9.3 %collective-permute-start = (bf16[2048,512]{1,0:T(8,128)(2,1)}, bf16[2048,512]{1,0:T(8,128)(2,1)S(1)}, u32[]{:S(2)}, u32[]{:S(2)}) collective-permute-start(bf16[2048,512]{1,0:T(8,128)(2,1)} %here.1), channel_id=1, source_target_pairs={{0,1},{1,0},{2,3},{3,2},{4,5},{5,4},{6,7},{7,6},{8,9},{9,8},{10,11... | collective-permute-start | bytes 6291464 | tf_op jit(solution)/shard_map/ppermute | solution.py:16
  10.5 7.1 %collective-permute-start.1 = (bf16[2048,512]{1,0:T(8,128)(2,1)}, bf16[2048,512]{1,0:T(8,128)(2,1)}, u32[]{:S(2)}, u32[]{:S(2)}) collective-permute-start(bf16[2048,512]{1,0:T(8,128)(2,1)} %weight_here.1), channel_id=1, source_target_pairs={{0,1},{1,0},{2,3},{3,2},{4,5},{5,4},{6,7},{7,6},{8,9},{9,8},{10,11... | collective-permute-start | bytes 6291464 | tf_op jit(solution)/shard_map/ppermute | solution.py:16
  16.5 1.3 copy-start.4
  27.0 1.1 copy-start.1
  27.0 26.2 %copy-start = (bf16[8,128,512]{2,1,0:T(8,128)(2,1)S(1)}, bf16[8,128,512]{2,1,0:T(8,128)(2,1)}, u32[]{:S(2)}) copy-start(bf16[8,128,512]{2,1,0:T(8,128)(2,1)} %get-tuple-element.17) | copy-start | bytes 3145732
  27.1 26.2 %collective-permute-start.2 = (bf16[8,128,512]{2,1,0:T(8,128)(2,1)}, bf16[8,128,512]{2,1,0:T(8,128)(2,1)S(1)}, u32[]{:S(2)}, u32[]{:S(2)}) collective-permute-start(bf16[8,128,512]{2,1,0:T(8,128)(2,1)} %get-tuple-element.18), channel_id=1, source_target_pairs={{0,2},{2,0},{1,3},{3,1},{4,6},{6,4},{5,7},{7,5},{8,10},{10,8},{9,1... | collective-permute-start | bytes 3145736 | tf_op jit(solution)/shard_map/ppermute | solution.py:16
  28.2 46.2 %collective-permute-start.7 = (s32[64,2]{0,1:T(2,128)S(1)}, s32[64,2]{0,1:T(2,128)S(1)}, u32[]{:S(2)}, u32[]{:S(2)}) collective-permute-start(s32[64,2]{0,1:T(2,128)S(1)} %copy-done.1), channel_id=1, source_target_pairs={{0,1},{1,0},{2,3},{3,2},{4,5},{5,4},{6,7},{7,6},{8,9},{9,8},{10,11... | collective-permute-start | bytes 1544 | tf_op jit(solution)/shard_map/ppermute | solution.py:16
  30.4 0.8 collective-permute-start.3
  31.2 25.3 %collective-permute-start.4 = (bf16[256,512]{1,0:T(8,128)(2,1)S(1)}, bf16[256,512]{1,0:T(8,128)(2,1)S(1)}, u32[]{:S(2)}, u32[]{:S(2)}) collective-permute-start(bf16[256,512]{1,0:T(8,128)(2,1)S(1)} %collective-permute-done.3), channel_id=1, source_target_pairs={{0,0},{1,2},{2,1},{3,3},{4,100},{5,102},{6,101},{7,103},{8,200},{9... | collective-permute-start | bytes 786440 | tf_op jit(solution)/shard_map/ppermute | solution.py:235
  54.5 19.0 %copy-start.3 = (f32[64,2]{0,1:T(2,128)S(1)}, f32[64,2]{0,1:T(2,128)}, u32[]{:S(2)}) copy-start(f32[64,2]{0,1:T(2,128)} %param.11) | copy-start | bytes 1540
  54.6 19.8 %copy-start.2 = (f32[2048]{0:T(1024)S(1)}, f32[2048]{0:T(1024)}, u32[]{:S(2)}) copy-start(f32[2048]{0:T(1024)} %param.9) | copy-start | bytes 24580
  56.6 45.2 %all-to-all-start = ((bf16[8,128,512]{2,1,0:T(8,128)(2,1)}), bf16[8,128,512]{2,1,0:T(8,128)(2,1)S(1)}, u32[]{:S(2)}, u32[]{:S(2)}) async-start(bf16[8,128,512]{2,1,0:T(8,128)(2,1)} %add_convert_fusion), calls=%async_computation | async-start | bytes 2097152 | tf_op jit(solution)/shard_map/all_to_all | solution.py:268
  75.1 5.4 %collective-permute-start.6 = (bf16[128,512]{1,0:T(8,128)(2,1)S(1)}, bf16[128,512]{1,0:T(8,128)(2,1)S(1)}, u32[]{:S(2)}, u32[]{:S(2)}) collective-permute-start(bf16[128,512]{1,0:T(8,128)(2,1)S(1)} %get-tuple-element.38), channel_id=1, source_target_pairs={{0,2},{2,0},{1,3},{3,1},{4,6},{6,4},{5,7},{7,5},{8,10},{10,8},{9,1... | collective-permute-start | bytes 393224 | tf_op jit(solution)/shard_map/ppermute | solution.py:16
  76.2 25.6 %collective-permute-start.5 = (bf16[128,512]{1,0:T(8,128)(2,1)S(1)}, bf16[128,512]{1,0:T(8,128)(2,1)S(1)}, u32[]{:S(2)}, u32[]{:S(2)}) collective-permute-start(bf16[128,512]{1,0:T(8,128)(2,1)S(1)} %get-tuple-element.37), channel_id=1, source_target_pairs={{0,2},{2,0},{1,3},{3,1},{4,6},{6,4},{5,7},{7,5},{8,10},{10,8},{9,1... | collective-permute-start | bytes 393224 | tf_op jit(solution)/shard_map/ppermute | solution.py:16
  145.9 18.3 %all-to-all-start.2 = ((bf16[8,256,256]{2,1,0:T(8,128)(2,1)}), bf16[8,256,256]{2,1,0:T(8,128)(2,1)S(1)}, u32[]{:S(2)}, u32[]{:S(2)}) async-start(bf16[8,256,256]{2,1,0:T(8,128)(2,1)} %shard_map.88), calls=%async_computation.3 | async-start | bytes 2097152 | tf_op jit(solution)/shard_map/all_to_all | solution.py:288
Sparse Core Ops, SparseCore 0:
  27.2 45.1 reduce-scatter.1

commit v12 on v11

--- a/solution.py
+++ b/solution.py
@@ -20,7 +20,7 @@
     return lax.dynamic_slice_in_dim(values, index * size, size, axis)
 
 
-EARLY = 512
+EARLY = 640
 GRANT = 56 << 20
 CHUNKS, CUTS = 4, 4
 NT = (((1,), (1,)), ((), ()))
@@ -224,16 +224,6 @@
         (r * Z_N + z, r * Z_N + (3 * z + r) % Z_N) for r in range(ROWS_N) for z in range(Z_N)
     ]
     plane = lax.ppermute(piece(held_features, plane_there, 4 * rows), ("row", "z"), perm)
-    perm = []
-    for r in range(ROWS_N):
-        for z in range(Z_N):
-            for u in range(XH_N):
-                for v in range(CORE_N):
-                    src = ((r * Z_N + z) * XH_N + u) * CORE_N + v
-                    dst = ((3 * (z - r) % Z_N * Z_N + z) * XH_N + v) * CORE_N + u
-                    perm.append((src, dst))
-    plane = lax.ppermute(plane, ALL, perm)
-
     ids_there = swap(expert_ids, "core")
     flat, position = slot_targets(expert_ids)
     flat_there, position_there = slot_targets(ids_there)
@@ -264,6 +254,15 @@
     send_grad = jnp.concatenate([send_grad[:, :, :lanes], send_grad[:, :, lanes:]], axis=1)
 
     late_sum, plane = lax.optimization_barrier((late_sum, plane))
+    perm = []
+    for r in range(ROWS_N):
+        for z in range(Z_N):
+            for u in range(XH_N):
+                for v in range(CORE_N):
+                    src = ((r * Z_N + z) * XH_N + u) * CORE_N + v
+                    dst = ((3 * (z - r) % Z_N * Z_N + z) * XH_N + v) * CORE_N + u
+                    perm.append((src, dst))
+    plane = lax.ppermute(plane, ALL, perm)
     pieces = [piece(plane, xh_at, 2 * rows), swap(piece(plane, 1 - xh_at, 2 * rows), "xh")]
     late_parts = lax.all_to_all(late_sum, "z", split_axis=0, concat_axis=0, tiled=True)
     part_there = swap(piece(part, 1 - xh_at, 2 * rows), "xh")

time: 239 us -> 243 us (1.017)
  starting transfers between devices: 32.4 us -> 25.8 us
  waiting for transfers between devices: 62.8 us -> 69.2 us
  blocking collectives: 93.6 us -> 97.9 us
    reduce_scatter x1, waiting for transfers between devices: 0.02 us -> 21.3 us  [local(): part = lax.psum_scatter(early, 'z', scatter_dimension=0, tiled=True)]
    all_to_all x1, waiting for transfers between devices: 21.3 us -> 0.01 us  [local(): lax.all_to_all(late_sum, 'z', split_axis=0, concat_axis=0, tiled=True)]
    ppermute x1, waiting for transfers between devices: 2.01 us -> 6.58 us  [local(): plane = lax.ppermute(plane, ALL, perm)]
    all_to_all x1, starting transfers between devices: 16 us -> 11.8 us  [local(): lax.all_to_all(late_sum, 'z', split_axis=0, concat_axis=0, tiled=True)]
    all_to_all x1, blocking collectives: 36.7 us -> 40.3 us  [local(): routed = lax.all_to_all(send, COL, split_axis=0, concat_axis=0, tiled=True)]
    ppermute x6, starting transfers between devices: 8.27 us -> 5.51 us  [swap(): return lax.ppermute(values, axis, [(0, 1), (1, 0)])]
where the time goes in v12:
time: 243 us
  blocking collectives  97.9 us (40%)
  waiting for transfers between devices  69.2 us (28%)
  starting transfers between devices  25.8 us (11%)
  Pallas kernels  23.4 us (10%)
  between operations  14.3 us (6%)
  local copies, waits for them, and re-layouts  5.61 us (2%)
  other arithmetic  4.86 us (2%)
    all_to_all x1, blocking collectives, local(): routed = lax.all_to_all(send, COL, split_axis=0, concat_axis=0, tiled=True)  40.3 us
    all_to_all x1, blocking collectives, local(): lax.all_to_all(answer.reshape(COL_N, CAP, width + share), COL, split_axis...  39.2 us
    ppermute x6, waiting for transfers between devices, swap(): return lax.ppermute(values, axis, [(0, 1), (1, 0)])  27.7 us
    reduce_scatter x1, waiting for transfers between devices, local(): part = lax.psum_scatter(early, 'z', scatter_dimension=0, tiled=True)  21.3 us
    all_to_all x1, blocking collectives, local(): lax.all_to_all(jnp.broadcast_to(slope[None], (ROWS_N, slots, share)), 'ro...  18.4 us
    pallas_call x2, Pallas kernels, expert_call(): pl.pallas_call(kernel, in_specs=[VMEM] * (len(operands) - 1) + [pl.BlockS...  13.7 us
    all_to_all x1, waiting for transfers between devices, local(): parts = lax.all_to_all(pre, 'row', split_axis=0, concat_axis=0, tiled=True)  13.6 us
    all_to_all x1, starting transfers between devices, local(): lax.all_to_all(late_sum, 'z', split_axis=0, concat_axis=0, tiled=True)  11.8 us
  transfers between devices with their start and end apart: 11, of which 7 were waited for; matrix products, arithmetic and copies ran while one was open for 3% of the time, Pallas kernels for 0%

profile of v12, /device:TPU:1, one launch (start us, length us, event | category | flops | bytes accessed | tf_op | source)
XLA Modules:
  0.0 242.6 jit_solution(17632285349859685202)
XLA Ops:
  7.2 3.3 %collective-permute-start = (bf16[2048,512]{1,0:T(8,128)(2,1)}, bf16[2048,512]{1,0:T(8,128)(2,1)S(1)}, u32[]{:S(2)}, u32[]{:S(2)}) collective-permute-start(bf16[2048,512]{1,0:T(8,128)(2,1)} %here.1), channel_id=1, source_target_pairs={{0,1},{1,0},{2,3},{3,2},{4,5},{5,4},{6,7},{7,6},{8,9},{9,8},{10,11... | collective-permute-start | bytes 6291464 | tf_op jit(solution)/shard_map/ppermute | solution.py:16
  11.3 5.2 %collective-permute-done.there = bf16[2048,512]{1,0:T(8,128)(2,1)S(1)} collective-permute-done((bf16[2048,512]{1,0:T(8,128)(2,1)}, bf16[2048,512]{1,0:T(8,128)(2,1)S(1)}, u32[]{:S(2)}, u32[]{:S(2)}) %collective-permute-start) | collective-permute-done | bytes 2097184 | tf_op jit(solution)/shard_map/ppermute | solution.py:16
  16.5 1.2 collective-permute-done.1.weight_there
  17.8 9.2 %shard_map.86 = (bf16[2048,640]{1,0:T(8,128)(2,1)}, bf16[8,128,384]{2,1,0:T(8,128)(2,1)}, bf16[8,128,384]{2,1,0:T(8,128)(2,1)}) custom-call(s32[2]{0:T(128)} %pad_add_fusion.at, bf16[2048,512]{1,0:T(8,128)(2,1)} %here.1, bf16[2048,512]{1,0:T(8,128)(2,1)} %copy-done.4, bf16[2048,512]{1,0:T(8,128)(2,1)} %weight_here.1, ...), custom_call_target="tpu_custom_call" | custom-call | flops 4294967296 | bytes 10485760 | tf_op jit(solution)/shard_map/pallas_call | solution.py:65
  28.7 1.1 collective-permute-start.2
  31.3 1.0 constant_dynamic-slice_fusion.4
  32.9 16.4 %collective-permute-done.2 = bf16[8,128,384]{2,1,0:T(8,128)(2,1)S(1)} collective-permute-done((bf16[8,128,384]{2,1,0:T(8,128)(2,1)S(1)}, bf16[8,128,384]{2,1,0:T(8,128)(2,1)S(1)}, u32[]{:S(2)}, u32[]{:S(2)}) %collective-permute-start.2) | collective-permute-done | bytes 786464 | tf_op jit(solution)/shard_map/ppermute | solution.py:16
  49.3 1.1 add_convert_fusion
  50.4 11.8 %all-to-all-start = ((bf16[8,128,384]{2,1,0:T(8,128)(2,1)}), bf16[8,128,384]{2,1,0:T(8,128)(2,1)S(1)}, u32[]{:S(2)}, u32[]{:S(2)}) async-start(bf16[8,128,384]{2,1,0:T(8,128)(2,1)} %add_convert_fusion), calls=%async_computation | async-start | bytes 1572864 | tf_op jit(solution)/shard_map/all_to_all | solution.py:267
  62.6 2.2 collective-permute-start.5
  65.5 6.6 %collective-permute-done.5 = bf16[256,512]{1,0:T(8,128)(2,1)S(1)} collective-permute-done((bf16[256,512]{1,0:T(8,128)(2,1)S(1)}, bf16[256,512]{1,0:T(8,128)(2,1)S(1)}, u32[]{:S(2)}, u32[]{:S(2)}) %collective-permute-start.5) | collective-permute-done | bytes 262176 | tf_op jit(solution)/shard_map/ppermute | solution.py:265
  72.2 21.3 %reduce-scatter.2.cloned.1.call-done = bf16[256,640]{1,0:T(8,128)(2,1)} async-done(((bf16[2048,640]{1,0:T(8,128)(2,1)}), bf16[256,640]{1,0:T(8,128)(2,1)}) %reduce-scatter.2.cloned.1.call-update) | async-done | bytes 327696 | tf_op jit(solution)/shard_map/reduce_scatter | solution.py:217
  93.5 1.0 constant_dynamic-slice_fusion
  95.4 4.9 %collective-permute-done.4.there = bf16[128,640]{1,0:T(8,128)(2,1)S(1)} collective-permute-done((bf16[128,640]{1,0:T(8,128)(2,1)S(1)}, bf16[128,640]{1,0:T(8,128)(2,1)S(1)}, u32[]{:S(2)}, u32[]{:S(2)}) %collective-permute-start.4) | collective-permute-done | bytes 163872 | tf_op jit(solution)/shard_map/ppermute | solution.py:16
  100.9 40.3 %all_to_all.25 = bf16[32,16,1152]{2,1,0:T(8,128)(2,1)} all-to-all(bf16[32,16,1152]{2,1,0:T(8,128)(2,1)S(1)} %shard_map.87), channel_id=1, replica_groups=mesh['row'=8,'z'=8,'xh'=2,'core'=2] {'z','xh','core'}, dimensions={0} | all-to-all | bytes 2359296 | tf_op jit(solution)/shard_map/all_to_all | solution.py:280
  141.2 6.8 %shard_map.88 = bf16[8,256,256]{2,1,0:T(8,128)(2,1)} custom-call(bf16[16,2,16,1152]{3,2,1,0:T(8,128)(2,1)} %bitcast.24, bf16[2048,2048]{1,0:T(8,128)(2,1)} %bitcast.22), custom_call_target="tpu_custom_call" | custom-call | flops 2147483648 | bytes 10485760 | tf_op jit(solution)/shard_map/pallas_call | solution.py:172
  148.0 5.7 %all-to-all-start.2 = ((bf16[8,256,256]{2,1,0:T(8,128)(2,1)}), bf16[8,256,256]{2,1,0:T(8,128)(2,1)S(1)}, u32[]{:S(2)}, u32[]{:S(2)}) async-start(bf16[8,256,256]{2,1,0:T(8,128)(2,1)} %shard_map.88), calls=%async_computation.3 | async-start | bytes 2097152 | tf_op jit(solution)/shard_map/all_to_all | solution.py:287
  153.7 0.9 fusion.15
  154.6 13.6 %all-to-all-done.2 = bf16[8,256,256]{2,1,0:T(8,128)(2,1)S(1)} async-done(((bf16[8,256,256]{2,1,0:T(8,128)(2,1)}), bf16[8,256,256]{2,1,0:T(8,128)(2,1)S(1)}, u32[]{:S(2)}, u32[]{:S(2)}) %all-to-all-start.2) | async-done | bytes 1048608 | tf_op jit(solution)/shard_map/all_to_all | solution.py:287
  169.2 18.4 %all_to_all.26.slopes = bf16[8,256,256]{2,1,0:T(8,128)(2,1)} all-to-all(bf16[8,256,256]{2,1,0:T(8,128)(2,1)S(1)} %broadcast_in_dim.2), channel_id=1, replica_groups=mesh['row'=8,'z'=8,'xh'=2,'core'=2] {'row'}, dimensions={0} | all-to-all | bytes 2097152 | tf_op jit(solution)/shard_map/all_to_all | solution.py:294
  187.5 6.9 %shard_map.89 = bf16[256,2304]{1,0:T(8,128)(2,1)} custom-call(bf16[8,256,256]{2,1,0:T(8,128)(2,1)} %all_to_all.26.slopes, bf16[256,256]{1,0:T(8,128)(2,1)} %get-tuple-element.36.activated, bf16[2048,2048]{1,0:T(8,128)(2,1)} %bitcast.23), custom_call_target="tpu_custom_call" | custom-call | flops 2147483648 | bytes 10485760 | tf_op jit(solution)/shard_map/pallas_call | solution.py:172
  194.4 39.2 %all_to_all.27 = bf16[32,8,2304]{2,1,0:T(8,128)(2,1)S(1)} all-to-all(bf16[32,8,2304]{2,1,0:T(8,128)(2,1)} %bitcast.27), channel_id=1, replica_groups=mesh['row'=8,'z'=8,'xh'=2,'core'=2] {'z','xh','core'}, dimensions={0} | all-to-all | bytes 2359296 | tf_op jit(solution)/shard_map/all_to_all | solution.py:303
  233.9 0.9 multiply_reduce_fusion
  234.8 1.0 convolution_convert_fusion
  (62 shorter events, 8.5 us)
Async XLA Ops:
  7.2 86.4 %reduce-scatter.2.cloned.1.call-start = ((), (), s32[]{:S(2)}) async-start(), calls=%async_computation.6 | async-start | bytes 2949120 | tf_op jit(solution)/shard_map/reduce_scatter | solution.py:217
  7.2 9.3 %collective-permute-start = (bf16[2048,512]{1,0:T(8,128)(2,1)}, bf16[2048,512]{1,0:T(8,128)(2,1)S(1)}, u32[]{:S(2)}, u32[]{:S(2)}) collective-permute-start(bf16[2048,512]{1,0:T(8,128)(2,1)} %here.1), channel_id=1, source_target_pairs={{0,1},{1,0},{2,3},{3,2},{4,5},{5,4},{6,7},{7,6},{8,9},{9,8},{10,11... | collective-permute-start | bytes 6291464 | tf_op jit(solution)/shard_map/ppermute | solution.py:16
  10.5 7.1 %collective-permute-start.1 = (bf16[2048,512]{1,0:T(8,128)(2,1)}, bf16[2048,512]{1,0:T(8,128)(2,1)}, u32[]{:S(2)}, u32[]{:S(2)}) collective-permute-start(bf16[2048,512]{1,0:T(8,128)(2,1)} %weight_here.1), channel_id=1, source_target_pairs={{0,1},{1,0},{2,3},{3,2},{4,5},{5,4},{6,7},{7,6},{8,9},{9,8},{10,11... | collective-permute-start | bytes 6291464 | tf_op jit(solution)/shard_map/ppermute | solution.py:16
  16.5 1.3 copy-start.4
  27.1 0.7 copy-start.1
  27.1 1.7 copy-start.5
  27.1 3.7 %copy-start.3 = (f32[64,2]{0,1:T(2,128)S(1)}, f32[64,2]{0,1:T(2,128)}, u32[]{:S(2)}) copy-start(f32[64,2]{0,1:T(2,128)} %param.11) | copy-start | bytes 1540
  27.7 21.6 %copy-start = (bf16[8,128,384]{2,1,0:T(8,128)(2,1)S(1)}, bf16[8,128,384]{2,1,0:T(8,128)(2,1)}, u32[]{:S(2)}) copy-start(bf16[8,128,384]{2,1,0:T(8,128)(2,1)} %get-tuple-element.17) | copy-start | bytes 2359300
  27.7 37.1 %collective-permute-start.7 = (s32[64,2]{0,1:T(2,128)S(1)}, s32[64,2]{0,1:T(2,128)S(1)}, u32[]{:S(2)}, u32[]{:S(2)}) collective-permute-start(s32[64,2]{0,1:T(2,128)S(1)} %copy-done.1), channel_id=1, source_target_pairs={{0,1},{1,0},{2,3},{3,2},{4,5},{5,4},{6,7},{7,6},{8,9},{9,8},{10,11... | collective-permute-start | bytes 1544 | tf_op jit(solution)/shard_map/ppermute | solution.py:16
  28.7 20.6 %collective-permute-start.2 = (bf16[8,128,384]{2,1,0:T(8,128)(2,1)S(1)}, bf16[8,128,384]{2,1,0:T(8,128)(2,1)S(1)}, u32[]{:S(2)}, u32[]{:S(2)}) collective-permute-start(bf16[8,128,384]{2,1,0:T(8,128)(2,1)S(1)} %copy-done.5), channel_id=1, source_target_pairs={{0,2},{2,0},{1,3},{3,1},{4,6},{6,4},{5,7},{7,5},{8,10},{10,8},{9,1... | collective-permute-start | bytes 2359304 | tf_op jit(solution)/shard_map/ppermute | solution.py:16
  32.3 18.2 %collective-permute-start.3 = (bf16[256,512]{1,0:T(8,128)(2,1)S(1)}, bf16[256,512]{1,0:T(8,128)(2,1)S(1)}, u32[]{:S(2)}, u32[]{:S(2)}) collective-permute-start(bf16[256,512]{1,0:T(8,128)(2,1)S(1)} %constant_dynamic-slice_fusion.4), channel_id=1, source_target_pairs={{0,0},{4,12},{8,24},{12,4},{16,16},{20,28},{24,8},{28,20},{32,36},... | collective-permute-start | bytes 786440 | tf_op jit(solution)/shard_map/ppermute | solution.py:226
  50.4 12.2 %copy-start.2 = (f32[2048]{0:T(1024)S(1)}, f32[2048]{0:T(1024)}, u32[]{:S(2)}) copy-start(f32[2048]{0:T(1024)} %param.9) | copy-start | bytes 24580
  50.4 45.0 %all-to-all-start = ((bf16[8,128,384]{2,1,0:T(8,128)(2,1)}), bf16[8,128,384]{2,1,0:T(8,128)(2,1)S(1)}, u32[]{:S(2)}, u32[]{:S(2)}) async-start(bf16[8,128,384]{2,1,0:T(8,128)(2,1)} %add_convert_fusion), calls=%async_computation | async-start | bytes 1572864 | tf_op jit(solution)/shard_map/all_to_all | solution.py:267
  62.6 9.5 %collective-permute-start.5 = (bf16[256,512]{1,0:T(8,128)(2,1)S(1)}, bf16[256,512]{1,0:T(8,128)(2,1)S(1)}, u32[]{:S(2)}, u32[]{:S(2)}) collective-permute-start(bf16[256,512]{1,0:T(8,128)(2,1)S(1)} %collective-permute-done.3), channel_id=1, source_target_pairs={{0,0},{1,2},{2,1},{3,3},{4,100},{5,102},{6,101},{7,103},{8,200},{9... | collective-permute-start | bytes 786440 | tf_op jit(solution)/shard_map/ppermute | solution.py:265
  72.1 23.3 %collective-permute-start.6 = (bf16[128,512]{1,0:T(8,128)(2,1)S(1)}, bf16[128,512]{1,0:T(8,128)(2,1)S(1)}, u32[]{:S(2)}, u32[]{:S(2)}) collective-permute-start(bf16[128,512]{1,0:T(8,128)(2,1)S(1)} %get-tuple-element.38), channel_id=1, source_target_pairs={{0,2},{2,0},{1,3},{3,1},{4,6},{6,4},{5,7},{7,5},{8,10},{10,8},{9,1... | collective-permute-start | bytes 393224 | tf_op jit(solution)/shard_map/ppermute | solution.py:16
  94.6 5.8 %collective-permute-start.4 = (bf16[128,640]{1,0:T(8,128)(2,1)S(1)}, bf16[128,640]{1,0:T(8,128)(2,1)S(1)}, u32[]{:S(2)}, u32[]{:S(2)}) collective-permute-start(bf16[128,640]{1,0:T(8,128)(2,1)S(1)} %get-tuple-element.35), channel_id=1, source_target_pairs={{0,2},{2,0},{1,3},{3,1},{4,6},{6,4},{5,7},{7,5},{8,10},{10,8},{9,1... | collective-permute-start | bytes 491528 | tf_op jit(solution)/shard_map/ppermute | solution.py:16
  148.0 20.2 %all-to-all-start.2 = ((bf16[8,256,256]{2,1,0:T(8,128)(2,1)}), bf16[8,256,256]{2,1,0:T(8,128)(2,1)S(1)}, u32[]{:S(2)}, u32[]{:S(2)}) async-start(bf16[8,256,256]{2,1,0:T(8,128)(2,1)} %shard_map.88), calls=%async_computation.3 | async-start | bytes 2097152 | tf_op jit(solution)/shard_map/all_to_all | solution.py:287
Sparse Core Ops, SparseCore 0:
  27.2 66.2 reduce-scatter.1
